TPU v7x, 32 devices: a whole 2x2x4 slice. The times are simulated.
32 devices in a mesh: rep: 4 (over z), fsdp: 8 (over y, x, core).
Axes of the slice: x: 2, y: 2, z: 4, core: 2. Of those that a mesh axis runs over, the one named last changes fastest.
Arguments:
- layer_input: bfloat16 [16, 1024, 768], P('rep', 'fsdp'), may hold values from -40 to 40
- positions: int32 [16, 1024], P('rep', 'fsdp'), may hold values from 0 to 1023, as said below
- cotangent: bfloat16 [16, 1024, 768], P('rep', 'fsdp'), may hold values from -6 to 6
- w_qkv: bfloat16 [768, 2304], P('fsdp'), may hold values from -4 to 4
- w_out: bfloat16 [768, 768], P('fsdp'), may hold values from -1.75 to 1.75
- w_up: bfloat16 [768, 3072], P('fsdp'), may hold values from -0.21875 to 0.21875
- w_down: bfloat16 [768, 3072], P('fsdp'), may hold values from -0.109375 to 0.109375
- ln1_gain: bfloat16 [768], P('fsdp'), may hold values from 0.5 to 1.5
- ln1_bias: bfloat16 [768], P('fsdp'), may hold values from -1.5 to 1.5
- ln2_gain: bfloat16 [768], P('fsdp'), may hold values from 0.5 to 1.5
- ln2_bias: bfloat16 [768], P('fsdp'), may hold values from -1.5 to 1.5
- qkv_bias: bfloat16 [2304], P('fsdp'), may hold values from -2.5 to 2.5
- out_bias: bfloat16 [768], P('fsdp'), may hold values from -2.5 to 2.5
- up_bias: bfloat16 [3072], P('fsdp'), may hold values from -2.5 to 2.5
- down_bias: bfloat16 [768], P('fsdp'), may hold values from -2.5 to 2.5
Outputs:
- output: bfloat16 [16, 1024, 768], P('rep', 'fsdp')
- grad_input: bfloat16 [16, 1024, 768], P('rep', 'fsdp')
- grad_w_qkv: float32 [768, 2304], P('fsdp')
- grad_w_out: float32 [768, 768], P('fsdp')
- grad_w_up: float32 [768, 3072], P('fsdp')
- grad_w_down: float32 [768, 3072], P('fsdp')
- grad_ln1_gain: float32 [768], P('fsdp')
- grad_ln1_bias: float32 [768], P('fsdp')
- grad_ln2_gain: float32 [768], P('fsdp')
- grad_ln2_bias: float32 [768], P('fsdp')
- grad_qkv_bias: float32 [2304], P('fsdp')
- grad_out_bias: float32 [768], P('fsdp')
- grad_up_bias: float32 [3072], P('fsdp')
- grad_down_bias: float32 [768], P('fsdp')
Inputs may be any that keep to these rules, and one draw needn't show every extreme that they name: positions[s, 0] is 0, and each later positions[s, t] is either 0 or positions[s, t - 1] + 1; sequence 0 is one document of 1024 tokens.
All inputs are finite; a program needn't handle non-finite values.
Results may differ from a plain program's by a relative error of at most 0.0093.
Values may be sent and summed in bfloat16 or wider, within the bound.
No kernel may reach another device: no remote copies, remote signals or barrier semaphores. Data moves between devices by JAX's collectives and lax.ppermute only.
A program may use at most 320 MiB of HBM per device.

v0:
```python
import jax
import jax.numpy as jnp
from jax import lax
from jax.sharding import PartitionSpec as P

H = 12
HD = 64
ROT = 16


EPS = 1e-05
NEG = -1e30


def norm_rows(values, gain, shift):
    mean = jnp.mean(values, axis=-1, keepdims=True)
    centred = values - mean
    spread = jnp.mean(centred * centred, axis=-1, keepdims=True)
    return centred * lax.rsqrt(spread + EPS) * gain + shift


def rotate(values, cosine, sine):
    half = ROT // 2
    head = values[..., :ROT]
    turned = jnp.concatenate([-head[..., half:], head[..., :half]], axis=-1)
    return jnp.concatenate([head * cosine + turned * sine, values[..., ROT:]], axis=-1)


def angles(positions):
    inverse = 10000.0 ** (-jnp.arange(0, ROT, 2, dtype=jnp.float32) / ROT)
    phase = positions.astype(jnp.float32)[..., None] * inverse
    phase = jnp.concatenate([phase, phase], axis=-1)[..., None, :]
    return (jnp.cos(phase), jnp.sin(phase))


def on_device(
    layer_input,
    positions,
    cotangent,
    w_qkv,
    w_out,
    w_up,
    w_down,
    ln1_gain,
    ln1_bias,
    ln2_gain,
    ln2_bias,
    qkv_bias,
    out_bias,
    up_bias,
    down_bias,
):
    seq_count, span_len, width = layer_input.shape
    shard_count = lax.axis_size("fsdp")
    shard_index = lax.axis_index("fsdp")
    row_count = seq_count * span_len
    qkv_cols = w_qkv.shape[1]
    hidden_cols = w_up.shape[1]
    vectors = (
        lax.all_gather(ln1_gain, "fsdp", axis=0, tiled=True),
        lax.all_gather(ln1_bias, "fsdp", axis=0, tiled=True),
        lax.all_gather(ln2_gain, "fsdp", axis=0, tiled=True),
        lax.all_gather(ln2_bias, "fsdp", axis=0, tiled=True),
        lax.all_gather(qkv_bias, "fsdp", axis=0, tiled=True),
        lax.all_gather(out_bias, "fsdp", axis=0, tiled=True),
        lax.all_gather(up_bias, "fsdp", axis=0, tiled=True),
        lax.all_gather(down_bias, "fsdp", axis=0, tiled=True),
    )
    gain_one, shift_one, gain_two, shift_two, bias_qkv, bias_out, bias_up, bias_down = [
        v.astype(jnp.float32) for v in vectors
    ]
    source = layer_input.reshape(row_count, width).astype(jnp.float32)
    normed_one, pull_one = jax.vjp(norm_rows, source, gain_one, shift_one)
    normed_two, pull_two = jax.vjp(norm_rows, source, gain_two, shift_two)
    input_one = normed_one.astype(jnp.bfloat16)
    input_two = normed_two.astype(jnp.bfloat16)
    pieces = (
        lax.all_gather(w_qkv, "fsdp", axis=0, tiled=True),
        lax.all_gather(w_up, "fsdp", axis=0, tiled=True),
    )
    count = pieces[0].shape[0]
    qkv_sum = jnp.dot(input_one, pieces[0], preferred_element_type=jnp.float32)
    up_sum = jnp.dot(input_two, pieces[1], preferred_element_type=jnp.float32)
    qkv_full = qkv_sum + bias_qkv
    up_full = up_sum + bias_up
    cosine, sine = angles(positions)

    def turn_all(packed):
        shaped = packed.reshape(seq_count, span_len, 3, H, HD)
        return (
            rotate(shaped[:, :, 0], cosine, sine),
            rotate(shaped[:, :, 1], cosine, sine),
            shaped[:, :, 2],
        )

    turned, pull_turn = jax.vjp(turn_all, qkv_full)
    query_low = turned[0].astype(jnp.bfloat16)
    key_low = turned[1].astype(jnp.bfloat16)
    value_low = turned[2].astype(jnp.bfloat16)
    key_flat = key_low.reshape(seq_count, span_len, width)
    value_flat = value_low.reshape(seq_count, span_len, width)
    query_index = shard_index * span_len + jnp.arange(span_len, dtype=jnp.int32)
    first_seen = query_index[None, :] - positions

    def scores_with(key_piece):
        count = key_piece.shape[1]
        keys = key_piece.reshape(seq_count, count, H, HD)
        raw = (
            jnp.einsum("sqhd,skhd->shqk", query_low, keys, preferred_element_type=jnp.float32)
            * 0.125
        )
        key_index = jnp.arange(count, dtype=jnp.int32)
        seen = (key_index[None, None, :] <= query_index[None, :, None]) & (
            key_index[None, None, :] >= first_seen[:, :, None]
        )
        return (raw, seen[:, None])

    start_top = jnp.full((seq_count, H, span_len), NEG, jnp.float32)
    raw, seen = scores_with(lax.all_gather(key_flat, "fsdp", axis=1, tiled=True))
    masked = jnp.where(seen, raw, NEG)
    new_top = jnp.maximum(start_top, jnp.max(masked, axis=-1))
    weights = jnp.where(seen, jnp.exp(masked - new_top[..., None]), 0.0)
    total = jnp.sum(weights, axis=-1)
    log_total = new_top + jnp.log(total)
    pieces = (
        lax.all_gather(key_flat, "fsdp", axis=1, tiled=True),
        lax.all_gather(value_flat, "fsdp", axis=1, tiled=True),
    )
    raw, seen = scores_with(pieces[0])
    count = pieces[1].shape[1]
    values = pieces[1].reshape(seq_count, count, H, HD)
    probs = jnp.where(seen, jnp.exp(raw - log_total[..., None]), 0.0)
    probs_low = probs.astype(jnp.bfloat16)
    residue = (probs - probs_low.astype(jnp.float32)).astype(jnp.bfloat16)
    mixed_sum = jnp.einsum("shqk,skhd->sqhd", probs_low, values, preferred_element_type=jnp.float32)
    residue_sum = jnp.einsum("shqk,skhd->sqhd", residue, values, preferred_element_type=jnp.float32)
    attended = mixed_sum.reshape(row_count, width).astype(jnp.bfloat16)
    hidden = jax.nn.gelu(up_full, approximate=False).astype(jnp.bfloat16)
    pieces = (
        lax.all_gather(w_out, "fsdp", axis=0, tiled=True),
        lax.all_gather(w_down, "fsdp", axis=0, tiled=True),
    )
    columns = jnp.einsum("rk,ck->rc", attended, pieces[0], preferred_element_type=jnp.float32)
    columns = columns + jnp.einsum(
        "rk,ck->rc", hidden, pieces[1], preferred_element_type=jnp.float32
    )
    output = (
        (source + columns + bias_out + bias_down).astype(jnp.bfloat16).reshape(layer_input.shape)
    )
    grad_out = cotangent.reshape(row_count, width)
    pieces = (
        lax.all_gather(w_out, "fsdp", axis=0, tiled=True),
        lax.all_gather(w_down, "fsdp", axis=0, tiled=True),
    )
    count = pieces[0].shape[0]
    grad_attended = jnp.dot(grad_out, pieces[0], preferred_element_type=jnp.float32)
    grad_hidden = jnp.dot(grad_out, pieces[1], preferred_element_type=jnp.float32)
    grad_mixed = grad_attended.astype(jnp.bfloat16)
    gelu_value, pull_gelu = jax.vjp(lambda v: jax.nn.gelu(v, approximate=False), up_full)
    grad_up = pull_gelu(grad_hidden)[0].astype(jnp.bfloat16)
    grad_heads = grad_mixed.reshape(seq_count, span_len, H, HD)
    carried = jnp.sum(grad_heads.astype(jnp.float32) * (mixed_sum + residue_sum), axis=-1)
    carried_rows = jnp.transpose(carried, (0, 2, 1))
    pieces = (
        lax.all_gather(key_flat, "fsdp", axis=1, tiled=True),
        lax.all_gather(value_flat, "fsdp", axis=1, tiled=True),
    )
    raw, seen = scores_with(pieces[0])
    count = pieces[0].shape[1]
    keys = pieces[0].reshape(seq_count, count, H, HD)
    values = pieces[1].reshape(seq_count, count, H, HD)
    probs = jnp.where(seen, jnp.exp(raw - log_total[..., None]), 0.0)
    probs_low = probs.astype(jnp.bfloat16)
    grad_probs = jnp.einsum(
        "sqhd,skhd->shqk", grad_heads, values, preferred_element_type=jnp.float32
    )
    grad_scores = (probs * (grad_probs - carried_rows[..., None])).astype(jnp.bfloat16)
    grad_query = jnp.einsum(
        "shqk,skhd->sqhd", grad_scores, keys, preferred_element_type=jnp.float32
    )
    key_part = jnp.einsum(
        "shqk,sqhd->skhd", grad_scores, query_low, preferred_element_type=jnp.float32
    )
    value_part = jnp.einsum(
        "shqk,sqhd->skhd", probs_low, grad_heads, preferred_element_type=jnp.float32
    )
    both = jnp.concatenate(
        [key_part.reshape(seq_count, count, width), value_part.reshape(seq_count, count, width)],
        axis=2,
    )
    key_terms = both
    grad_query, key_terms = (grad_query, key_terms)
    grad_query = grad_query * 0.125
    key_owned = lax.psum_scatter(key_terms, "fsdp", scatter_dimension=1, tiled=True)
    grad_key = key_owned[..., :width].reshape(seq_count, span_len, H, HD) * 0.125
    grad_value = key_owned[..., width:].reshape(seq_count, span_len, H, HD)
    grad_qkv = pull_turn((grad_query, grad_key, grad_value))[0].astype(jnp.bfloat16)
    pieces = (
        lax.all_gather(w_qkv, "fsdp", axis=0, tiled=True),
        lax.all_gather(w_up, "fsdp", axis=0, tiled=True),
    )
    columns_one = jnp.einsum("rk,ck->rc", grad_qkv, pieces[0], preferred_element_type=jnp.float32)
    columns_two = jnp.einsum("rk,ck->rc", grad_up, pieces[1], preferred_element_type=jnp.float32)
    grad_source_one, grad_gain_one, grad_shift_one = pull_one(columns_one)
    grad_source_two, grad_gain_two, grad_shift_two = pull_two(columns_two)
    grad_out_float = grad_out.astype(jnp.float32)
    grad_input = (
        (grad_out_float + grad_source_one + grad_source_two)
        .astype(jnp.bfloat16)
        .reshape(layer_input.shape)
    )
    grad_out_total = jnp.sum(grad_out_float, axis=0)
    local_vectors = (
        grad_gain_one,
        grad_shift_one,
        grad_gain_two,
        grad_shift_two,
        jnp.sum(grad_qkv.astype(jnp.float32), axis=0),
        grad_out_total,
        jnp.sum(grad_up.astype(jnp.float32), axis=0),
    )
    summed = lax.psum(
        (
            local_vectors[0],
            local_vectors[1],
            local_vectors[2],
            local_vectors[3],
            local_vectors[4],
            local_vectors[5],
            local_vectors[6],
        ),
        ("rep", "fsdp"),
    )
    owned_vectors = [
        lax.dynamic_slice_in_dim(
            v, shard_index * (v.shape[0] // shard_count), v.shape[0] // shard_count
        )
        for v in summed
    ]
    owned = lax.psum_scatter(
        jnp.concatenate(
            [
                jnp.einsum("rc,rk->ck", input_one, grad_qkv, preferred_element_type=jnp.float32),
                jnp.einsum("rc,rk->ck", grad_out, attended, preferred_element_type=jnp.float32),
                jnp.einsum("rc,rk->ck", input_two, grad_up, preferred_element_type=jnp.float32),
                jnp.einsum("rc,rk->ck", grad_out, hidden, preferred_element_type=jnp.float32),
            ],
            axis=1,
        ),
        "fsdp",
        scatter_dimension=0,
        tiled=True,
    )
    owned = lax.psum(owned, "rep")
    edge_two = qkv_cols + width
    edge_three = edge_two + hidden_cols
    grad_w_qkv = owned[:, :qkv_cols]
    grad_w_out = owned[:, qkv_cols:edge_two]
    grad_w_up = owned[:, edge_two:edge_three]
    grad_w_down = owned[:, edge_three:]
    return (
        output,
        grad_input,
        grad_w_qkv,
        grad_w_out,
        grad_w_up,
        grad_w_down,
        owned_vectors[0],
        owned_vectors[1],
        owned_vectors[2],
        owned_vectors[3],
        owned_vectors[4],
        owned_vectors[5],
        owned_vectors[6],
        owned_vectors[5],
    )


def solution(mesh):
    return jax.shard_map(
        on_device,
        mesh=mesh,
        in_specs=(
            P("rep", "fsdp", None),
            P("rep", "fsdp"),
            P("rep", "fsdp", None),
            P("fsdp", None),
            P("fsdp", None),
            P("fsdp", None),
            P("fsdp", None),
            P("fsdp"),
            P("fsdp"),
            P("fsdp"),
            P("fsdp"),
            P("fsdp"),
            P("fsdp"),
            P("fsdp"),
            P("fsdp"),
        ),
        out_specs=(
            P("rep", "fsdp", None),
            P("rep", "fsdp", None),
            P("fsdp", None),
            P("fsdp", None),
            P("fsdp", None),
            P("fsdp", None),
            P("fsdp"),
            P("fsdp"),
            P("fsdp"),
            P("fsdp"),
            P("fsdp"),
            P("fsdp"),
            P("fsdp"),
            P("fsdp"),
        ),
        check_vma=False,
    )
```

profile of v0, /device:TPU:0, one launch (start us, length us, event | category | flops | bytes accessed | tf_op | source)
XLA Modules:
  0.0 780.7 jit_solution(14124956346842506521)
XLA Ops:
  10.1 1.5 fusion.28
  21.0 26.5 %all-reduce.19 = (bf16[768]{0:T(1024)(128)(2,1)S(1)}, bf16[768]{0:T(1024)(128)(2,1)S(1)}, bf16[768]{0:T(1024)(128)(2,1)}, bf16[768]{0:T(1024)(128)(2,1)}, bf16[7...) all-reduce(bf16[768]{0:T(1024)(128)(2,1)S(1)} %dynamic-update-slice, ...), channel_id=1, replica_groups=mesh['rep'=4,'fsdp'=8] {'fsdp'}, use_global_device_ids=true, to_apply=%add.15 | all-reduce | flops 6912 | bytes 27648
  47.6 1.6 fusion.33
  49.2 6.1 convolution_add_fusion
  55.4 6.2 copy.46
  61.5 6.3 reshape.249
  67.9 2.2 fusion.78
  72.9 1.7 slice.108
  77.7 2.9 convolution_convert_fusion
  80.6 1.5 copy.51
  84.6 37.4 %all-gather.12.cloned.1.call-done = bf16[4,1024,768]{1,2,0:T(8,128)(2,1)} async-done(((bf16[4,128,768]{1,2,0:T(8,128)(2,1)}), bf16[4,1024,768]{1,2,0:T(8,128)(2,1)}) %all-gather.12.cloned.1.call-update) | async-done | bytes 6291472 | tf_op jit(solution)/shard_map/all_gather | solution.py:126
  121.9 12.9 %select_reduce_fusion.1 = (f32[4,12,128]{2,1,0:T(8,128)S(1)}, f32[4,12,128,1024]{3,2,1,0:T(8,128)}) fusion(pred[4,128,1024]{2,1,0:T(8,128)(4,1)S(1)} %fusion.13, bf16[4,1024,12,64]{1,3,2,0:T(8,128)(2,1)} %bitcast.164, bf16[4,128,12,48]{1,3,2,0:T(8,128)(2,1)S(1)} %slice.110, bf16[4,128,12,16]{1,3,2,0:T(8,128)(2,1)S(1)} %get-tuple-element.61), kind=kOutput, calls=%fused_computation.6 | convolution fusion | flops 825747456 | bytes 32792576 | tf_op jit(solution)/shard_map/sqhd,skhd->shqk/dot_general | solution.py:109
  134.9 12.2 %select_reduce_fusion = f32[4,12,128]{2,1,0:T(8,128)S(1)} fusion(f32[4,12,128,1024]{3,2,1,0:T(8,128)} %get-tuple-element.76, f32[4,12,128]{2,1,0:T(8,128)S(1)} %broadcast_maximum_fusion, pred[4,128,1024]{2,1,0:T(8,128)(4,1)S(1)} %fusion.13), kind=kLoop, calls=%fused_computation.5 | loop fusion | flops 31451136 | bytes 25739264 | tf_op jit(solution)/shard_map/reduce_sum | solution.py:123
  147.1 23.9 %all-gather.10.cloned.1.call-done = bf16[4,1024,768]{1,2,0:T(8,128)(2,1)} async-done(((bf16[4,128,768]{1,2,0:T(8,128)(2,1)}), bf16[4,1024,768]{1,2,0:T(8,128)(2,1)}) %all-gather.10.cloned.1.call-update) | async-done | bytes 6291472 | tf_op jit(solution)/shard_map/all_gather | solution.py:127
  170.9 14.2 %fusion.58 = f32[4,12,64,128]{3,2,1,0:T(8,128)} fusion(bf16[4,1024,12,64]{1,3,2,0:T(8,128)(2,1)} %bitcast.190, f32[4,12,128,1024]{3,2,1,0:T(8,128)} %get-tuple-element.76, f32[4,12,128]{2,1,0:T(8,128)S(1)} %log_add_fusion, pred[4,128,1024]{2,1,0:T(8,128)(4,1)S(1)} %fusion.13), kind=kOutput, calls=%fused_computation.110 | convolution fusion | flops 830472192 | bytes 33579008 | tf_op jit(solution)/shard_map/shqk,skhd->sqhd/dot_general | solution.py:135
  185.2 15.0 %fusion.16 = f32[4,128,12]{1,2,0:T(8,128)S(1)} fusion(f32[4,12,64,128]{3,2,1,0:T(8,128)} %fusion.58, bf16[4,1024,12,64]{1,3,2,0:T(8,128)(2,1)} %bitcast.191, f32[4,12,128,1024]{3,2,1,0:T(8,128)} %get-tuple-element.76, f32[4,12,128]{2,1,0:T(8,128)S(1)} %log_add_fusion, pred[4,128,1024]{2,1,0:T(8,128)(4,1)S(1)} %fusion.13, bf16[4,128,12,64]{1,0,3,2:T(4,128)(2,1)} %reshape.254), kind=kOutput, calls=%fused_computation.48 | convolution fusion | flops 850913280 | bytes 34390016 | tf_op jit(solution)/shard_map/shqk,skhd->sqhd/dot_general | solution.py:136
  200.2 20.5 %multiply_convert_fusion = bf16[4,12,128,1024]{3,2,1,0:T(8,128)(2,1)} fusion(f32[4,12,128,1024]{3,2,1,0:T(8,128)} %get-tuple-element.76, f32[4,12,128]{2,1,0:T(8,128)S(1)} %bitcast.194, f32[4,12,128]{2,1,0:T(8,128)S(1)} %log_add_fusion, pred[4,128,1024]{2,1,0:T(8,128)(4,1)S(1)} %fusion.13, bf16[4,1024,12,64]{1,3,2,0:T(8,128)(2,1)} %bitcast.192, ...), kind=kOutput, calls=%fused_computation.2 | convolution fusion | flops 843055104 | bytes 45400064 | tf_op jit(solution)/shard_map/sqhd,skhd->shqk/dot_general | solution.py:174
  220.6 11.1 %fusion.50 = f32[4,12,64,1024]{3,2,1,0:T(8,128)} fusion(bf16[4,12,128,1024]{3,2,1,0:T(8,128)(2,1)} %multiply_convert_fusion, bf16[4,128,12,48]{1,3,2,0:T(8,128)(2,1)S(1)} %slice.110, bf16[4,128,12,16]{1,3,2,0:T(8,128)(2,1)S(1)} %get-tuple-element.61), kind=kOutput, calls=%fused_computation.98 | convolution fusion | flops 806879232 | bytes 25952256 | tf_op jit(solution)/shard_map/shqk,sqhd->skhd/dot_general | solution.py:181
  231.8 14.8 %fusion.47 = f32[4,12,64,1024]{3,2,1,0:T(8,128)} fusion(bf16[4,128,12,64]{1,0,3,2:T(4,128)(2,1)S(1)} %copy-done.12, f32[4,12,128,1024]{3,2,1,0:T(8,128)} %get-tuple-element.76, f32[4,12,128]{2,1,0:T(8,128)S(1)} %log_add_fusion, pred[4,128,1024]{2,1,0:T(8,128)(4,1)S(1)} %fusion.13), kind=kOutput, calls=%fused_computation.94 | convolution fusion | flops 830472192 | bytes 39084032 | tf_op jit(solution)/shard_map/shqk,sqhd->skhd/dot_general | solution.py:184
  246.5 18.8 %pad_maximum_fusion.1 = f32[4,1024,1536]{1,2,0:T(8,128)} fusion(f32[4,1024,768]{1,2,0:T(8,128)} %bitcast.163, f32[4,1024,768]{1,2,0:T(8,128)} %bitcast.162), kind=kLoop, calls=%fused_computation.1 | loop fusion | flops 6291456 | bytes 50331648 | tf_op jit(solution)/shard_map/concatenate | solution.py:187
  266.0 9.4 %all-gather = bf16[8,1,384]{2,1,0:T(2,128)(2,1)S(1)} all-gather(bf16[1,1,384]{2,1,0:T(2,128)(2,1)S(1)} %reshape.280), channel_id=1, replica_groups=mesh['rep'=4,'fsdp'=8] {'fsdp'}, dimensions={0}, use_global_device_ids=true | all-gather | bytes 6912 | tf_op jit(solution)/shard_map/all_gather | solution.py:66
  276.7 8.9 %fusion.83 = f32[512,3072]{1,0:T(8,128)} fusion(bf16[512,768]{1,0:T(8,128)(2,1)S(1)} %get-tuple-element.54, bf16[768,3072]{1,0:T(8,128)(2,1)} %all-gather.16.cloned.1.call-done), kind=kOutput, calls=%fused_computation.154 | convolution fusion | flops 2415919104 | bytes 11796480 | tf_op jit(solution)/shard_map/dot_general | solution.py:83
  285.6 19.4 %convert_reduce_fusion = (f32[3072]{0:T(1024)S(1)}, bf16[512,3072]{1,0:T(8,128)(2,1)S(1)}, f32[512,3072]{1,0:T(8,128)S(1)}) fusion(f32[512,3072]{1,0:T(8,128)} %fusion.83, f32[3072]{0:T(1024)S(1)} %bitcast.188, bf16[512,768]{1,0:T(8,128)(2,1)S(1)} %bitcast.170, bf16[768,3072]{1,0:T(8,128)(2,1)} %all-gather.18.cloned.1.call-done), kind=kOutput, calls=%fused_computation.12 | convolution fusion | flops 2533880832 | bytes 21258240 | tf_op jit(solution)/shard_map/dot_general | solution.py:157
  305.0 3.2 multiply_convert_fusion.1
  308.2 7.8 convolution_bitcast_fusion
  316.0 5.2 fusion.86
  321.2 11.3 %multiply_bitcast_fusion = f32[4,128,12,64]{1,3,2,0:T(8,128)S(1)} fusion(bf16[4,1024,12,64]{1,3,2,0:T(8,128)(2,1)} %bitcast.165, bf16[4,12,128,1024]{3,2,1,0:T(8,128)(2,1)} %multiply_convert_fusion), kind=kOutput, calls=%fused_computation.82 | convolution fusion | flops 805699584 | bytes 20447232 | tf_op jit(solution)/shard_map/shqk,skhd->sqhd/dot_general | solution.py:178
  332.5 2.3 convert_bitcast_fusion
  336.3 2.2 convolution_bitcast_fusion.1
  338.5 2.0 copy.57
  340.6 82.4 %reduce-scatter.3.cloned.1.call-done = f32[4,128,1536]{1,2,0:T(8,128)} async-done(((f32[4,1024,1536]{1,2,0:T(8,128)}), f32[4,128,1536]{1,2,0:T(8,128)}) %reduce-scatter.3.cloned.1.call-update) | async-done | bytes 3145744 | tf_op jit(solution)/shard_map/reduce_scatter | solution.py:194
  423.0 2.2 fusion.80
  427.4 2.2 copy.55
  429.7 1.5 copy-done.13
  431.2 4.9 fusion.9
  436.1 19.4 %pad_maximum_fusion = f32[768,9216]{1,0:T(8,128)} fusion(f32[768,3072]{1,0:T(8,128)} %convolution_bitcast_fusion, f32[768,3072]{1,0:T(8,128)} %fusion.86, f32[768,768]{1,0:T(8,128)S(1)} %copy.57, f32[768,2304]{1,0:T(8,128)} %fusion.9), kind=kLoop, calls=%fused_computation | loop fusion | flops 21233664 | bytes 56623104 | tf_op jit(solution)/shard_map/concatenate | solution.py:241
  456.4 172.6 %reduce-scatter.5.cloned.1.call-done = f32[96,9216]{1,0:T(8,128)} async-done(((f32[768,9216]{1,0:T(8,128)}), f32[96,9216]{1,0:T(8,128)}) %reduce-scatter.5.cloned.1.call-update) | async-done | bytes 3538960 | tf_op jit(solution)/shard_map/reduce_scatter | solution.py:240
  629.0 6.1 fusion.85
  635.1 5.8 fusion.84
  641.0 1.8 fusion.42
  642.9 5.4 fusion.76
  649.4 1.4 fusion.37
  650.8 44.4 %all-reduce.18 = (f32[768]{0:T(1024)S(1)}, f32[768]{0:T(1024)S(1)}, f32[768]{0:T(1024)S(1)}, f32[768]{0:T(1024)S(1)}, f32[2304]{0:T(1024)S(1)}, /*index=5*/f32[768]{0:T(1024)S(1)}, f32[3072]{0:T(1024)S(1)}) all-reduce(f32[768]{0:T(1024)S(1)} %get-tuple-element.23, ...), channel_id=1, replica_groups=mesh['rep'=4,'fsdp'=8] {'rep','fsdp'}, use_global_device_ids=true, to_apply=%region_13.14 | all-reduce | flops 9216 | bytes 73728 | tf_op jit(solution)/shard_map/psum | solution.py:222
  698.9 3.0 add_convert_fusion.2
  701.9 64.2 %all-reduce.22.cloned.1.call-done = f32[96,9216]{1,0:T(8,128)} async-done(((f32[96,9216]{1,0:T(8,128)}), f32[96,9216]{1,0:T(8,128)}) %all-reduce.22.cloned.1.call-update) | async-done | bytes 3538960 | tf_op jit(solution)/shard_map/psum | solution.py:254
  766.1 3.3 fusion.79
  769.4 2.1 slice.88
  771.5 1.7 slice.89
  (160 shorter events, 31.1 us)
Async XLA Ops:
  7.2 42.0 %all-gather.8.cloned.1.call-start = ((), (), s32[]{:S(2)}) async-start(), calls=%async_computation.2 | async-start | bytes 3981312 | tf_op jit(solution)/shard_map/all_gather | solution.py:78
  7.9 69.8 %all-gather.14.cloned.1.call-start = ((), (), s32[]{:S(2)}) async-start(), calls=%async_computation.5 | async-start | bytes 1327104 | tf_op jit(solution)/shard_map/all_gather | solution.py:140
  8.7 113.3 %all-gather.12.cloned.1.call-start = ((), (), s32[]{:S(2)}) async-start(), calls=%async_computation.4 | async-start | bytes 7077888 | tf_op jit(solution)/shard_map/all_gather | solution.py:126
  10.0 45.3 %copy-start.23 = (f32[512]{0:T(512)}, f32[512]{0:T(512)S(1)}, u32[]{:S(2)}) copy-start(f32[512]{0:T(512)S(1)} %get-tuple-element.73) | copy-start | bytes 6148
  11.6 263.9 %copy-start.27 = (f32[4,128]{1,0:T(4,128)}, f32[4,128]{1,0:T(4,128)S(1)}, u32[]{:S(2)}) copy-start(f32[4,128]{1,0:T(4,128)S(1)} %fusion.28) | copy-start | bytes 6148
  12.5 58.2 %copy-start.15 = (f32[4,128,16]{1,2,0:T(8,128)}, f32[4,128,16]{1,2,0:T(8,128)S(1)}, u32[]{:S(2)}) copy-start(f32[4,128,16]{1,2,0:T(8,128)S(1)} %get-tuple-element.67) | copy-start | bytes 98308
  12.5 58.2 %copy-start.17 = (f32[4,128,16]{1,2,0:T(8,128)}, f32[4,128,16]{1,2,0:T(8,128)S(1)}, u32[]{:S(2)}) copy-start(f32[4,128,16]{1,2,0:T(8,128)S(1)} %get-tuple-element.68) | copy-start | bytes 98308
  47.5 228.0 %copy-start.19 = (f32[768]{0:T(1024)}, f32[768]{0:T(1024)S(1)}, u32[]{:S(2)}) copy-start(f32[768]{0:T(1024)S(1)} %convert_element_type.126) | copy-start | bytes 9220
  47.5 7.9 %copy-start.21 = (f32[768]{0:T(1024)}, f32[768]{0:T(1024)S(1)}, u32[]{:S(2)}) copy-start(f32[768]{0:T(1024)S(1)} %convert_element_type.137) | copy-start | bytes 9220
  47.6 7.8 copy-start.25
  70.5 1.2 copy-start.7
  71.7 6.0 copy-start.5
  72.8 98.1 %all-gather.10.cloned.1.call-start = ((), (), s32[]{:S(2)}) async-start(), calls=%async_computation.3 | async-start | bytes 7077888 | tf_op jit(solution)/shard_map/all_gather | solution.py:127
  75.6 201.1 %all-gather.16.cloned.1.call-start = ((), (), s32[]{:S(2)}) async-start(), calls=%async_computation.6 | async-start | bytes 5308416 | tf_op jit(solution)/shard_map/all_gather | solution.py:79
  76.2 209.3 %all-gather.18.cloned.1.call-start = ((), (), s32[]{:S(2)}) async-start(), calls=%async_computation.7 | async-start | bytes 5308416 | tf_op jit(solution)/shard_map/all_gather | solution.py:141
  76.8 346.2 %reduce-scatter.3.cloned.1.call-start = ((), (), s32[]{:S(2)}) async-start(), calls=%async_computation.8 | async-start | bytes 28311552 | tf_op jit(solution)/shard_map/reduce_scatter | solution.py:194
  220.6 11.1 %copy-start.12 = (bf16[4,128,12,64]{1,0,3,2:T(4,128)(2,1)S(1)}, bf16[4,128,12,64]{1,0,3,2:T(4,128)(2,1)}, u32[]{:S(2)}) copy-start(bf16[4,128,12,64]{1,0,3,2:T(4,128)(2,1)} %reshape.254) | copy-start | bytes 2359300
  265.3 0.7 copy-start.31
  265.3 10.1 %copy-start = (bf16[4,128,768]{2,1,0:T(8,128)(2,1)S(1)}, bf16[4,128,768]{2,1,0:T(8,128)(2,1)}, u32[]{:S(2)}) copy-start(bf16[4,128,768]{2,1,0:T(8,128)(2,1)} %param.15) | copy-start | bytes 2359300
  265.3 363.6 %reduce-scatter.5.cloned.1.call-start = ((), (), s32[]{:S(2)}) async-start(), calls=%async_computation.9 | async-start | bytes 31850496 | tf_op jit(solution)/shard_map/reduce_scatter | solution.py:240
  285.6 19.4 %copy-start.2 = (f32[512,3072]{1,0:T(8,128)S(1)}, f32[512,3072]{1,0:T(8,128)}, u32[]{:S(2)}) copy-start(f32[512,3072]{1,0:T(8,128)} %fusion.83) | copy-start | bytes 18874372
  305.0 11.0 %copy-start.8 = (bf16[512,3072]{1,0:T(8,128)(2,1)}, bf16[512,3072]{1,0:T(8,128)(2,1)S(1)}, u32[]{:S(2)}) copy-start(bf16[512,3072]{1,0:T(8,128)(2,1)S(1)} %get-tuple-element.39) | copy-start | bytes 9437188
  332.5 3.0 copy-start.3
  335.5 0.9 copy-start.9
  338.5 86.7 %copy-start.18 = (f32[4,128,16]{1,2,0:T(8,128)S(1)}, f32[4,128,16]{1,2,0:T(8,128)}, u32[]{:S(2)}) copy-start(f32[4,128,16]{1,2,0:T(8,128)} %copy-done.17) | copy-start | bytes 98308
  340.6 85.1 %copy-start.16 = (f32[4,128,16]{1,2,0:T(8,128)S(1)}, f32[4,128,16]{1,2,0:T(8,128)}, u32[]{:S(2)}) copy-start(f32[4,128,16]{1,2,0:T(8,128)} %copy-done.15) | copy-start | bytes 98308
  423.0 2.4 copy-start.4
  425.5 1.3 slice-start
  427.0 4.2 copy-start.14
  429.7 1.5 copy-start.13
  455.5 0.7 copy-start.30
  455.5 0.7 copy-start.29
  455.5 310.6 %all-reduce.22.cloned.1.call-start = ((), (), s32[]{:S(2)}) async-start(), calls=%async_computation.10 | async-start | bytes 7077888 | tf_op jit(solution)/shard_map/psum | solution.py:254
  629.0 6.1 copy-start.11
  635.1 5.9 copy-start.1
  635.1 5.9 copy-start.10
  635.1 5.9 copy-start.32
  641.0 1.9 copy-start.20
  641.0 1.9 copy-start.22
  641.0 1.9 copy-start.24
  642.9 5.4 copy-start.28
  642.9 6.5 copy-start.26
  648.2 1.2 copy-start.6
  695.3 78.0 %copy-start.33 = (f32[96]{0:T(128)}, f32[96]{0:T(128)S(1)}, u32[]{:S(2)}) copy-start(f32[96]{0:T(128)S(1)} %dynamic_slice.26) | copy-start | bytes 1156
Sparse Core Ops, SparseCore 0:
  9.9 36.8 all-gather.7
  48.7 24.0 all-gather.13
  75.2 46.6 all-gather.11
  124.2 46.6 all-gather.9
  172.7 38.9 all-gather.15
  213.4 38.8 all-gather.17
  265.5 157.4 reduce-scatter.2
  455.7 173.2 reduce-scatter.4
  631.3 134.7 all-reduce.21
where the time goes:
time: 787 us; the launch traced here: 781 us
  waiting for transfers between devices  383 us (49%)
  matrix products  176 us (22%)
  blocking collectives  80.3 us (10%)
  other arithmetic  72.3 us (9%)
  local copies, waits for them, and re-layouts  51.7 us (7%)
  between operations  16.3 us (2%)
    reduce_scatter x1, waiting for transfers between devices, on_device(): lax.psum_scatter(jnp.concatenate([jnp.einsum('rc,rk->ck', input_one, grad...  173 us
    reduce_scatter x1, waiting for transfers between devices, on_device(): lax.psum_scatter(key_terms, 'fsdp', scatter_dimension=1, tiled=True)  82.4 us
    psum x1, waiting for transfers between devices, on_device(): owned = lax.psum(owned, 'rep')  64.2 us
    psum x1, blocking collectives, on_device(): lax.psum((local_vectors[0], local_vectors[1], local_vectors[2], local_vec...  44.4 us
    all_gather x1, waiting for transfers between devices, on_device(): lax.all_gather(key_flat, 'fsdp', axis=1, tiled=True)  37.4 us
    unnamed x1, blocking collectives  26.5 us
    all_gather x1, waiting for transfers between devices, on_device(): lax.all_gather(value_flat, 'fsdp', axis=1, tiled=True)  23.9 us
    dot_general x1, matrix products, on_device(): jnp.einsum('sqhd,skhd->shqk', grad_heads, values, preferred_element_type=...  20.5 us
  transfers between devices with their start and end apart: 9, of which 5 were waited for; matrix products, arithmetic and copies ran while one was open for 33% of the time, Pallas kernels for 0%

commit v1 on v0

v1 whole, which is shorter than its diff:
```python
import functools

import jax
import jax.numpy as jnp
from jax import lax
from jax.experimental import pallas as pl
from jax.experimental.pallas import tpu as pltpu
from jax.sharding import PartitionSpec as P

H = 12
HD = 64
ROT = 16

EPS = 1e-05
NEG = -1e30

F32 = jnp.float32
BF16 = jnp.bfloat16


def dot(a, b, dims):
    return lax.dot_general(a, b, (dims, ((), ())), preferred_element_type=F32)


def attention_kernel(
    span, heads, slot, q_in, k_in, v_in, g_in, first_in,
    o_out, gq_out, gk_out, gv_out,
    qs, ks, vs, gs, o_turned, gq_turned, gk_sum, gv_sum,
):
    length = q_in.shape[1]
    blocks = length // span
    tile = 256
    for f in range(blocks):
        at = pl.ds(pl.multiple_of(slot[f] * span, span), span)
        to = slice(f * span, (f + 1) * span)
        for source, kept in ((q_in, qs), (k_in, ks), (v_in, vs), (g_in, gs)):
            rows = source[0, at, :]
            for h in range(heads):
                kept[h, to, :] = rows[:, h * HD : (h + 1) * HD]

    def one_head(h, carry):
        keys = ks[h]
        values = vs[h]
        keys_turned = keys.astype(F32).T.astype(BF16)
        values_turned = values.astype(F32).T.astype(BF16)
        for i in range(length // tile):
            seen = (i + 1) * tile
            here = slice(i * tile, seen)
            query = qs[h, here, :]
            grad = gs[h, here, :]
            first = first_in[0, :, here]
            raw = dot(keys[:seen], query, ((1,), (1,))) * 0.125
            key_index = lax.broadcasted_iota(jnp.int32, (seen, tile), 0)
            query_index = i * tile + lax.broadcasted_iota(jnp.int32, (seen, tile), 1)
            raw = jnp.where((key_index >= first) & (key_index <= query_index), raw, NEG)
            weights = jnp.exp(raw - jnp.max(raw, axis=0, keepdims=True))
            probs = weights * (1.0 / jnp.sum(weights, axis=0, keepdims=True))
            grad_probs = dot(values[:seen], grad, ((1,), (1,)))
            carried = jnp.sum(probs * grad_probs, axis=0, keepdims=True)
            grad_scores = (probs * (grad_probs - carried)).astype(BF16)
            low = probs.astype(BF16)
            o_turned[h, :, here] = dot(values_turned[:, :seen], low, ((1,), (0,)))
            gq_turned[h, :, here] = dot(keys_turned[:, :seen], grad_scores, ((1,), (0,)))
            gk_part = dot(grad_scores, query, ((1,), (0,)))
            gv_part = dot(low, grad, ((1,), (0,)))
            if i > 0:
                old = slice(0, i * tile)
                gk_sum[h, old, :] += gk_part[: i * tile]
                gv_sum[h, old, :] += gv_part[: i * tile]
            gk_sum[h, here, :] = gk_part[i * tile :]
            gv_sum[h, here, :] = gv_part[i * tile :]
        return carry

    lax.fori_loop(0, heads, one_head, 0)
    for f in range(blocks):
        at = pl.ds(pl.multiple_of(slot[f] * span, span), span)
        to = slice(f * span, (f + 1) * span)
        o_out[0, at, :] = jnp.concatenate(
            [o_turned[h, :, to].T for h in range(heads)], axis=1
        ).astype(BF16)
        gq_out[0, at, :] = (
            jnp.concatenate([gq_turned[h, :, to].T for h in range(heads)], axis=1) * 0.125
        )
        gk_out[0, at, :] = (
            jnp.concatenate([gk_sum[h, to, :] for h in range(heads)], axis=1) * 0.125
        )
        gv_out[0, at, :] = jnp.concatenate(
            [gv_sum[h, to, :] for h in range(heads)], axis=1
        ).astype(BF16)


def attention(slot, query, key, value, grad, first, span):
    count, length, columns = query.shape
    heads = columns // HD
    block = pl.BlockSpec((1, length, columns), lambda s, slot: (s, 0, 0))
    shape = (count, length, columns)
    return pl.pallas_call(
        functools.partial(attention_kernel, span, heads),
        grid_spec=pltpu.PrefetchScalarGridSpec(
            num_scalar_prefetch=1,
            grid=(count,),
            in_specs=[block] * 4 + [pl.BlockSpec((1, 1, length), lambda s, slot: (s, 0, 0))],
            out_specs=[block] * 4,
            scratch_shapes=[pltpu.VMEM((heads, length, HD), BF16)] * 4
            + [pltpu.VMEM((heads, HD, length), F32)] * 2
            + [pltpu.VMEM((heads, length, HD), F32)] * 2,
        ),
        out_shape=[
            jax.ShapeDtypeStruct(shape, BF16),
            jax.ShapeDtypeStruct(shape, F32),
            jax.ShapeDtypeStruct(shape, F32),
            jax.ShapeDtypeStruct(shape, BF16),
        ],
        compiler_params=pltpu.CompilerParams(vmem_limit_bytes=56 * 2**20),
        cost_estimate=pl.CostEstimate(
            flops=6 * 2 * count * heads * length * length * 160,
            bytes_accessed=count * length * columns * 20,
            transcendentals=count * heads * length * length,
        ),
        name="attention",
    )(slot, query, key, value, grad, first)


def on_device(
    layer_input,
    positions,
    cotangent,
    w_qkv,
    w_out,
    w_up,
    w_down,
    ln1_gain,
    ln1_bias,
    ln2_gain,
    ln2_bias,
    qkv_bias,
    out_bias,
    up_bias,
    down_bias,
):
    seqs, span, width = layer_input.shape
    shards = lax.axis_size("fsdp")
    reps = lax.axis_size("rep")
    low_count = shards // seqs
    pair = 2 if reps % 2 == 0 and H % (2 * low_count) == 0 else 1
    parts = pair * low_count
    me = lax.axis_index("fsdp")
    rep = lax.axis_index("rep")
    chip = me // low_count
    low = me % low_count
    parity = me % 2
    pair_bit = rep % pair
    part = pair_bit * low_count + low
    high_masks = []
    while low_count * 2 ** len(high_masks) < shards:
        high_masks.append(2 ** len(high_masks))
    phases = len(high_masks)
    own_rows = w_qkv.shape[0]
    q_cols = H // parts * HD
    f_cols = w_up.shape[1] // parts

    def swap_fsdp(v, mask):
        return lax.ppermute(v, "fsdp", [(i, i ^ mask) for i in range(shards)])

    def swap_mixed(v, phase):
        def to(i):
            mask = high_masks[phase] if i % 2 == 0 else high_masks[phases - 1 - phase]
            return i ^ (mask * low_count)

        return lax.ppermute(v, "fsdp", [(i, to(i)) for i in range(shards)])

    def swap_rep(v, mask):
        return lax.ppermute(v, "rep", [(i, i ^ mask) for i in range(reps)])

    def pick(v, index, axis=0):
        return lax.dynamic_index_in_dim(v, index, axis, keepdims=False)

    slot_mask = []
    for s in range(seqs):
        even = sum(high_masks[p] for p in range(phases) if s >> p & 1)
        odd = sum(high_masks[phases - 1 - p] for p in range(phases) if s >> p & 1)
        slot_mask.append(jnp.where(parity == 0, even, odd))
    inverse_slot = jnp.zeros((seqs,), jnp.int32)
    for s in range(seqs):
        inverse_slot = inverse_slot.at[slot_mask[s]].set(s)

    def gather_rows(block):
        slots = [block]
        for p in range(phases):
            slots = slots + [swap_mixed(v, p) for v in slots]
        stacked = jnp.stack(slots)
        return jnp.concatenate([pick(stacked, inverse_slot[i ^ chip]) for i in range(seqs)])

    def take_part(w, index, groups):
        rows = w.shape[0]
        step = w.shape[1] // groups // parts
        return jnp.concatenate(
            [
                lax.dynamic_slice(
                    w, (0, g * (w.shape[1] // groups) + index * step), (rows, step)
                )
                for g in range(groups)
            ],
            axis=1,
        )

    def take_chunk(index):
        return [
            jnp.concatenate([take_part(w_qkv, index, 3), take_part(w_out, index, 1)], axis=1),
            take_part(w_up, index, 1),
            take_part(w_down, index, 1),
        ]

    def gather_low(own, messages):
        blocks = [own] + [swap_fsdp(m, o) for o, m in zip(range(1, low_count), messages)]
        stacked = jnp.stack(blocks)
        return jnp.concatenate([pick(stacked, i ^ low) for i in range(low_count)])

    def spread_tokens(v):
        mine = [pick(v, chip)]
        for j in range(1, seqs):
            mine.append(swap_fsdp(pick(v, chip ^ j), j * low_count))
        mine = jnp.stack(mine)
        both = [mine]
        if pair == 2:
            both.append(swap_rep(mine, 1))
        both = jnp.stack(both)
        cores = [both] + [swap_fsdp(both, o) for o in range(1, low_count)]
        return jnp.stack(cores, axis=1)

    def collect_tokens(v):
        total = v[:, 0].astype(F32)
        for o in range(1, low_count):
            total = total + swap_fsdp(v[:, o], o).astype(F32)
        total = total.astype(BF16)
        mine = total[0]
        if pair == 2:
            mine = (mine.astype(F32) + swap_rep(total[1], 1).astype(F32)).astype(BF16)
        blocks = [mine[0]] + [swap_fsdp(mine[j], j * low_count) for j in range(1, seqs)]
        stacked = jnp.stack(blocks)
        return jnp.stack([pick(stacked, s ^ chip) for s in range(seqs)])

    own_chunks = take_chunk(part)
    sent_chunks = [take_chunk(pair_bit * low_count + (low ^ o)) for o in range(1, low_count)]

    def weight(number):
        return gather_rows(gather_low(own_chunks[number], [m[number] for m in sent_chunks]))

    packed = jnp.concatenate(
        [ln1_gain, ln1_bias, ln2_gain, ln2_bias, qkv_bias, out_bias, up_bias, down_bias]
    )[None]
    mask = 1
    vectors = packed
    while mask < shards:
        other = swap_fsdp(vectors, mask)
        bit = (me & mask) != 0
        vectors = jnp.concatenate(
            [jnp.where(bit, other, vectors), jnp.where(bit, vectors, other)]
        )
        mask *= 2
    small = []
    at = 0
    for v in (ln1_gain, ln1_bias, ln2_gain, ln2_bias, qkv_bias, out_bias, up_bias, down_bias):
        small.append(vectors[:, at : at + v.shape[0]].reshape(-1).astype(F32))
        at += v.shape[0]
    gain_one, shift_one, gain_two, shift_two, bias_qkv, bias_out, bias_up, bias_down = small

    where = spread_tokens(positions)
    tokens = spread_tokens(layer_input)
    grads = spread_tokens(cotangent)
    rows = pair * shards * span
    source = tokens.reshape(rows, width).astype(F32)
    grad_out = grads.reshape(rows, width)

    block_index = jnp.arange(shards, dtype=jnp.int32)
    slot = ((block_index % low_count) ^ low) * seqs + ((block_index // low_count) ^ chip)
    length = shards * span
    blocks = where.reshape(pair, shards, span)
    in_order = jnp.concatenate([pick(blocks, slot[f], 1) for f in range(shards)], axis=1)
    in_order = in_order.reshape(pair, 1, length)
    first_seen = jnp.arange(length, dtype=jnp.int32) - in_order

    inverse = 10000.0 ** (-jnp.arange(0, ROT, 2, dtype=F32) / ROT)
    phase = where.reshape(rows).astype(F32)[:, None] * inverse
    cosine = jnp.cos(phase)
    sine = jnp.sin(phase)
    half = ROT // 2
    still = jnp.zeros((rows, HD - ROT), F32)
    one_cos = jnp.concatenate([cosine, cosine, still + 1.0], axis=1)
    one_sin = jnp.concatenate([-sine, sine, still], axis=1)
    cos_cols = jnp.tile(one_cos, (1, q_cols // HD))
    sin_cols = jnp.tile(one_sin, (1, q_cols // HD))
    in_first = (jnp.arange(q_cols) % HD) < half

    def turned(v):
        return jnp.where(in_first, jnp.roll(v, -half, axis=1), jnp.roll(v, half, axis=1))

    def rotate(v):
        return v * cos_cols + turned(v) * sin_cols

    def rotate_back(v):
        return v * cos_cols - turned(v) * sin_cols

    mean = jnp.mean(source, axis=1, keepdims=True)
    centred = source - mean
    scale = lax.rsqrt(jnp.mean(centred * centred, axis=1, keepdims=True) + EPS)
    normed = centred * scale
    input_one = (normed * gain_one + shift_one).astype(BF16)
    input_two = (normed * gain_two + shift_two).astype(BF16)

    chunk = weight(0)
    part_qkv = chunk[:, : 3 * q_cols]
    part_out = chunk[:, 3 * q_cols :]
    part_up = weight(1)
    part_down = weight(2)

    qkv_part_bias = take_part(bias_qkv[None], part, 3)
    up_part_bias = take_part(bias_up[None], part, 1)
    qkv = dot(input_one, part_qkv, ((1,), (0,))) + qkv_part_bias
    query = rotate(qkv[:, :q_cols]).astype(BF16)
    key = rotate(qkv[:, q_cols : 2 * q_cols]).astype(BF16)
    value = qkv[:, 2 * q_cols :].astype(BF16)
    grad_mixed = dot(grad_out, part_out, ((1,), (0,))).astype(BF16)

    up = dot(input_two, part_up, ((1,), (0,))) + up_part_bias
    grad_hidden = dot(grad_out, part_down, ((1,), (0,)))
    bell = 0.5 * (1.0 + lax.erf(up * (0.5**0.5)))
    hidden = (up * bell).astype(BF16)
    slope = bell + up * jnp.exp(-0.5 * up * up) * 0.3989422804014327
    grad_up = (grad_hidden * slope).astype(BF16)

    per_seq = lambda v: v.reshape(pair, length, q_cols)
    mixed, grad_query, grad_key, grad_value = attention(
        slot, per_seq(query), per_seq(key), per_seq(value), per_seq(grad_mixed), first_seen, span
    )
    flat = lambda v: v.reshape(rows, q_cols)
    attended = flat(mixed)
    grad_qkv = jnp.concatenate(
        [
            rotate_back(flat(grad_query)).astype(BF16),
            rotate_back(flat(grad_key)).astype(BF16),
            flat(grad_value),
        ],
        axis=1,
    )

    shaped = (pair, low_count, seqs, span, width)
    out_part = dot(attended, part_out, ((1,), (1,))) + dot(hidden, part_down, ((1,), (1,)))
    out_sum = collect_tokens(out_part.astype(BF16).reshape(shaped))
    output = (
        layer_input.astype(F32) + out_sum.astype(F32) + bias_out + bias_down
    ).astype(BF16)

    grad_one = dot(grad_qkv, part_qkv, ((1,), (1,)))
    grad_two = dot(grad_up, part_up, ((1,), (1,)))
    both = grad_one * gain_one + grad_two * gain_two
    grad_sum = collect_tokens(both.astype(BF16).reshape(shaped)).astype(F32)
    mine = layer_input.astype(F32)
    mine_mean = jnp.mean(mine, axis=-1, keepdims=True)
    mine_centred = mine - mine_mean
    mine_scale = lax.rsqrt(jnp.mean(mine_centred * mine_centred, axis=-1, keepdims=True) + EPS)
    mine_normed = mine_centred * mine_scale
    pulled = (
        grad_sum
        - jnp.mean(grad_sum, axis=-1, keepdims=True)
        - mine_normed * jnp.mean(grad_sum * mine_normed, axis=-1, keepdims=True)
    ) * mine_scale
    grad_input = (cotangent.astype(F32) + pulled).astype(BF16)

    def scatter_rows(v):
        blocks = v.reshape(seqs, width // seqs, v.shape[1])
        slots = [pick(blocks, chip ^ slot_mask[s]) for s in range(seqs)]
        for p in reversed(range(phases)):
            half_count = len(slots) // 2
            slots = [
                (kept.astype(F32) + swap_mixed(sent, p).astype(F32)).astype(BF16)
                for kept, sent in zip(slots[:half_count], slots[half_count:])
            ]
        return slots[0]

    def finish(v):
        v = scatter_rows(v.astype(BF16))
        mask = pair
        while mask < reps:
            v = (v.astype(F32) + swap_rep(v, mask).astype(F32)).astype(BF16)
            mask *= 2
        v = v.reshape(low_count, own_rows, v.shape[1])
        blocks = [pick(v, low)]
        for o in range(1, low_count):
            blocks.append(swap_fsdp(pick(v, low ^ o), o))
        blocks = jnp.stack(blocks)
        if pair == 2:
            blocks = jnp.concatenate([blocks, swap_rep(blocks, 1)])
        return [pick(blocks, i ^ part) for i in range(parts)]

    chunk_grads = finish(
        jnp.concatenate(
            [dot(input_one, grad_qkv, ((0,), (0,))), dot(grad_out, attended, ((0,), (0,)))], axis=1
        )
    )
    up_grads = finish(dot(input_two, grad_up, ((0,), (0,))))
    down_grads = finish(dot(grad_out, hidden, ((0,), (0,))))
    grad_w_qkv = jnp.concatenate(
        [c[:, g * q_cols : (g + 1) * q_cols] for g in range(3) for c in chunk_grads], axis=1
    ).astype(F32)
    grad_w_out = jnp.concatenate([c[:, 3 * q_cols :] for c in chunk_grads], axis=1).astype(F32)
    grad_w_up = jnp.concatenate(up_grads, axis=1).astype(F32)
    grad_w_down = jnp.concatenate(down_grads, axis=1).astype(F32)

    def place(v, groups):
        total = jnp.zeros((groups, parts, v.shape[0] // groups), F32)
        return lax.dynamic_update_slice(
            total, v.reshape(groups, 1, v.shape[0] // groups), (0, part, 0)
        ).reshape(-1)

    local = [
        jnp.sum(grad_one * normed, axis=0),
        jnp.sum(grad_one, axis=0),
        jnp.sum(grad_two * normed, axis=0),
        jnp.sum(grad_two, axis=0),
        place(jnp.sum(grad_qkv.astype(F32), axis=0), 3),
        jnp.sum(cotangent.astype(F32), axis=(0, 1)),
        place(jnp.sum(grad_up.astype(F32), axis=0), 1),
    ]
    owned = jnp.concatenate([v.reshape(shards, -1) for v in local], axis=1)
    mask = shards // 2
    while mask:
        count = owned.shape[0] // 2
        bit = (me & mask) != 0
        sent = jnp.where(bit, owned[:count], owned[count:])
        kept = jnp.where(bit, owned[count:], owned[:count])
        owned = kept + swap_fsdp(sent, mask)
        mask //= 2
    mask = 1
    while mask < reps:
        owned = owned + swap_rep(owned, mask)
        mask *= 2
    owned = owned[0]
    vector_outs = []
    at = 0
    for v in local:
        size = v.shape[0] // shards
        vector_outs.append(owned[at : at + size])
        at += size
    return (
        output,
        grad_input,
        grad_w_qkv,
        grad_w_out,
        grad_w_up,
        grad_w_down,
        *vector_outs,
        vector_outs[5],
    )


def solution(mesh):
    tokens = P("rep", "fsdp", None)
    matrix = P("fsdp", None)
    vector = P("fsdp")
    return jax.shard_map(
        on_device,
        mesh=mesh,
        in_specs=(tokens, P("rep", "fsdp"), tokens) + (matrix,) * 4 + (vector,) * 8,
        out_specs=(tokens, tokens) + (matrix,) * 4 + (vector,) * 8,
        check_vma=False,
    )
```

time: 787 us -> 418 us (0.53)
  waiting for transfers between devices: 383 us -> 125 us
  matrix products: 176 us -> 41.8 us
  blocking collectives: 80.3 us -> 0 us
  starting transfers between devices: 0.82 us -> 64.9 us
  Pallas kernels: 0 us -> 29.4 us
  local copies, waits for them, and re-layouts: 51.7 us -> 68.5 us
  other arithmetic: 72.3 us -> 55.6 us
  between operations: 16.3 us -> 25.5 us
    reduce_scatter x2 -> x0, waiting for transfers between devices: 255 us -> none  [the longest x1 173 us: on_device(): lax.psum_scatter(jnp.concatenate([jnp.einsum('rc,rk->ck', input_one, grad...]
    dot_general x19 -> x12, matrix products: 176 us -> 41.8 us  [dot(): return lax.dot_general(a, b, (dims, ((), ())), preferred_element_type=F32)]
    ppermute x0 -> x63, waiting for transfers between devices: none -> 125 us  [the longest x13 84.5 us: swap_rep(): return lax.ppermute(v, 'rep', [(i, i ^ mask) for i in range(reps)])]
    ppermute x0 -> x63, starting transfers between devices: none -> 64.9 us  [the longest x32 26.1 us: swap_fsdp(): return lax.ppermute(v, 'fsdp', [(i, i ^ mask) for i in range(shards)])]
    psum x1 -> x0, waiting for transfers between devices: 64.2 us -> none  [on_device(): owned = lax.psum(owned, 'rep')]
    all_gather x6 -> x0, waiting for transfers between devices: 61.3 us -> none  [the longest x1 37.4 us: on_device(): lax.all_gather(key_flat, 'fsdp', axis=1, tiled=True)]
    psum x1 -> x0, blocking collectives: 44.4 us -> none  [on_device(): lax.psum((local_vectors[0], local_vectors[1], local_vectors[2], local_vec...]
    concatenate x3 -> x10, other arithmetic: 39.2 us -> 5.81 us  [the longest x3 3.05 us: finish(): blocks = jnp.concatenate([blocks, swap_rep(blocks, 1)])]
  transfers between devices with their start and end apart: 9 -> 63, of which waited for: 5 -> 25; matrix products, arithmetic and copies ran while one was open for 33% -> 25% of each run, Pallas kernels for 0% -> 0%
where the time goes in v1:
time: 418 us; the launch traced here: 410 us
  waiting for transfers between devices  125 us (30%)
  local copies, waits for them, and re-layouts  68.5 us (16%)
  starting transfers between devices  64.9 us (16%)
  other arithmetic  55.6 us (13%)
  matrix products  41.8 us (10%)
  Pallas kernels  29.4 us (7%)
  between operations  25.5 us (6%)
    ppermute x13, waiting for transfers between devices, swap_rep(): return lax.ppermute(v, 'rep', [(i, i ^ mask) for i in range(reps)])  84.5 us
    dot_general x12, matrix products, dot(): return lax.dot_general(a, b, (dims, ((), ())), preferred_element_type=F32)  41.8 us
    pallas_call x1, Pallas kernels, attention(): pl.pallas_call(functools.partial(attention_kernel, span, heads), grid_spe...  29.4 us
    ppermute x32, starting transfers between devices, swap_fsdp(): return lax.ppermute(v, 'fsdp', [(i, i ^ mask) for i in range(shards)])  26.1 us
    ppermute x32, waiting for transfers between devices, swap_fsdp(): return lax.ppermute(v, 'fsdp', [(i, i ^ mask) for i in range(shards)])  21.9 us
    ppermute x18, starting transfers between devices, swap_mixed(): return lax.ppermute(v, 'fsdp', [(i, to(i)) for i in range(shards)])  20.2 us
    ppermute x13, starting transfers between devices, swap_rep(): return lax.ppermute(v, 'rep', [(i, i ^ mask) for i in range(reps)])  18.6 us
    ppermute x18, waiting for transfers between devices, swap_mixed(): return lax.ppermute(v, 'fsdp', [(i, to(i)) for i in range(shards)])  18.2 us
  transfers between devices with their start and end apart: 63, of which 25 were waited for; matrix products, arithmetic and copies ran while one was open for 25% of the time, Pallas kernels for 0%

profile of v1, /device:TPU:0, one launch (start us, length us, event | category | flops | bytes accessed | tf_op | source)
XLA Modules:
  0.0 410.2 jit_solution(2258381048519223533)
XLA Ops:
  1.5 2.9 collective-permute-start.12
  6.0 5.5 %concatenate.124 = bf16[1248]{0:T(1024)(128)(2,1)S(1)} concatenate(bf16[96]{0:T(256)(128)(2,1)} %param.30, bf16[96]{0:T(256)(128)(2,1)} %param.31, bf16[96]{0:T(256)(128)(2,1)} %param.32, bf16[96]{0:T(256)(128)(2,1)} %param.33, bf16[288]{0:T(512)(128)(2,1)} %param.34, bf16[96]{0:T(256)(128)(2,1)} %param.35, bf16[384]{0:T(512)(128)(2,1)} %param.36, bf16[96]{0:T(256)(128)(2,1)} %param.37), dimensions={0} | concatenate | bytes 4992 | tf_op jit(solution)/shard_map/concatenate | solution.py:249
  63.0 4.3 %collective-permute-done.1 = bf16[128,768]{1,0:T(8,128)(2,1)S(1)} collective-permute-done((bf16[128,768]{1,0:T(8,128)(2,1)S(1)}, bf16[128,768]{1,0:T(8,128)(2,1)S(1)}, u32[]{:S(2)}, u32[]{:S(2)}) %collective-permute-start.1) | collective-permute-done | bytes 196640 | tf_op jit(solution)/shard_map/ppermute | solution.py:163
  73.0 2.3 collective-permute-start.24
  75.3 8.4 %collective-permute-done.3 = bf16[4,128,768]{2,1,0:T(8,128)(2,1)S(1)} collective-permute-done((bf16[4,128,768]{2,1,0:T(8,128)(2,1)S(1)}, bf16[4,128,768]{2,1,0:T(8,128)(2,1)S(1)}, u32[]{:S(2)}, u32[]{:S(2)}) %collective-permute-start.3) | collective-permute-done | bytes 786464 | tf_op jit(solution)/shard_map/ppermute | solution.py:173
  90.6 3.8 collective-permute-done.19
  110.1 2.4 collective-permute-done.11
  113.9 5.3 %collective-permute-done.20 = bf16[4,128,768]{2,1,0:T(8,128)(2,1)S(1)} collective-permute-done((bf16[4,128,768]{2,1,0:T(8,128)(2,1)S(1)}, bf16[4,128,768]{2,1,0:T(8,128)(2,1)S(1)}, u32[]{:S(2)}, u32[]{:S(2)}) %collective-permute-start.20) | collective-permute-done | bytes 786464 | tf_op jit(solution)/shard_map/ppermute | solution.py:173
  122.8 3.6 add_convert_fusion.3
  131.0 3.0 fusion.104
  136.4 2.2 copy.87
  138.7 2.2 copy.85
  140.9 6.4 %fusion.25 = (bf16[2048,192]{0,1:T(8,128)(2,1)}, bf16[2048,192]{0,1:T(8,128)(2,1)}) fusion(f32[2048,576]{0,1:T(8,128)} %copy-done.1, f32[2048,8]{0,1:T(8,128)} %get-tuple-element.82, f32[2048,184]{0,1:T(8,128)} %get-tuple-element.86, f32[2048,184]{0,1:T(8,128)} %get-tuple-element.85, f32[2048,8]{0,1:T(8,128)S(1)} %get-tuple-element.81, ...), kind=kLoop, calls=%fused_computation.65 | loop fusion | flops 5505024 | bytes 12058816 | tf_op jit(solution)/shard_map/convert_element_type | solution.py:321
  147.3 2.2 copy.84
  149.5 2.2 copy.83
  151.7 29.4 %attention.1 = (bf16[2,1024,192]{2,1,0:T(8,128)(2,1)}, f32[2,1024,192]{2,1,0:T(8,128)}, f32[2,1024,192]{2,1,0:T(8,128)}, bf16[2,1024,192]{2,1,0:T(8,128)(2,1)}) custom-call(s32[8]{0:T(128)} %copy-done.43, bf16[2,1024,192]{2,1,0:T(8,128)(2,1)} %bitcast.381, bf16[2,1024,192]{2,1,0:T(8,128)(2,1)} %bitcast.380, bf16[2,1024,192]{2,1,0:T(8,128)(2,1)} %bitcast.378, ...), custom_call_target="tpu_custom_call" | custom-call | flops 12079595520 | bytes 7864320 | tf_op jit(solution)/shard_map/attention/pallas_call | solution.py:97
  181.2 2.8 copy.96
  185.5 3.8 fusion.108
  189.3 2.8 copy.91
  193.6 3.9 fusion.106
  197.5 3.0 copy.105
  200.5 4.7 %copy.104 = bf16[768,2048]{1,0:T(8,128)(2,1)} copy(bf16[768,2048]{0,1:T(8,128)(2,1)} %bitcast.356) | data formatting | bytes 6291456 | tf_op jit(solution)/shard_map/dot_general | solution.py:22
  205.2 2.2 copy.101
  207.4 5.5 %fusion.27 = (bf16[2048,192]{0,1:T(8,128)(2,1)S(1)}, bf16[2048,192]{0,1:T(8,128)(2,1)S(1)}) fusion(f32[2048,192]{0,1:T(8,128)} %copy.91, f32[2048,8]{0,1:T(8,128)} %get-tuple-element.90, f32[2048,184]{0,1:T(8,128)} %get-tuple-element.92, f32[2048,184]{0,1:T(8,128)} %get-tuple-element.91, f32[2048,8]{0,1:T(8,128)} %get-tuple-element.89, ...), kind=kLoop, calls=%fused_computation.67 | loop fusion | flops 5505024 | bytes 12058816 | tf_op jit(solution)/shard_map/convert_element_type | solution.py:340
  212.9 4.8 %fusion.36 = f32[2048,768]{1,0:T(8,128)} fusion(bf16[768,768]{1,0:T(8,128)(2,1)S(1)} %copy-done.24, bf16[2048,192]{0,1:T(8,128)(2,1)S(1)} %copy-done.13, bf16[2048,192]{0,1:T(8,128)(2,1)S(1)} %get-tuple-element.120, bf16[2048,192]{0,1:T(8,128)(2,1)S(1)} %get-tuple-element.119), kind=kOutput, calls=%fused_computation.100 | convolution fusion | flops 1819017216 | bytes 9633792 | tf_op jit(solution)/shard_map/dot_general | solution.py:22
  217.7 2.6 fusion.32
  224.4 7.2 %multiply_convert_fusion = (bf16[2048,768]{1,0:T(8,128)(2,1)S(1)}, f32[2048,768]{1,0:T(8,128)S(1)}) fusion(f32[768]{0:T(1024)S(1)} %dynamic-slice.42, bf16[2048,768]{1,0:T(8,128)(2,1)S(1)} %copy-done.16, bf16[192,768]{1,0:T(8,128)(2,1)S(1)} %copy-done.31, bf16[192,768]{1,0:T(8,128)(2,1)S(1)} %copy-done.32, bf16[192,768]{1,0:T(8,128)(2,1)S(1)} %copy-done.33, ...), kind=kOutput, calls=%fused_computation.14 | convolution fusion | flops 2430074880 | bytes 13765632 | tf_op jit(solution)/shard_map/dot_general | solution.py:22
  231.7 2.7 convolution_convert_fusion.1
  234.4 2.7 fusion.53
  237.1 6.4 %convert_reduce_fusion = (f32[768]{0:T(1024)S(1)}, bf16[2048,768]{1,0:T(8,128)(2,1)S(1)}) fusion(f32[2048,768]{1,0:T(8,128)S(1)} %get-tuple-element.256, f32[768]{0:T(1024)S(1)} %dynamic-slice.42, bf16[2048,768]{1,0:T(8,128)(2,1)S(1)} %bitcast.350, bf16[192,768]{1,0:T(8,128)(2,1)S(1)} %copy-done.36, bf16[192,768]{1,0:T(8,128)(2,1)S(1)} %copy-done.37, ...), kind=kOutput, calls=%fused_computation.9 | convolution fusion | flops 2441084160 | bytes 13768704 | tf_op jit(solution)/shard_map/dot_general | solution.py:22
  245.2 2.7 convolution_convert_fusion.2
  247.9 6.4 %multiply_reduce_fusion = (f32[768]{0:T(1024)S(1)}, f32[768]{0:T(1024)S(1)}, f32[768]{0:T(1024)S(1)}, f32[768]{0:T(1024)S(1)}, bf16[2048,768]{1,0:T(8,128)(2,1)S(1)}) fusion(f32[2,2,4,128,768]{4,3,2,1,0:T(8,128)S(1)} %bitcast.352, f32[2048]{0:T(1024)S(1)} %bitcast.406, f32[2048]{0:T(1024)S(1)} %bitcast.404, f32[2048,768]{1,0:T(8,128)} %fusion.36, ...), kind=kOutput, calls=%fused_computation.10 | convolution fusion | flops 2439508992 | bytes 20088832 | tf_op jit(solution)/shard_map/dot_general | solution.py:22
  261.3 3.0 collective-permute-done.47
  267.8 6.7 %collective-permute-done.53 = bf16[192,768]{1,0:T(8,128)(2,1)S(1)} collective-permute-done((bf16[192,768]{1,0:T(8,128)(2,1)S(1)}, bf16[192,768]{1,0:T(8,128)(2,1)S(1)}, u32[]{:S(2)}, u32[]{:S(2)}) %collective-permute-start.53) | collective-permute-done | bytes 294944 | tf_op jit(solution)/shard_map/ppermute | solution.py:170
  277.1 4.1 %collective-permute-done.42 = bf16[192,768]{1,0:T(8,128)(2,1)S(1)} collective-permute-done((bf16[192,768]{1,0:T(8,128)(2,1)S(1)}, bf16[192,768]{1,0:T(8,128)(2,1)S(1)}, u32[]{:S(2)}, u32[]{:S(2)}) %collective-permute-start.42) | collective-permute-done | bytes 294944 | tf_op jit(solution)/shard_map/ppermute | solution.py:170
  281.3 2.6 collective-permute-start.49
  285.5 2.6 collective-permute-start.55
  288.2 19.5 %collective-permute-done.49 = bf16[192,768]{1,0:T(8,128)(2,1)S(1)} collective-permute-done((bf16[192,768]{1,0:T(8,128)(2,1)S(1)}, bf16[192,768]{1,0:T(8,128)(2,1)S(1)}, u32[]{:S(2)}, u32[]{:S(2)}) %collective-permute-start.49) | collective-permute-done | bytes 294944 | tf_op jit(solution)/shard_map/ppermute | solution.py:173
  307.8 11.2 %collective-permute-done.55 = bf16[192,768]{1,0:T(8,128)(2,1)S(1)} collective-permute-done((bf16[192,768]{1,0:T(8,128)(2,1)S(1)}, bf16[192,768]{1,0:T(8,128)(2,1)S(1)}, u32[]{:S(2)}, u32[]{:S(2)}) %collective-permute-start.55) | collective-permute-done | bytes 294944 | tf_op jit(solution)/shard_map/ppermute | solution.py:173
  327.0 4.4 %collective-permute-done.51 = bf16[2,96,768]{2,1,0:T(8,128)(2,1)} collective-permute-done((bf16[2,96,768]{2,1,0:T(8,128)(2,1)}, bf16[2,96,768]{2,1,0:T(8,128)(2,1)}, u32[]{:S(2)}, u32[]{:S(2)}) %collective-permute-start.51) | collective-permute-done | bytes 294944 | tf_op jit(solution)/shard_map/ppermute | solution.py:173
  332.4 4.3 %collective-permute-done.57 = bf16[2,96,768]{2,1,0:T(8,128)(2,1)} collective-permute-done((bf16[2,96,768]{2,1,0:T(8,128)(2,1)}, bf16[2,96,768]{2,1,0:T(8,128)(2,1)}, u32[]{:S(2)}, u32[]{:S(2)}) %collective-permute-start.57) | collective-permute-done | bytes 294944 | tf_op jit(solution)/shard_map/ppermute | solution.py:173
  344.9 15.4 %collective-permute-done.36 = bf16[4,128,768]{2,1,0:T(8,128)(2,1)S(1)} collective-permute-done((bf16[4,128,768]{2,1,0:T(8,128)(2,1)S(1)}, bf16[4,128,768]{2,1,0:T(8,128)(2,1)S(1)}, u32[]{:S(2)}, u32[]{:S(2)}) %collective-permute-start.36) | collective-permute-done | bytes 786464 | tf_op jit(solution)/shard_map/ppermute | solution.py:173
  364.2 11.2 %collective-permute-done.31 = bf16[4,128,768]{2,1,0:T(8,128)(2,1)S(1)} collective-permute-done((bf16[4,128,768]{2,1,0:T(8,128)(2,1)S(1)}, bf16[4,128,768]{2,1,0:T(8,128)(2,1)S(1)}, u32[]{:S(2)}, u32[]{:S(2)}) %collective-permute-start.31) | collective-permute-done | bytes 786464 | tf_op jit(solution)/shard_map/ppermute | solution.py:173
  381.1 2.9 collective-permute-done.34
  391.6 2.2 collective-permute-done.58
  394.5 3.1 collective-permute-done.59
  399.7 2.8 collective-permute-done.61
  402.5 2.9 collective-permute-start.62
  (371 shorter events, 135.7 us)
Async XLA Ops:
  1.5 43.3 %collective-permute-start.12 = (s32[128]{0:T(128)S(1)}, s32[128]{0:T(128)S(1)}, u32[]{:S(2)}, u32[]{:S(2)}) collective-permute-start(s32[128]{0:T(128)S(1)} %get-tuple-element.240), channel_id=1, source_target_pairs={{0,2},{1,3},{2,0},{3,1},{4,6},{5,7},{6,4},{7,5},{8,10},{9,11},{10,... | collective-permute-start | bytes 1544 | tf_op jit(solution)/shard_map/ppermute | solution.py:163
  4.5 40.5 %collective-permute-start.14 = (s32[128]{0:T(128)S(1)}, s32[128]{0:T(128)S(1)}, u32[]{:S(2)}, u32[]{:S(2)}) collective-permute-start(s32[128]{0:T(128)S(1)} %get-tuple-element.241), channel_id=1, source_target_pairs={{0,6},{1,7},{2,4},{3,5},{4,2},{5,3},{6,0},{7,1},{8,14},{9,15},{10,... | collective-permute-start | bytes 1544 | tf_op jit(solution)/shard_map/ppermute | solution.py:163
  6.0 41.0 %collective-permute-start.13 = (s32[128]{0:T(128)S(1)}, s32[128]{0:T(128)S(1)}, u32[]{:S(2)}, u32[]{:S(2)}) collective-permute-start(s32[128]{0:T(128)S(1)} %get-tuple-element.242), channel_id=1, source_target_pairs={{0,4},{1,5},{2,6},{3,7},{4,0},{5,1},{6,2},{7,3},{8,12},{9,13},{10,... | collective-permute-start | bytes 1544 | tf_op jit(solution)/shard_map/ppermute | solution.py:163
  11.5 37.0 %collective-permute-start.5 = (bf16[1,1248]{1,0:T(2,128)(2,1)S(1)}, bf16[1,1248]{1,0:T(2,128)(2,1)S(1)}, u32[]{:S(2)}, u32[]{:S(2)}) collective-permute-start(bf16[1,1248]{1,0:T(2,128)(2,1)S(1)} %broadcast_in_dim.21), channel_id=1, source_target_pairs={{0,1},{1,0},{2,3},{3,2},{4,5},{5,4},{6,7},{7,6},{8,9},{9,8},{10,11... | collective-permute-start | bytes 7496 | tf_op jit(solution)/shard_map/ppermute | solution.py:163
  14.7 58.3 %collective-permute-start.8 = (bf16[96,768]{1,0:T(8,128)(2,1)}, bf16[96,768]{1,0:T(8,128)(2,1)}, u32[]{:S(2)}, u32[]{:S(2)}) collective-permute-start(bf16[96,768]{1,0:T(8,128)(2,1)} %pad_maximum_fusion.29), channel_id=1, source_target_pairs={{0,1},{1,0},{2,3},{3,2},{4,5},{5,4},{6,7},{7,6},{8,9},{9,8},{10,11... | collective-permute-start | bytes 442376 | tf_op jit(solution)/shard_map/ppermute | solution.py:163
  44.8 24.4 %collective-permute-start.22 = (bf16[96,768]{1,0:T(8,128)(2,1)}, bf16[96,768]{1,0:T(8,128)(2,1)S(1)}, u32[]{:S(2)}, u32[]{:S(2)}) collective-permute-start(bf16[96,768]{1,0:T(8,128)(2,1)} %get-tuple-element.166), channel_id=1, source_target_pairs={{0,1},{1,0},{2,3},{3,2},{4,5},{5,4},{6,7},{7,6},{8,9},{9,8},{10,11... | collective-permute-start | bytes 442376 | tf_op jit(solution)/shard_map/ppermute | solution.py:163
  45.0 17.4 %collective-permute-start = (bf16[128,768]{1,0:T(8,128)(2,1)S(1)}, bf16[128,768]{1,0:T(8,128)(2,1)S(1)}, u32[]{:S(2)}, u32[]{:S(2)}) collective-permute-start(bf16[128,768]{1,0:T(8,128)(2,1)S(1)} %get-tuple-element.149), channel_id=1, source_target_pairs={{0,2},{1,3},{2,0},{3,1},{4,6},{5,7},{6,4},{7,5},{8,10},{9,11},{10,... | collective-permute-start | bytes 589832 | tf_op jit(solution)/shard_map/ppermute | solution.py:163
  46.9 15.5 %collective-permute-start.2 = (bf16[128,768]{1,0:T(8,128)(2,1)S(1)}, bf16[128,768]{1,0:T(8,128)(2,1)S(1)}, u32[]{:S(2)}, u32[]{:S(2)}) collective-permute-start(bf16[128,768]{1,0:T(8,128)(2,1)S(1)} %get-tuple-element.150), channel_id=1, source_target_pairs={{0,6},{1,7},{2,4},{3,5},{4,2},{5,3},{6,0},{7,1},{8,14},{9,15},{10,... | collective-permute-start | bytes 589832 | tf_op jit(solution)/shard_map/ppermute | solution.py:163
  62.3 9.2 %collective-permute-start.26 = (bf16[96,768]{1,0:T(8,128)(2,1)}, bf16[96,768]{1,0:T(8,128)(2,1)S(1)}, u32[]{:S(2)}, u32[]{:S(2)}) collective-permute-start(bf16[96,768]{1,0:T(8,128)(2,1)} %get-tuple-element.164), channel_id=1, source_target_pairs={{0,1},{1,0},{2,3},{3,2},{4,5},{5,4},{6,7},{7,6},{8,9},{9,8},{10,11... | collective-permute-start | bytes 442376 | tf_op jit(solution)/shard_map/ppermute | solution.py:163
  62.4 23.9 %collective-permute-start.18 = (bf16[128,768]{1,0:T(8,128)(2,1)}, bf16[128,768]{1,0:T(8,128)(2,1)}, u32[]{:S(2)}, u32[]{:S(2)}) collective-permute-start(bf16[128,768]{1,0:T(8,128)(2,1)} %get-tuple-element.143), channel_id=1, source_target_pairs={{0,4},{1,5},{2,6},{3,7},{4,0},{5,1},{6,2},{7,3},{8,12},{9,13},{10,... | collective-permute-start | bytes 589832 | tf_op jit(solution)/shard_map/ppermute | solution.py:163
  67.4 16.3 %collective-permute-start.3 = (bf16[4,128,768]{2,1,0:T(8,128)(2,1)S(1)}, bf16[4,128,768]{2,1,0:T(8,128)(2,1)S(1)}, u32[]{:S(2)}, u32[]{:S(2)}) collective-permute-start(bf16[4,128,768]{2,1,0:T(8,128)(2,1)S(1)} %get-tuple-element.147), channel_id=1, source_target_pairs={{0,8},{8,0},{16,24},{24,16},{1,9},{9,1},{17,25},{25,17},{2,10},{10... | collective-permute-start | bytes 2359304 | tf_op jit(solution)/shard_map/ppermute | solution.py:173
  69.2 18.6 %collective-permute-start.17 = (bf16[128,768]{1,0:T(8,128)(2,1)}, bf16[128,768]{1,0:T(8,128)(2,1)S(1)}, u32[]{:S(2)}, u32[]{:S(2)}) collective-permute-start(bf16[128,768]{1,0:T(8,128)(2,1)} %get-tuple-element.144), channel_id=1, source_target_pairs={{0,2},{1,3},{2,0},{3,1},{4,6},{5,7},{6,4},{7,5},{8,10},{9,11},{10,... | collective-permute-start | bytes 589832 | tf_op jit(solution)/shard_map/ppermute | solution.py:163
  71.6 17.4 %collective-permute-start.23 = (bf16[192,768]{1,0:T(8,128)(2,1)S(1)}, bf16[192,768]{1,0:T(8,128)(2,1)}, u32[]{:S(2)}, u32[]{:S(2)}) collective-permute-start(bf16[192,768]{1,0:T(8,128)(2,1)S(1)} %get-tuple-element.189), channel_id=1, source_target_pairs={{0,2},{1,5},{2,0},{3,7},{4,6},{5,1},{6,4},{7,3},{8,10},{9,13},{10,... | collective-permute-start | bytes 884744 | tf_op jit(solution)/shard_map/ppermute | solution.py:170
  73.0 22.1 %collective-permute-start.24 = (bf16[192,768]{1,0:T(8,128)(2,1)S(1)}, bf16[192,768]{1,0:T(8,128)(2,1)}, u32[]{:S(2)}, u32[]{:S(2)}) collective-permute-start(bf16[192,768]{1,0:T(8,128)(2,1)S(1)} %get-tuple-element.189), channel_id=1, source_target_pairs={{0,4},{1,3},{2,6},{3,1},{4,0},{5,7},{6,2},{7,5},{8,12},{9,11},{10,... | collective-permute-start | bytes 884744 | tf_op jit(solution)/shard_map/ppermute | solution.py:170
  83.7 13.1 %collective-permute-start.27 = (bf16[192,768]{1,0:T(8,128)(2,1)}, bf16[192,768]{1,0:T(8,128)(2,1)}, u32[]{:S(2)}, u32[]{:S(2)}) collective-permute-start(bf16[192,768]{1,0:T(8,128)(2,1)} %get-tuple-element.185), channel_id=1, source_target_pairs={{0,2},{1,5},{2,0},{3,7},{4,6},{5,1},{6,4},{7,3},{8,10},{9,13},{10,... | collective-permute-start | bytes 884744 | tf_op jit(solution)/shard_map/ppermute | solution.py:170
  87.8 31.7 %collective-permute-start.4 = (bf16[2,4,128,768]{3,2,1,0:T(8,128)(2,1)}, bf16[2,4,128,768]{3,2,1,0:T(8,128)(2,1)S(1)}, u32[]{:S(2)}, u32[]{:S(2)}) collective-permute-start(bf16[2,4,128,768]{3,2,1,0:T(8,128)(2,1)} %get-tuple-element.100), channel_id=1, source_target_pairs={{0,1},{1,0},{2,3},{3,2},{4,5},{5,4},{6,7},{7,6},{8,9},{9,8},{10,11... | collective-permute-start | bytes 4718600 | tf_op jit(solution)/shard_map/ppermute | solution.py:163
  89.0 11.3 %collective-permute-start.25 = (bf16[192,768]{1,0:T(8,128)(2,1)}, bf16[192,768]{1,0:T(8,128)(2,1)}, u32[]{:S(2)}, u32[]{:S(2)}) collective-permute-start(bf16[192,768]{1,0:T(8,128)(2,1)} %collective-permute-done.23), channel_id=1, source_target_pairs={{0,4},{1,3},{2,6},{3,1},{4,0},{5,7},{6,2},{7,5},{8,12},{9,11},{10,... | collective-permute-start | bytes 884744 | tf_op jit(solution)/shard_map/ppermute | solution.py:170
  94.4 8.8 %collective-permute-start.28 = (bf16[192,768]{1,0:T(8,128)(2,1)}, bf16[192,768]{1,0:T(8,128)(2,1)}, u32[]{:S(2)}, u32[]{:S(2)}) collective-permute-start(bf16[192,768]{1,0:T(8,128)(2,1)} %get-tuple-element.185), channel_id=1, source_target_pairs={{0,4},{1,3},{2,6},{3,1},{4,0},{5,7},{6,2},{7,5},{8,12},{9,11},{10,... | collective-permute-start | bytes 884744 | tf_op jit(solution)/shard_map/ppermute | solution.py:170
  95.1 10.3 %collective-permute-start.9 = (bf16[192,768]{1,0:T(8,128)(2,1)}, bf16[192,768]{1,0:T(8,128)(2,1)}, u32[]{:S(2)}, u32[]{:S(2)}) collective-permute-start(bf16[192,768]{1,0:T(8,128)(2,1)} %get-tuple-element.181), channel_id=1, source_target_pairs={{0,2},{1,5},{2,0},{3,7},{4,6},{5,1},{6,4},{7,3},{8,10},{9,13},{10,... | collective-permute-start | bytes 884744 | tf_op jit(solution)/shard_map/ppermute | solution.py:170
  96.8 9.9 %collective-permute-start.29 = (bf16[192,768]{1,0:T(8,128)(2,1)}, bf16[192,768]{1,0:T(8,128)(2,1)}, u32[]{:S(2)}, u32[]{:S(2)}) collective-permute-start(bf16[192,768]{1,0:T(8,128)(2,1)} %collective-permute-done.27), channel_id=1, source_target_pairs={{0,4},{1,3},{2,6},{3,1},{4,0},{5,7},{6,2},{7,5},{8,12},{9,11},{10,... | collective-permute-start | bytes 884744 | tf_op jit(solution)/shard_map/ppermute | solution.py:170
  100.3 9.8 %collective-permute-start.10 = (bf16[192,768]{1,0:T(8,128)(2,1)}, bf16[192,768]{1,0:T(8,128)(2,1)S(1)}, u32[]{:S(2)}, u32[]{:S(2)}) collective-permute-start(bf16[192,768]{1,0:T(8,128)(2,1)} %get-tuple-element.181), channel_id=1, source_target_pairs={{0,4},{1,3},{2,6},{3,1},{4,0},{5,7},{6,2},{7,5},{8,12},{9,11},{10,... | collective-permute-start | bytes 884744 | tf_op jit(solution)/shard_map/ppermute | solution.py:170
  103.2 16.1 %collective-permute-start.20 = (bf16[4,128,768]{2,1,0:T(8,128)(2,1)S(1)}, bf16[4,128,768]{2,1,0:T(8,128)(2,1)S(1)}, u32[]{:S(2)}, u32[]{:S(2)}) collective-permute-start(bf16[4,128,768]{2,1,0:T(8,128)(2,1)S(1)} %get-tuple-element.141), channel_id=1, source_target_pairs={{0,8},{8,0},{16,24},{24,16},{1,9},{9,1},{17,25},{25,17},{2,10},{10... | collective-permute-start | bytes 2359304 | tf_op jit(solution)/shard_map/ppermute | solution.py:173
  119.4 14.5 %collective-permute-start.21 = (bf16[2,4,128,768]{3,2,1,0:T(8,128)(2,1)S(1)}, bf16[2,4,128,768]{3,2,1,0:T(8,128)(2,1)S(1)}, u32[]{:S(2)}, u32[]{:S(2)}) collective-permute-start(bf16[2,4,128,768]{3,2,1,0:T(8,128)(2,1)S(1)} %get-tuple-element.98), channel_id=1, source_target_pairs={{0,1},{1,0},{2,3},{3,2},{4,5},{5,4},{6,7},{7,6},{8,9},{9,8},{10,11... | collective-permute-start | bytes 4718600 | tf_op jit(solution)/shard_map/ppermute | solution.py:163
  222.4 54.6 %collective-permute-start.40 = (bf16[192,768]{1,0:T(8,128)(2,1)}, bf16[192,768]{1,0:T(8,128)(2,1)}, u32[]{:S(2)}, u32[]{:S(2)}) collective-permute-start(bf16[192,768]{1,0:T(8,128)(2,1)} %get-tuple-element.101), channel_id=1, source_target_pairs={{0,4},{1,3},{2,6},{3,1},{4,0},{5,7},{6,2},{7,5},{8,12},{9,11},{10,... | collective-permute-start | bytes 884744 | tf_op jit(solution)/shard_map/ppermute | solution.py:170
  223.1 42.0 %collective-permute-start.41 = (bf16[192,768]{1,0:T(8,128)(2,1)}, bf16[192,768]{1,0:T(8,128)(2,1)}, u32[]{:S(2)}, u32[]{:S(2)}) collective-permute-start(bf16[192,768]{1,0:T(8,128)(2,1)} %get-tuple-element.102), channel_id=1, source_target_pairs={{0,4},{1,3},{2,6},{3,1},{4,0},{5,7},{6,2},{7,5},{8,12},{9,11},{10,... | collective-permute-start | bytes 884744 | tf_op jit(solution)/shard_map/ppermute | solution.py:170
  254.4 20.6 %collective-permute-start.46 = (bf16[192,768]{1,0:T(8,128)(2,1)S(1)}, bf16[192,768]{1,0:T(8,128)(2,1)S(1)}, u32[]{:S(2)}, u32[]{:S(2)}) collective-permute-start(bf16[192,768]{1,0:T(8,128)(2,1)S(1)} %get-tuple-element.105), channel_id=1, source_target_pairs={{0,4},{1,3},{2,6},{3,1},{4,0},{5,7},{6,2},{7,5},{8,12},{9,11},{10,... | collective-permute-start | bytes 884744 | tf_op jit(solution)/shard_map/ppermute | solution.py:170
  255.2 9.1 %collective-permute-start.47 = (bf16[192,768]{1,0:T(8,128)(2,1)S(1)}, bf16[192,768]{1,0:T(8,128)(2,1)S(1)}, u32[]{:S(2)}, u32[]{:S(2)}) collective-permute-start(bf16[192,768]{1,0:T(8,128)(2,1)S(1)} %get-tuple-element.106), channel_id=1, source_target_pairs={{0,4},{1,3},{2,6},{3,1},{4,0},{5,7},{6,2},{7,5},{8,12},{9,11},{10,... | collective-permute-start | bytes 884744 | tf_op jit(solution)/shard_map/ppermute | solution.py:170
  256.5 28.4 %collective-permute-start.52 = (bf16[192,768]{1,0:T(8,128)(2,1)S(1)}, bf16[192,768]{1,0:T(8,128)(2,1)S(1)}, u32[]{:S(2)}, u32[]{:S(2)}) collective-permute-start(bf16[192,768]{1,0:T(8,128)(2,1)S(1)} %get-tuple-element.103), channel_id=1, source_target_pairs={{0,4},{1,3},{2,6},{3,1},{4,0},{5,7},{6,2},{7,5},{8,12},{9,11},{10,... | collective-permute-start | bytes 884744 | tf_op jit(solution)/shard_map/ppermute | solution.py:170
  264.3 10.2 %collective-permute-start.53 = (bf16[192,768]{1,0:T(8,128)(2,1)S(1)}, bf16[192,768]{1,0:T(8,128)(2,1)S(1)}, u32[]{:S(2)}, u32[]{:S(2)}) collective-permute-start(bf16[192,768]{1,0:T(8,128)(2,1)S(1)} %get-tuple-element.104), channel_id=1, source_target_pairs={{0,4},{1,3},{2,6},{3,1},{4,0},{5,7},{6,2},{7,5},{8,12},{9,11},{10,... | collective-permute-start | bytes 884744 | tf_op jit(solution)/shard_map/ppermute | solution.py:170
  265.2 9.9 %collective-permute-start.48 = (bf16[192,768]{1,0:T(8,128)(2,1)S(1)}, bf16[192,768]{1,0:T(8,128)(2,1)S(1)}, u32[]{:S(2)}, u32[]{:S(2)}) collective-permute-start(bf16[192,768]{1,0:T(8,128)(2,1)S(1)} %fusion.41), channel_id=1, source_target_pairs={{0,2},{1,5},{2,0},{3,7},{4,6},{5,1},{6,4},{7,3},{8,10},{9,13},{10,... | collective-permute-start | bytes 884744 | tf_op jit(solution)/shard_map/ppermute | solution.py:170
  275.0 62.9 %collective-permute-start.35 = (bf16[2,4,128,768]{3,2,1,0:T(8,128)(2,1)}, bf16[2,4,128,768]{3,2,1,0:T(8,128)(2,1)}, u32[]{:S(2)}, u32[]{:S(2)}) collective-permute-start(bf16[2,4,128,768]{3,2,1,0:T(8,128)(2,1)} %slice_bitcast_fusion), channel_id=1, source_target_pairs={{0,1},{1,0},{2,3},{3,2},{4,5},{5,4},{6,7},{7,6},{8,9},{9,8},{10,11... | collective-permute-start | bytes 4718600 | tf_op jit(solution)/shard_map/ppermute | solution.py:163
  275.1 10.3 %collective-permute-start.54 = (bf16[192,768]{1,0:T(8,128)(2,1)S(1)}, bf16[192,768]{1,0:T(8,128)(2,1)S(1)}, u32[]{:S(2)}, u32[]{:S(2)}) collective-permute-start(bf16[192,768]{1,0:T(8,128)(2,1)S(1)} %fusion.39), channel_id=1, source_target_pairs={{0,2},{1,5},{2,0},{3,7},{4,6},{5,1},{6,4},{7,3},{8,10},{9,13},{10,... | collective-permute-start | bytes 884744 | tf_op jit(solution)/shard_map/ppermute | solution.py:170
  277.0 63.6 %collective-permute-start.30 = (bf16[2,4,128,768]{3,2,1,0:T(8,128)(2,1)}, bf16[2,4,128,768]{3,2,1,0:T(8,128)(2,1)}, u32[]{:S(2)}, u32[]{:S(2)}) collective-permute-start(bf16[2,4,128,768]{3,2,1,0:T(8,128)(2,1)} %slice_bitcast_fusion.2), channel_id=1, source_target_pairs={{0,1},{1,0},{2,3},{3,2},{4,5},{5,4},{6,7},{7,6},{8,9},{9,8},{10,11... | collective-permute-start | bytes 4718600 | tf_op jit(solution)/shard_map/ppermute | solution.py:163
  281.3 26.3 %collective-permute-start.49 = (bf16[192,768]{1,0:T(8,128)(2,1)S(1)}, bf16[192,768]{1,0:T(8,128)(2,1)S(1)}, u32[]{:S(2)}, u32[]{:S(2)}) collective-permute-start(bf16[192,768]{1,0:T(8,128)(2,1)S(1)} %add_convert_fusion.7), channel_id=1, source_target_pairs={{0,16},{8,24},{16,0},{24,8},{1,17},{9,25},{17,1},{25,9},{2,18},{10... | collective-permute-start | bytes 884744 | tf_op jit(solution)/shard_map/ppermute | solution.py:173
  285.0 34.2 %collective-permute-start.43 = (bf16[192,768]{1,0:T(8,128)(2,1)S(1)}, bf16[192,768]{1,0:T(8,128)(2,1)S(1)}, u32[]{:S(2)}, u32[]{:S(2)}) collective-permute-start(bf16[192,768]{1,0:T(8,128)(2,1)S(1)} %add_convert_fusion.9), channel_id=1, source_target_pairs={{0,16},{8,24},{16,0},{24,8},{1,17},{9,25},{17,1},{25,9},{2,18},{10... | collective-permute-start | bytes 884744 | tf_op jit(solution)/shard_map/ppermute | solution.py:173
  285.5 33.4 %collective-permute-start.55 = (bf16[192,768]{1,0:T(8,128)(2,1)S(1)}, bf16[192,768]{1,0:T(8,128)(2,1)S(1)}, u32[]{:S(2)}, u32[]{:S(2)}) collective-permute-start(bf16[192,768]{1,0:T(8,128)(2,1)S(1)} %add_convert_fusion.5), channel_id=1, source_target_pairs={{0,16},{8,24},{16,0},{24,8},{1,17},{9,25},{17,1},{25,9},{2,18},{10... | collective-permute-start | bytes 884744 | tf_op jit(solution)/shard_map/ppermute | solution.py:173
  307.7 12.7 %collective-permute-start.50 = (bf16[96,768]{1,0:T(8,128)(2,1)S(1)}, bf16[96,768]{1,0:T(8,128)(2,1)S(1)}, u32[]{:S(2)}, u32[]{:S(2)}) collective-permute-start(bf16[96,768]{1,0:T(8,128)(2,1)S(1)} %get-tuple-element.177), channel_id=1, source_target_pairs={{0,1},{1,0},{2,3},{3,2},{4,5},{5,4},{6,7},{7,6},{8,9},{9,8},{10,11... | collective-permute-start | bytes 442376 | tf_op jit(solution)/shard_map/ppermute | solution.py:163
  321.2 10.2 %collective-permute-start.51 = (bf16[2,96,768]{2,1,0:T(8,128)(2,1)}, bf16[2,96,768]{2,1,0:T(8,128)(2,1)}, u32[]{:S(2)}, u32[]{:S(2)}) collective-permute-start(bf16[2,96,768]{2,1,0:T(8,128)(2,1)} %pad_maximum_fusion.23), channel_id=1, source_target_pairs={{0,8},{8,0},{16,24},{24,16},{1,9},{9,1},{17,25},{25,17},{2,10},{10... | collective-permute-start | bytes 884744 | tf_op jit(solution)/shard_map/ppermute | solution.py:173
  322.6 14.2 %collective-permute-start.57 = (bf16[2,96,768]{2,1,0:T(8,128)(2,1)}, bf16[2,96,768]{2,1,0:T(8,128)(2,1)}, u32[]{:S(2)}, u32[]{:S(2)}) collective-permute-start(bf16[2,96,768]{2,1,0:T(8,128)(2,1)} %pad_maximum_fusion.24), channel_id=1, source_target_pairs={{0,8},{8,0},{16,24},{24,16},{1,9},{9,1},{17,25},{25,17},{2,10},{10... | collective-permute-start | bytes 884744 | tf_op jit(solution)/shard_map/ppermute | solution.py:173
  339.8 20.5 %collective-permute-start.36 = (bf16[4,128,768]{2,1,0:T(8,128)(2,1)S(1)}, bf16[4,128,768]{2,1,0:T(8,128)(2,1)S(1)}, u32[]{:S(2)}, u32[]{:S(2)}) collective-permute-start(bf16[4,128,768]{2,1,0:T(8,128)(2,1)S(1)} %slice_bitcast_fusion.4), channel_id=1, source_target_pairs={{0,8},{8,0},{16,24},{24,16},{1,9},{9,1},{17,25},{25,17},{2,10},{10... | collective-permute-start | bytes 2359304 | tf_op jit(solution)/shard_map/ppermute | solution.py:173
  342.4 33.0 %collective-permute-start.31 = (bf16[4,128,768]{2,1,0:T(8,128)(2,1)S(1)}, bf16[4,128,768]{2,1,0:T(8,128)(2,1)S(1)}, u32[]{:S(2)}, u32[]{:S(2)}) collective-permute-start(bf16[4,128,768]{2,1,0:T(8,128)(2,1)S(1)} %slice_bitcast_fusion.6), channel_id=1, source_target_pairs={{0,8},{8,0},{16,24},{24,16},{1,9},{9,1},{17,25},{25,17},{2,10},{10... | collective-permute-start | bytes 2359304 | tf_op jit(solution)/shard_map/ppermute | solution.py:173
  360.6 16.9 %collective-permute-start.39 = (bf16[128,768]{1,0:T(8,128)(2,1)S(1)}, bf16[128,768]{1,0:T(8,128)(2,1)S(1)}, u32[]{:S(2)}, u32[]{:S(2)}) collective-permute-start(bf16[128,768]{1,0:T(8,128)(2,1)S(1)} %get-tuple-element.129), channel_id=1, source_target_pairs={{0,6},{1,7},{2,4},{3,5},{4,2},{5,3},{6,0},{7,1},{8,14},{9,15},{10,... | collective-permute-start | bytes 589832 | tf_op jit(solution)/shard_map/ppermute | solution.py:163
  362.1 18.2 %collective-permute-start.38 = (bf16[128,768]{1,0:T(8,128)(2,1)S(1)}, bf16[128,768]{1,0:T(8,128)(2,1)S(1)}, u32[]{:S(2)}, u32[]{:S(2)}) collective-permute-start(bf16[128,768]{1,0:T(8,128)(2,1)S(1)} %get-tuple-element.130), channel_id=1, source_target_pairs={{0,4},{1,5},{2,6},{3,7},{4,0},{5,1},{6,2},{7,3},{8,12},{9,13},{10,... | collective-permute-start | bytes 589832 | tf_op jit(solution)/shard_map/ppermute | solution.py:163
  362.5 18.4 %collective-permute-start.37 = (bf16[128,768]{1,0:T(8,128)(2,1)S(1)}, bf16[128,768]{1,0:T(8,128)(2,1)S(1)}, u32[]{:S(2)}, u32[]{:S(2)}) collective-permute-start(bf16[128,768]{1,0:T(8,128)(2,1)S(1)} %get-tuple-element.131), channel_id=1, source_target_pairs={{0,2},{1,3},{2,0},{3,1},{4,6},{5,7},{6,4},{7,5},{8,10},{9,11},{10,... | collective-permute-start | bytes 589832 | tf_op jit(solution)/shard_map/ppermute | solution.py:163
  375.6 8.3 %collective-permute-start.34 = (bf16[128,768]{1,0:T(8,128)(2,1)S(1)}, bf16[128,768]{1,0:T(8,128)(2,1)S(1)}, u32[]{:S(2)}, u32[]{:S(2)}) collective-permute-start(bf16[128,768]{1,0:T(8,128)(2,1)S(1)} %get-tuple-element.137), channel_id=1, source_target_pairs={{0,6},{1,7},{2,4},{3,5},{4,2},{5,3},{6,0},{7,1},{8,14},{9,15},{10,... | collective-permute-start | bytes 589832 | tf_op jit(solution)/shard_map/ppermute | solution.py:163
  377.1 8.8 %collective-permute-start.33 = (bf16[128,768]{1,0:T(8,128)(2,1)S(1)}, bf16[128,768]{1,0:T(8,128)(2,1)S(1)}, u32[]{:S(2)}, u32[]{:S(2)}) collective-permute-start(bf16[128,768]{1,0:T(8,128)(2,1)S(1)} %get-tuple-element.138), channel_id=1, source_target_pairs={{0,4},{1,5},{2,6},{3,7},{4,0},{5,1},{6,2},{7,3},{8,12},{9,13},{10,... | collective-permute-start | bytes 589832 | tf_op jit(solution)/shard_map/ppermute | solution.py:163
  377.5 8.3 %collective-permute-start.32 = (bf16[128,768]{1,0:T(8,128)(2,1)S(1)}, bf16[128,768]{1,0:T(8,128)(2,1)S(1)}, u32[]{:S(2)}, u32[]{:S(2)}) collective-permute-start(bf16[128,768]{1,0:T(8,128)(2,1)S(1)} %get-tuple-element.139), channel_id=1, source_target_pairs={{0,2},{1,3},{2,0},{3,1},{4,6},{5,7},{6,4},{7,5},{8,10},{9,11},{10,... | collective-permute-start | bytes 589832 | tf_op jit(solution)/shard_map/ppermute | solution.py:163
  380.3 10.3 %collective-permute-start.45 = (bf16[2,96,768]{2,1,0:T(8,128)(2,1)}, bf16[2,96,768]{2,1,0:T(8,128)(2,1)S(1)}, u32[]{:S(2)}, u32[]{:S(2)}) collective-permute-start(bf16[2,96,768]{2,1,0:T(8,128)(2,1)} %pad_maximum_fusion.22), channel_id=1, source_target_pairs={{0,8},{8,0},{16,24},{24,16},{1,9},{9,1},{17,25},{25,17},{2,10},{10... | collective-permute-start | bytes 884744 | tf_op jit(solution)/shard_map/ppermute | solution.py:173
  (63 other events, 346.8 us)

commit v2 on v0

v2 whole, which is shorter than its diff:
```python
import functools

import jax
import jax.numpy as jnp
from jax import lax
from jax.experimental import pallas as pl
from jax.experimental.pallas import tpu as pltpu
from jax.sharding import PartitionSpec as P

H = 12
HD = 64
ROT = 16
TILE = 256
VEC = 16
HEADS = 3

COST = {
    "split_input": 1.0,
    "split_cotangent": 1.0,
    "split_weights": 1.0,
    "tables_second": 0.1,
    "middle_1": 0.1,
    "back_1": 0.1,
    "middle_0": 10.0,
    "second_grads": 0.1,
    "tables_first": 0.1,
    "front": 0.1,
    "attention_0": 10.0,
    "first_grads_0": 0.1,
    "attention_1": 10.0,
    "back_0": 10.0,
    "first_grads_1": 0.1,
    "finish_tokens": 1.0,
    "second_end": 1.0,
    "first_end": 1.0,
}
FLOPS = 1.15e9
BYTES = 3.6e6

EPS = 1e-05
NEG = -1e30

F32 = jnp.float32
BF16 = jnp.bfloat16
I32 = jnp.int32

NN = ((1,), (0,))
NT = ((1,), (1,))
TN = ((0,), (0,))


def dot(a, b, dims):
    return lax.dot_general(a, b, (dims, ((), ())), preferred_element_type=F32)


def at(start, size, multiple):
    return pl.ds(pl.multiple_of(start, multiple), size)


class Place:
    def __init__(self, seqs, shards, reps):
        self.seqs, self.shards, self.reps = seqs, shards, reps
        self.low_count = shards // seqs
        self.pair = 2 if reps % 2 == 0 and H % (2 * self.low_count) == 0 else 1
        self.parts = self.pair * self.low_count
        self.line = Line()
        self.groups = H // self.low_count // HEADS
        self.masks = []
        while 2 ** len(self.masks) < seqs:
            self.masks.append(2 ** len(self.masks))
        self.phases = len(self.masks)

    def chip(self):
        return lax.axis_index("fsdp") // self.low_count

    def low(self):
        return lax.axis_index("fsdp") % self.low_count

    def part(self):
        return (lax.axis_index("rep") % self.pair) * self.low_count + self.low()

    def owner(self, slot):
        even = sum(self.masks[p] for p in range(self.phases) if slot >> p & 1)
        odd = sum(self.masks[self.phases - 1 - p] for p in range(self.phases) if slot >> p & 1)
        if even == odd:
            return self.chip() ^ even
        return self.chip() ^ jnp.where(lax.axis_index("fsdp") % 2 == 0, even, odd)

    def slot(self, block):
        j = (block // self.low_count) ^ self.chip()
        other = sum((j >> p & 1) << (self.phases - 1 - p) for p in range(self.phases))
        even = lax.axis_index("fsdp") % 2 == 0 if self.low_count == 1 else block % self.low_count % 2 == 0
        return jnp.where(even, j, other)

    def swap_low(self, v, mask):
        return lax.ppermute(v, "fsdp", [(i, i ^ mask) for i in range(self.shards)])

    def swap_slot(self, v, slot):
        def to(i):
            order = self.masks if i % 2 == 0 else self.masks[::-1]
            return i ^ (sum(m for p, m in enumerate(order) if slot >> p & 1) * self.low_count)

        return lax.ppermute(v, "fsdp", [(i, to(i)) for i in range(self.shards)])

    def swap_phase(self, v, phase):
        def to(i):
            mask = self.masks[phase] if i % 2 == 0 else self.masks[self.phases - 1 - phase]
            return i ^ (mask * self.low_count)

        return lax.ppermute(v, "fsdp", [(i, to(i)) for i in range(self.shards)])

    def swap_rep(self, v, mask):
        return lax.ppermute(v, "rep", [(i, i ^ mask) for i in range(self.reps)])


def after(v, *others):
    return lax.optimization_barrier((v, *others))[0]


def whole(shape):
    return pl.BlockSpec(shape, lambda *_: (0,) * len(shape))


class Line:
    def __init__(self):
        self.ahead = []

    def take(self, *arrays):
        found = lax.optimization_barrier((*arrays, *self.ahead))[: len(arrays)]
        self.ahead = [min(found, key=lambda v: v.size)]
        return found

    def hold(self, *arrays):
        self.ahead.extend(arrays)

    def call(self, kernel, name, grid, in_specs, out_specs, out_shape, scratch, args, vmem=40):
        args = list(args)
        if self.ahead:
            args[0] = after(args[0], *self.ahead)
        outs = pl.pallas_call(
            kernel,
            grid=grid,
            in_specs=in_specs,
            out_specs=out_specs,
            out_shape=out_shape,
            scratch_shapes=scratch,
            compiler_params=pltpu.CompilerParams(vmem_limit_bytes=vmem * 2**20),
            cost_estimate=pl.CostEstimate(
                flops=int(COST[name] * FLOPS), bytes_accessed=int(COST[name] * BYTES),
                transcendentals=0,
            ),
            name=name,
        )(*args)
        self.ahead = [min(jax.tree.leaves(outs), key=lambda v: v.size)]
        return outs


def split_kernel(place, source, *outs):
    for j, out in enumerate(outs):
        out[...] = source[place.owner(j)]


def split_tokens(place, v, name):
    seqs, span, width = v.shape
    return place.line.call(
        functools.partial(split_kernel, place),
        name,
        (1,),
        [whole(v.shape)],
        [whole((span, width))] * seqs,
        [jax.ShapeDtypeStruct((span, width), v.dtype)] * seqs,
        [],
        (v,),
        vmem=58,
    )


def weights_kernel(place, w_qkv, w_out, w_up, w_down, *rest):
    vectors, pos, outs = rest[:8], rest[8], rest[9:]
    rows = w_qkv.shape[0]
    parts, low_count = place.parts, place.low_count
    width = w_out.shape[1]
    step = HEADS * HD
    hidden = w_up.shape[1] // parts
    firsts, seconds = outs[:low_count], outs[low_count:]
    for k in range(low_count):

        @pl.when(place.low() == k)
        def _():
            for o in range(low_count):
                for h in range(place.groups):
                    begin = ((k ^ o) * place.groups + h) * step
                    for g in range(3):
                        to = (3 * h + g) * step
                        firsts[o][:, to : to + step] = w_qkv[
                            :, g * width + begin : g * width + begin + step
                        ]
                    to = (3 * place.groups + h) * step
                    firsts[o][:, to : to + step] = w_out[:, begin : begin + step]

    for o in range(low_count):
        lanes = at((place.part() ^ o) * hidden, hidden, 128)
        seconds[o][:rows, :hidden] = w_up[:, lanes]
        seconds[o][:rows, hidden:] = w_down[:, lanes]

    lanes = seconds[0].shape[1]
    lines = []
    for v in vectors:
        lines.append(
            jnp.concatenate([v[...].astype(F32), jnp.zeros((1, lanes - v.shape[1]), F32)], axis=1)
        )
    span = pos.shape[1]
    for values in (
        [(pos[s : s + 1, :] // 64).astype(F32) for s in range(pos.shape[0])],
        [(pos[s : s + 1, :] % 64).astype(F32) for s in range(pos.shape[0])],
    ):
        lines.append(
            jnp.concatenate(values + [jnp.zeros((1, lanes - span * pos.shape[0]), F32)], axis=1)
        )
    lines.append(jnp.zeros((VEC - len(lines), lanes), F32))
    block = jnp.concatenate(lines, axis=0).astype(BF16)
    for o in range(low_count):
        seconds[o][rows:, :] = block


def split_weights(place, w_qkv, w_out, w_up, w_down, vectors, pos):
    rows = w_qkv.shape[0]
    args = [w_qkv, w_out, w_up, w_down] + [v.reshape(1, -1) for v in vectors] + [pos]
    first = (rows, (w_qkv.shape[1] + w_out.shape[1]) // place.low_count)
    second = (rows + VEC, (w_up.shape[1] + w_down.shape[1]) // place.parts)
    shapes = [first] * place.low_count + [second] * place.low_count
    outs = place.line.call(
        functools.partial(weights_kernel, place),
        "split_weights",
        (1,),
        [whole(v.shape) for v in args],
        [whole(s) for s in shapes],
        [jax.ShapeDtypeStruct(s, BF16) for s in shapes],
        [],
        args,
        vmem=58,
    )
    return outs[: place.low_count], outs[place.low_count :]


def second_tables_kernel(place, rows, *rest):
    slots = rest[: place.seqs]
    w_out, vec_out, bias, lines_kept = rest[place.seqs :]
    seqs, low_count, parts = place.seqs, place.low_count, place.parts
    block = rows + VEC
    width = w_out.shape[0]
    step = HEADS * HD
    low = place.low()
    for s in range(seqs):
        owner = place.owner(s)
        for o in range(low_count):
            found = slots[s][o * block : (o + 1) * block, :]
            l = low ^ o
            w_out[at((owner * low_count + l) * rows, rows, 16), :] = found[:rows]
            lines_kept[owner * low_count + l] = found[rows:].astype(F32)

    def line(row, size):
        return jnp.concatenate(
            [lines_kept[n, row : row + 1, :size] for n in range(place.shards)], axis=1
        )

    for row in range(4):
        vec_out[row : row + 1, :] = line(row, rows)
    vec_out[4:5, :] = line(5, rows) + line(7, rows)
    all_up = line(6, 4 * rows)
    all_qkv = line(4, 3 * rows)
    for k in range(parts):

        @pl.when(place.part() == k)
        def _():
            vec_out[5:6, :] = all_up[:, k * width : (k + 1) * width]

    for k in range(low_count):

        @pl.when(low == k)
        def _():
            for h in range(place.groups):
                for g in range(3):
                    begin = g * width + (k * place.groups + h) * step
                    bias[h : h + 1, g * step : (g + 1) * step] = all_qkv[:, begin : begin + step]

    vec_out[6:, :] = jnp.zeros((2, width), F32)


def second_tables(place, slots, rows, width):
    shapes = [
        jax.ShapeDtypeStruct((width, slots[0].shape[1]), BF16),
        jax.ShapeDtypeStruct((8, width), F32),
        jax.ShapeDtypeStruct((8, 3 * HEADS * HD), F32),
        jax.ShapeDtypeStruct((place.shards, VEC, slots[0].shape[1]), F32),
    ]
    return place.line.call(
        functools.partial(second_tables_kernel, place, rows),
        "tables_second",
        (1,),
        [whole(v.shape) for v in slots],
        [whole(v.shape) for v in shapes],
        shapes,
        [],
        slots,
        vmem=16,
    )


def first_tables_kernel(place, rows, span, inverse, lines_kept, *rest):
    slots = rest[: place.seqs]
    w_out, first_out, cos_out, sin_out = rest[place.seqs :]
    low_count = place.low_count
    low, chip = place.low(), place.chip()
    for s in range(place.seqs):
        owner = place.owner(s)
        for o in range(low_count):
            w_out[at((owner * low_count + (low ^ o)) * rows, rows, 16), :] = slots[s][
                o * rows : (o + 1) * rows, :
            ]
    still = jnp.zeros((HD - ROT, span), F32)
    for f in range(place.shards):
        lanes = at(chip * span, span, 128)
        value = lines_kept[f, 8:9, lanes] * 64.0 + lines_kept[f, 9:10, lanes]
        index = f * span + lax.broadcasted_iota(I32, (1, span), 1)
        first_out[:, f * span : (f + 1) * span] = index - value.astype(I32)
        phase = inverse[...] * value
        cosine, sine = jnp.cos(phase), jnp.sin(phase)
        crel, j = (f % low_count) ^ low, place.slot(f)
        to = at(j * span, span, 128)
        cos_out[crel, to, :] = jnp.concatenate([cosine, cosine, still + 1.0] * 2, axis=0).T
        sin_out[crel, to, :] = jnp.concatenate([-sine, sine, still] * 2, axis=0).T


def first_tables(place, slots, lines_kept, rows, width, span):
    inverse = (10000.0 ** (-jnp.arange(0, ROT, 2, dtype=F32) / ROT)).reshape(-1, 1)
    shapes = [
        jax.ShapeDtypeStruct((width, slots[0].shape[1]), BF16),
        jax.ShapeDtypeStruct((1, place.shards * span), I32),
        jax.ShapeDtypeStruct((place.low_count, place.seqs * span, 128), F32),
        jax.ShapeDtypeStruct((place.low_count, place.seqs * span, 128), F32),
    ]
    args = [inverse, lines_kept] + slots
    return place.line.call(
        functools.partial(first_tables_kernel, place, rows, span),
        "tables_first",
        (1,),
        [whole(v.shape) for v in args],
        [whole(v.shape) for v in shapes],
        shapes,
        [],
        args,
        vmem=16,
    )


def piece_specs(pieces, lines):
    split = pieces[0].shape[0] // lines

    def spec(i, width):
        return pl.BlockSpec(
            (lines, width), lambda g: (jnp.clip(g - i * split, 0, split - 1), 0)
        )

    return [spec(i, v.shape[1]) for i, v in enumerate(pieces)]


def piece_now(refs, steps):
    found = refs[0][...]
    for i in range(1, len(refs)):
        found = jnp.where(pl.program_id(0) >= i * (steps // len(refs)), refs[i][...], found)
    return found


def norm(source):
    source = source.astype(F32)
    centred = source - jnp.mean(source, axis=1, keepdims=True)
    return centred * lax.rsqrt(jnp.mean(centred * centred, axis=1, keepdims=True) + EPS)


def turned(v):
    half = ROT // 2
    columns = v.shape[1]
    lane = lax.broadcasted_iota(I32, v.shape, 1) % HD
    ahead = pltpu.roll(v, columns - half, 1)
    behind = pltpu.roll(v, half, 1)
    return jnp.where(lane < half, ahead, behind)


def front_kernel(place, steps, *refs):
    tokens, refs = refs[: place.low_count], refs[place.low_count :]
    weight, vec, bias, cosine, sine, one_out, *outs = refs
    step = HEADS * HD
    one = (norm(piece_now(tokens, steps)) * vec[0:1, :] + vec[1:2, :]).astype(BF16)
    one_out[0] = one
    copies = 2 * step // 128
    cos_cols = jnp.concatenate([cosine[0]] * copies, axis=1)
    sin_cols = jnp.concatenate([sine[0]] * copies, axis=1)
    for h in range(place.groups):
        q_out, k_out, v_out = outs[3 * h : 3 * h + 3]
        qkv = dot(one, weight[:, 3 * step * h : 3 * step * (h + 1)], NN) + bias[h : h + 1, :]
        both = qkv[:, : 2 * step]
        both = both * cos_cols + turned(both) * sin_cols
        q_out[0] = both[:, :step].astype(BF16)
        k_out[0] = both[:, step:].astype(BF16)
        v_out[0] = qkv[:, 2 * step :].astype(BF16)


def front(place, tokens, weight, vec, bias, cosine, sine):
    groups = len(tokens)
    count, width = tokens[0].shape
    step = HEADS * HD
    split = 2
    lines = count // split
    by_step = lambda cols: pl.BlockSpec((1, lines, cols), lambda g: (g // split, g % split, 0))
    shaped = lambda cols: jax.ShapeDtypeStruct((groups, count, cols), BF16)
    outs = place.line.call(
        functools.partial(front_kernel, place, groups * split),
        "front",
        (groups * split,),
        piece_specs(tokens, lines)
        + [whole(weight.shape), whole(vec.shape), whole(bias.shape)] + [by_step(128)] * 2,
        [by_step(width)] + [by_step(step)] * (3 * place.groups),
        [shaped(width)] + [shaped(step)] * (3 * place.groups),
        [],
        [*tokens, weight, vec, bias, cosine, sine],
        vmem=24,
    )
    return outs[0], [outs[1 + 3 * h : 4 + 3 * h] for h in range(place.groups)]


def middle_kernel(count, steps, *refs):
    tokens, grads, refs = refs[:count], refs[count : 2 * count], refs[2 * count :]
    vec, weight, two_out, normed_out, hidden_out, grad_out, sums = refs

    @pl.when(pl.program_id(0) == 0)
    def _():
        sums[...] = jnp.zeros_like(sums)

    width = weight.shape[0]
    normed = norm(piece_now(tokens, steps))
    normed_out[0] = normed.astype(BF16)
    two = (normed * vec[2:3, :] + vec[3:4, :]).astype(BF16)
    two_out[0] = two
    up = dot(two, weight[:, :width], NN) + vec[5:6, :]
    grad = piece_now(grads, steps)
    grad_hidden = dot(grad, weight[:, width:], NN)
    bell = jnp.exp(-0.5 * up * up)
    below = 1.0 + (0.3275911 * 0.5**0.5) * jnp.abs(up)
    t = pl.reciprocal(below, approx=True)
    t = t * (2.0 - below * t)
    series = t * (
        0.127414796 + t * (-0.142248368 + t * (0.7107068705 + t * (-0.7265760135 + t * 0.5307027145)))
    )
    tail = series * bell
    share = jnp.where(up >= 0.0, 1.0 - tail, tail)
    hidden_out[0] = (up * share).astype(BF16)
    slope = share + up * (bell * 0.3989422804014327)
    grad_up = (grad_hidden * slope).astype(BF16)
    grad_out[0] = grad_up
    sums[0:1, :] += jnp.sum(grad_up.astype(F32), axis=0, keepdims=True)
    sums[1:2, :] += jnp.sum(grad.astype(F32), axis=0, keepdims=True)


def middle(place, z, tokens, grads, vec, weight):
    groups = len(tokens)
    count, width = tokens[0].shape
    split = 2
    lines = count // split
    by_step = pl.BlockSpec((1, lines, width), lambda g: (g // split, g % split, 0))
    return place.line.call(
        functools.partial(middle_kernel, groups, groups * split),
        f"middle_{z}",
        (groups * split,),
        piece_specs(tokens, lines)
        + piece_specs(grads, lines)
        + [whole(vec.shape), whole(weight.shape)],
        [by_step] * 4 + [whole((8, width))],
        [jax.ShapeDtypeStruct((groups, count, width), BF16)] * 4 + [jax.ShapeDtypeStruct((8, width), F32)],
        [],
        [*tokens, *grads, vec, weight],
        vmem=24,
    )


def attention_kernel(
    place, group, span, q_in, k_in, v_in, w_in, first_in, cos_in, sin_in, *refs
):
    cot_in, refs = refs[: place.low_count], refs[place.low_count :]
    o_out, g_out, sums, qs, ks, vs, gs, o_turned, gq_turned, gk_sum, gv_sum = refs
    low_count = place.low_count
    count, columns = q_in.shape[1:]
    heads = columns // HD
    length = low_count * count
    begin = (3 * place.groups + group) * columns
    w_out = w_in[:, begin : begin + columns]

    def slot(f):
        crel = (f % low_count) ^ place.low()
        j = place.slot(f)
        return crel, at(j * span, span, 128)

    for f in range(length // span):
        to = slice(f * span, (f + 1) * span)
        crel, lines = slot(f)
        for source, kept in ((q_in, qs), (k_in, ks), (v_in, vs)):
            found = source[crel, lines, :]
            for h in range(heads):
                kept[h, to, :] = found[:, h * HD : (h + 1) * HD]
        cot = cot_in[0][lines, :]
        for o in range(1, low_count):
            cot = jnp.where(crel == o, cot_in[o][lines, :], cot)
        found = dot(cot, w_out, NN).astype(BF16)
        for h in range(heads):
            gs[h, to, :] = found[:, h * HD : (h + 1) * HD]

    def one_head(h, carry):
        keys = ks[h]
        values = vs[h]
        keys_turned = keys.astype(F32).T.astype(BF16)
        values_turned = values.astype(F32).T.astype(BF16)
        for i in range(length // TILE):
            seen = (i + 1) * TILE
            here = slice(i * TILE, seen)
            query = qs[h, here, :]
            grad = gs[h, here, :]
            first = first_in[:, here]
            raw = dot(keys[:seen], query, NT) * 0.125
            key_index = lax.broadcasted_iota(I32, (seen, TILE), 0)
            query_index = i * TILE + lax.broadcasted_iota(I32, (seen, TILE), 1)
            raw = jnp.where((key_index >= first) & (key_index <= query_index), raw, NEG)
            weights = jnp.exp(raw - jnp.max(raw, axis=0, keepdims=True))
            probs = weights * (1.0 / jnp.sum(weights, axis=0, keepdims=True))
            grad_probs = dot(values[:seen], grad, NT)
            carried = jnp.sum(probs * grad_probs, axis=0, keepdims=True)
            grad_scores = (probs * (grad_probs - carried)).astype(BF16)
            low = probs.astype(BF16)
            o_turned[h, :, here] = dot(values_turned[:, :seen], low, NN)
            gq_turned[h, :, here] = dot(keys_turned[:, :seen], grad_scores, NN)
            gk_part = dot(grad_scores, query, NN)
            gv_part = dot(low, grad, NN)
            if i > 0:
                old = slice(0, i * TILE)
                gk_sum[h, old, :] += gk_part[: i * TILE]
                gv_sum[h, old, :] += gv_part[: i * TILE]
            gk_sum[h, here, :] = gk_part[i * TILE :]
            gv_sum[h, here, :] = gv_part[i * TILE :]
        return carry

    lax.fori_loop(0, heads, one_head, 0)
    total = jnp.zeros((1, 3 * columns), F32)
    for f in range(length // span):
        crel, lines = slot(f)
        to = slice(f * span, (f + 1) * span)
        o_out[crel, lines, :] = jnp.concatenate(
            [o_turned[h, :, to].T for h in range(heads)], axis=1
        ).astype(BF16)
        both = jnp.concatenate(
            [gq_turned[h, :, to].T for h in range(heads)] + [gk_sum[h, to, :] for h in range(heads)],
            axis=1,
        )
        both = both * 0.125
        copies = 2 * columns // 128
        cos_cols = jnp.concatenate([cos_in[crel, lines, :]] * copies, axis=1)
        sin_cols = jnp.concatenate([sin_in[crel, lines, :]] * copies, axis=1)
        both = both * cos_cols - turned(both) * sin_cols
        value = jnp.concatenate([gv_sum[h, to, :] for h in range(heads)], axis=1)
        grad = jnp.concatenate([both, value], axis=1).astype(BF16)
        g_out[crel, lines, :] = grad
        total = total + jnp.sum(grad.astype(F32), axis=0, keepdims=True)
    sums[...] = jnp.concatenate([total, jnp.zeros((7, 3 * columns), F32)], axis=0)


def attention(place, group, span, q, k, v, cot, w, first, cosine, sine):
    count, columns = q.shape[1:]
    low_count = place.low_count
    heads = columns // HD
    length = low_count * count
    outs = [
        jax.ShapeDtypeStruct((low_count, count, columns), BF16),
        jax.ShapeDtypeStruct((low_count, count, 3 * columns), BF16),
        jax.ShapeDtypeStruct((8, 3 * columns), F32),
    ]
    args = [q, k, v, w, first, cosine, sine, *cot]
    return place.line.call(
        functools.partial(attention_kernel, place, group, span),
        f"attention_{group}",
        (1,),
        [whole(a.shape) for a in args],
        [whole(a.shape) for a in outs],
        outs,
        [pltpu.VMEM((heads, length, HD), BF16)] * 4
        + [pltpu.VMEM((heads, HD, length), F32)] * 2
        + [pltpu.VMEM((heads, length, HD), F32)] * 2,
        args,
    )


def back_kernel(place, groups, *refs):
    normed, hidden, grad_up = refs[:3]
    attended, grad_qkv = refs[3 : 3 + groups], refs[3 + groups : 3 + 2 * groups]
    vec, second = refs[3 + 2 * groups : 5 + 2 * groups]
    keep, send, sums = refs[-3:]
    step = pl.program_id(0)
    width = normed.shape[2]

    @pl.when(step == 0)
    def _():
        sums[...] = jnp.zeros_like(sums)

    two = dot(grad_up[0], second[:, :width], NT)
    out = dot(hidden[0], second[:, width:], NT)
    both = two * vec[2:3, :]
    source = normed[0].astype(F32)
    sums[2:3, :] += jnp.sum(two * source, axis=0, keepdims=True)
    sums[3:4, :] += jnp.sum(two, axis=0, keepdims=True)
    if groups:
        first = refs[5 + 2 * groups]
        cols = HEADS * HD
        one = None
        for h in range(groups):
            term = dot(grad_qkv[h][0], first[:, 3 * cols * h : 3 * cols * (h + 1)], NT)
            one = term if one is None else one + term
            begin = (3 * groups + h) * cols
            out = out + dot(attended[h][0], first[:, begin : begin + cols], NT)
        both = both + one * vec[0:1, :]
        sums[0:1, :] += jnp.sum(one * source, axis=0, keepdims=True)
        sums[1:2, :] += jnp.sum(one, axis=0, keepdims=True)
    split = pl.num_programs(0) // place.low_count

    @pl.when(step < split)
    def _():
        keep[0] = out.astype(BF16)
        keep[1] = both.astype(BF16)

    @pl.when(step >= split)
    def _():
        send[0, 0] = out.astype(BF16)
        send[0, 1] = both.astype(BF16)


def back(place, z, normed, hidden, grad_up, attended, grad_qkv, vec, second, first):
    low_count = place.low_count
    groups, count, width = normed.shape
    split = 2
    lines = count // split
    by_step = lambda cols: pl.BlockSpec((1, lines, cols), lambda g: (g // split, g % split, 0))
    args = [normed, hidden, grad_up, *attended, *grad_qkv]
    fixed = [vec, second] + ([first] if attended else [])

    def sent(g):
        later = jnp.maximum(g - split, 0)
        return (later // split, 0, later % split, 0)

    return place.line.call(
        functools.partial(back_kernel, place, len(attended)),
        f"back_{z}",
        (groups * split,),
        [by_step(v.shape[2]) for v in args] + [whole(v.shape) for v in fixed],
        [
            pl.BlockSpec((2, lines, width), lambda g: (0, jnp.minimum(g, split - 1), 0)),
            pl.BlockSpec((1, 2, lines, width), sent),
            whole((8, width)),
        ],
        [
            jax.ShapeDtypeStruct((2, count, width), BF16),
            jax.ShapeDtypeStruct((low_count - 1, 2, count, width), BF16),
            jax.ShapeDtypeStruct((8, width), F32),
        ],
        [],
        args + fixed,
        vmem=32,
    )


def store_rows(place, rows, block, value, scratch, columns):
    low_count = place.low_count
    for s in range(place.seqs):
        owner = place.owner(s)
        for o in range(low_count):
            begin = owner * (low_count * rows) + (place.low() ^ o) * rows
            scratch[s, o * block : o * block + rows, columns] = value[at(begin, rows, 16), :].astype(BF16)


def product(lefts, rights):
    each = len(lefts) // len(rights)
    total = None
    for i, left in enumerate(lefts):
        lines = left.shape[0]
        right = rights[i // each][(i % each) * lines : (i % each + 1) * lines, :]
        term = dot(left[...], right, TN)
        total = term if total is None else total + term
    return total


def second_grads_kernel(place, rows, count, *refs):
    two, grad_up, hidden = [refs[k * count : (k + 1) * count] for k in range(3)]
    cot, (keep, send, total, turned_rows) = refs[3 * count : -4], refs[-4:]
    step = pl.program_id(0)
    width = two[0].shape[1]
    half = place.seqs // 2

    def one(left, right, columns):
        total[...] = product(left, right)
        store_rows(place, rows, rows, total, turned_rows, columns)

    @pl.when(step == 0)
    def _():
        one(two, grad_up, slice(0, width))

    @pl.when(step == 1)
    def _():
        one(cot, hidden, slice(width, 2 * width))
        keep[...] = turned_rows[:half]
        send[...] = turned_rows[half:]


def second_grads(place, rows, two, grad_up, cot, hidden):
    width = two[0].shape[2]
    flat = [v.reshape(-1, width) for v in (*two, *grad_up, *hidden)] + [p for c in cot for p in c]
    half = (place.seqs // 2, place.low_count * rows, 2 * width)
    return place.line.call(
        functools.partial(second_grads_kernel, place, rows, len(two)),
        "second_grads",
        (2,),
        [whole(v.shape) for v in flat],
        [whole(half)] * 2,
        [jax.ShapeDtypeStruct(half, BF16)] * 2,
        [pltpu.VMEM((width, width), F32), pltpu.VMEM((2 * half[0],) + half[1:], BF16)],
        flat,
    )


def first_grads_kernel(place, rows, last, *refs):
    one, grad_qkv, attended = refs[:3]
    cot, refs = refs[3 : 3 + place.low_count], (None,) * 4 + refs[3 + place.low_count :]
    keep, send, total, turned_rows = refs[-4:]
    seqs, low_count, parts = place.seqs, place.low_count, place.parts
    width = one.shape[1]
    step = HEADS * HD
    block = rows + (VEC if last else 0)
    half = seqs // 2
    total[:, : 3 * step] = dot(one[...], grad_qkv[...], TN)
    total[:, 3 * step :] = product(cot, [attended])
    store_rows(place, rows, block, total, turned_rows, slice(0, width))
    if last:
        at_qkv = 4 + place.groups
        sums_qkv, sums_back, sums_middle = (
            refs[4:at_qkv],
            refs[at_qkv : at_qkv + place.pair],
            refs[at_qkv + place.pair : -4],
        )
        back = sum(s[...] for s in sums_back)
        up = sum(s[0:1, :] for s in sums_middle)
        grad = sums_middle[0][1:2, :] * (1.0 / low_count)
        zero = jnp.zeros((1, step), F32)
        all_qkv = jnp.concatenate(
            [
                jnp.where(place.low() == k, sums_qkv[h][0:1, g * step : (g + 1) * step], zero)
                for g in range(3)
                for k in range(low_count)
                for h in range(place.groups)
            ],
            axis=1,
        )
        all_up = jnp.concatenate(
            [jnp.where(place.part() == k, up, 0.0) for k in range(parts)], axis=1
        )
        lines = [(back[r : r + 1], rows) for r in range(4)]
        lines += [(all_qkv, 3 * rows), (grad, rows), (all_up, 4 * rows)]
        for i in range(seqs):
            for l in range(low_count):
                n = i * low_count + l
                made = [
                    jnp.concatenate(
                        [v[:, n * size : (n + 1) * size], jnp.zeros((1, width - size), F32)], axis=1
                    )
                    for v, size in lines
                ]
                made.append(jnp.zeros((VEC - len(made), width), F32))
                made = jnp.concatenate(made, axis=0).astype(BF16)
                for s in range(seqs):
                    for o in range(low_count):

                        @pl.when((place.owner(s) == i) & ((place.low() ^ o) == l))
                        def _():
                            turned_rows[s, o * block + rows : (o + 1) * block, :] = made

    keep[...] = turned_rows[:half]
    send[...] = turned_rows[half:]


def first_grads(place, group, rows, one, cot, grad_qkv, attended, sums):
    width = one.shape[2]
    args = [v.reshape(-1, v.shape[2]) for v in (one, grad_qkv, attended)] + list(cot) + list(sums)
    half = (place.seqs // 2, place.low_count * (rows + (VEC if sums else 0)), width)
    return place.line.call(
        functools.partial(first_grads_kernel, place, rows, bool(sums)),
        f"first_grads_{group}",
        (1,),
        [whole(v.shape) for v in args],
        [whole(half)] * 2,
        [jax.ShapeDtypeStruct(half, BF16)] * 2,
        [pltpu.VMEM((width, width), F32), pltpu.VMEM((2 * half[0],) + half[1:], BF16)],
        args,
    )


def tokens_kernel(place, source, cot, vec, *rest):
    blocks, (out, grad_in) = rest[: place.seqs], rest[place.seqs :]
    for j in range(place.seqs):
        s = place.owner(j)
        x = source[s].astype(F32)
        out[s] = (x + blocks[j][0].astype(F32) + vec[4:5, :]).astype(BF16)
        mean = jnp.mean(x, axis=1, keepdims=True)
        centred = x - mean
        scale = lax.rsqrt(jnp.mean(centred * centred, axis=1, keepdims=True) + EPS)
        normed = centred * scale
        e = blocks[j][1].astype(F32)
        pulled = (
            e
            - jnp.mean(e, axis=1, keepdims=True)
            - normed * jnp.mean(e * normed, axis=1, keepdims=True)
        ) * scale
        grad_in[s] = (cot[s].astype(F32) + pulled).astype(BF16)


def finish_tokens(place, source, cot, vec, blocks):
    return place.line.call(
        functools.partial(tokens_kernel, place),
        "finish_tokens",
        (1,),
        [whole(source.shape)] * 2 + [whole(vec.shape)] + [whole(b.shape) for b in blocks],
        [whole(source.shape)] * 2,
        [jax.ShapeDtypeStruct(source.shape, BF16)] * 2,
        [],
        [source, cot, vec] + blocks,
    )


def first_end_kernel(place, rows, *refs):
    w_qkv, w_out, lines = refs[-3:]
    low_count, groups = place.low_count, place.groups
    width = w_out.shape[1]
    step = HEADS * HD
    found = refs[:-3]
    even = (lax.axis_index("rep") % 2) == 0
    count = len(found) // groups
    total = None
    for h in range(groups):
        ours = found[h * count : (h + 1) * count]
        for o in range(low_count):
            if count == 1:
                piece = ours[0][o].astype(F32)
            else:
                mine, other = ours[0][o].astype(F32), ours[1][o].astype(F32)
                piece = jnp.concatenate(
                    [jnp.where(even, mine, other), jnp.where(even, other, mine)], axis=1
                )
            for k in range(low_count):

                @pl.when(place.low() == k)
                def _():
                    begin = ((k ^ o) * groups + h) * step
                    for g in range(3):
                        to = g * width + begin
                        w_qkv[:, to : to + step] = piece[:rows, g * step : (g + 1) * step]
                    w_out[:, begin : begin + step] = piece[:rows, 3 * step :]

            if h == groups - 1:
                total = piece[rows:] if total is None else total + piece[rows:]
    lines[...] = total


def first_end(place, rows, width, pieces):
    return place.line.call(
        functools.partial(first_end_kernel, place, rows),
        "first_end",
        (1,),
        [whole(p.shape) for p in pieces],
        [whole((rows, 3 * width)), whole((rows, width)), whole((VEC, width))],
        [
            jax.ShapeDtypeStruct((rows, 3 * width), F32),
            jax.ShapeDtypeStruct((rows, width), F32),
            jax.ShapeDtypeStruct((VEC, width), F32),
        ],
        [],
        pieces,
    )


def second_end_kernel(place, *refs):
    pieces = refs[: place.parts]
    w_up, w_down = refs[place.parts :]
    parts = place.parts
    step = w_up.shape[1] // parts
    for r in range(parts):
        t = place.part() ^ r
        w_up[:, at(t * step, step, 128)] = pieces[r][:, :step].astype(F32)
        w_down[:, at(t * step, step, 128)] = pieces[r][:, step:].astype(F32)


def second_end(place, pieces):
    rows, columns = pieces[0].shape
    shape = (rows, columns // 2 * place.parts)
    return place.line.call(
        functools.partial(second_end_kernel, place),
        "second_end",
        (1,),
        [whole(p.shape) for p in pieces],
        [whole(shape)] * 2,
        [jax.ShapeDtypeStruct(shape, F32)] * 2,
        [],
        pieces,
    )


def add(a, b):
    return (a.astype(F32) + b.astype(F32)).astype(BF16)


def on_device(
    layer_input,
    positions,
    cotangent,
    w_qkv,
    w_out,
    w_up,
    w_down,
    ln1_gain,
    ln1_bias,
    ln2_gain,
    ln2_bias,
    qkv_bias,
    out_bias,
    up_bias,
    down_bias,
):
    seqs, span, width = layer_input.shape
    place = Place(seqs, lax.axis_size("fsdp"), lax.axis_size("rep"))
    low_count, pair = place.low_count, place.pair
    rows = w_qkv.shape[0]

    line = place.line
    lows = range(1, low_count)

    def to_low(v):
        return [place.swap_low(v, o) for o in lows]

    class Gather:
        def __init__(self, block):
            self.slots = [block]
            self.coming = [[place.swap_phase(block, p)] for p in range(place.phases)]

        def step(self, more=0):
            count = len(self.coming[0])
            ahead = self.coming[1][:more] if more else []
            got = line.take(*self.coming.pop(0), *ahead)
            if more:
                self.coming[0][:more] = got[count:]
            for later, p in zip(self.coming, range(place.phases - len(self.coming), place.phases)):
                later.extend(place.swap_phase(v, p) for v in got[:count])
            self.slots.extend(got[:count])

    class Scatter:
        def __init__(self, keep, send):
            self.phase = place.phases - 1
            self.kept = [keep[s] for s in range(keep.shape[0])]
            self.got = place.swap_phase(send, self.phase)

        def step(self):
            got = line.take(self.got)[0]
            self.phase -= 1
            half = len(self.kept) // 2
            sums = [add(v, got[s]) for s, v in enumerate(self.kept)]
            if self.phase >= 0:
                self.kept = sums[:half]
                sent = sums[half] if half == 1 else jnp.stack(sums[half:])
                line.hold(sent)
                got = place.swap_phase(sent, self.phase)
                self.got = got[None] if half == 1 else got
            else:
                block = sums[0].reshape(low_count, sums[0].shape[0] // low_count, -1)
                self.kept = [block[0]]
                line.hold(sums[0])
                self.got = [place.swap_low(block[o], o) for o in lows]

        def end(self):
            return jnp.stack(self.kept + list(line.take(*self.got)))

    masks = [m for m in (1, 2, 4, 8, 16) if m < place.reps]
    even = lax.axis_index("rep") % 2 == 0

    class Reps:
        def __init__(self, mine):
            columns = mine.shape[2] // 2
            low_half, high_half = mine[..., :columns], mine[..., columns:]
            self.held = jnp.where(even, low_half, high_half)
            sent = jnp.where(even, high_half, low_half)
            line.hold(sent)
            self.masks = masks[1:]
            self.got = place.swap_rep(sent, 1)

        def step(self):
            self.held = add(self.held, line.take(self.got)[0])
            line.hold(self.held)
            self.got = place.swap_rep(self.held, self.masks.pop(0) if self.masks else 1)

        def end(self):
            return [self.held, line.take(self.got)[0]]

    class Pairs:
        def __init__(self, mine):
            self.mine = mine
            self.masks = masks[1:] + masks[:1]
            self.got = place.swap_rep(mine, self.masks.pop(0))

        def step(self):
            self.mine = add(self.mine, line.take(self.got)[0])
            line.hold(self.mine)
            self.got = place.swap_rep(self.mine, self.masks.pop(0))

        def end(self):
            return self.mine, line.take(self.got)[0]

    split_x = split_tokens(place, layer_input, "split_input")
    coming = [place.swap_slot(split_x[j], j) for j in range(1, seqs)]
    if pair == 2:
        coming.append(place.swap_rep(split_x[0], 1))
    split_c = split_tokens(place, cotangent, "split_cotangent")
    vectors = (ln1_gain, ln1_bias, ln2_gain, ln2_bias, qkv_bias, out_bias, up_bias, down_bias)
    firsts, seconds = split_weights(place, w_qkv, w_out, w_up, w_down, vectors, positions)
    coming_second = [place.swap_low(seconds[o], o) for o in lows]
    coming = line.take(*coming)
    block_x = jnp.concatenate([split_x[0], *coming[: seqs - 1]], axis=0)
    tokens, grads = [[block_x]], []
    coming_x = to_low(block_x)
    if pair == 2:
        rest = jnp.concatenate(coming[: seqs - 1], axis=0)
        line.hold(rest)
        later_x = place.swap_rep(rest, 1)
    coming_second = line.take(*coming_second)
    block_second = jnp.concatenate([seconds[0], *coming_second], axis=0)
    line.hold(block_x, block_second)
    sent = line.take(*split_c[1:])
    coming_c = [place.swap_slot(v, j) for v, j in zip(sent, range(1, seqs))]
    tokens[0].extend(line.take(*coming_x))
    coming_c = line.take(*coming_c)
    block_c = jnp.concatenate([split_c[0], *coming_c], axis=0)
    line.hold(block_c)
    second = Gather(line.take(block_second)[0])
    grads.append([block_c])
    coming_c = to_low(block_c)
    if pair == 2:
        later_x = line.take(later_x)[0]
        other_x = jnp.concatenate([coming[seqs - 1], later_x], axis=0)
        line.hold(other_x)
        coming_x = to_low(other_x)
        other_c = place.swap_rep(after(block_c, later_x), 1)
    grads[0].extend(line.take(*coming_c))
    second.step()
    if pair == 2:
        tokens.append([other_x, *line.take(*coming_x)])
    coming_first = [place.swap_low(v, o) for v, o in zip(line.take(*firsts[1:]), lows)]
    coming_first = line.take(*coming_first)
    block_first = jnp.concatenate([firsts[0], *coming_first], axis=0)
    line.hold(block_first)
    second.step()
    first = Gather(after(block_first, *second.slots))
    if pair == 2:
        other_c = line.take(other_c)[0]
        coming_c = to_low(other_c)

    w_second, vec, bias, lines_kept = second_tables(place, second.slots, rows, width)
    two, normed, hidden, grad_up, sums_middle, sums_back = [[None] * pair for _ in range(6)]

    def forward(z):
        two[z], normed[z], hidden[z], grad_up[z], sums_middle[z] = middle(
            place, z, tokens[z], grads[z], vec, w_second
        )

    def backward(z, attended, grad_qkv, w_first):
        keep, send, sums_back[z] = back(
            place, z, normed[z], hidden[z], grad_up[z], attended, grad_qkv, vec, w_second, w_first
        )
        return keep, [place.swap_low(send[o - 1], o) for o in lows]

    def low_sum(keep, coming):
        total = keep.astype(F32)
        for v in line.take(*coming):
            total = total + v.astype(F32)
        return total

    if pair == 2:
        grads.append([other_c, *line.take(*coming_c)])
        forward(1)
        keep, coming = backward(1, [], [], None)
    first.step(more=1)
    forward(0)
    out_pieces, out_found = [], []

    def next_piece():
        if out_pieces:
            out_found.append(line.take(out_coming.pop())[0])
            out_pieces.pop(0)
        if out_pieces:
            out_coming.append(place.swap_rep(after(out_pieces[0], out_found[-1]), 1))

    out_coming = []
    if pair == 2:
        out_other = low_sum(keep, coming).astype(BF16).reshape(2 * seqs, span, width)
        cuts = [2 * seqs * k // 8 for k in (0, 3, 6, 8)]
        out_pieces = [out_other[a:b] for a, b in zip(cuts, cuts[1:])]
        line.hold(*out_pieces)
        out_coming.append(place.swap_rep(out_pieces[0], 1))
    second_sums = Scatter(*second_grads(place, rows, two, grad_up, grads, hidden))

    first.step()
    w_first, seen, cosine, sine = first_tables(place, first.slots, lines_kept, rows, width, span)
    one, heads = front(place, tokens[0], w_first, vec, bias, cosine, sine)
    attended, grad_qkv, sums_qkv, first_sums = [[None] * place.groups for _ in range(4)]
    cot = grads[0]
    for h in range(place.groups):
        next_piece()
        attended[h], grad_qkv[h], sums_qkv[h] = attention(
            place, h, span, *heads[h], cot, w_first, seen, cosine, sine
        )
        second_sums.step()
        if h > 0:
            first_sums[h - 1].step()
        if h < place.groups - 1:
            first_sums[h] = Scatter(
                *first_grads(place, h, rows, one, cot, grad_qkv[h], attended[h], [])
            )
    while second_sums.phase >= 0:
        second_sums.step()
    second_mine = second_sums.end()
    line.hold(second_mine)
    while out_pieces:
        next_piece()
    second_reps = Pairs(second_mine[0]) if pair == 2 else Reps(second_mine)
    keep, coming = backward(0, attended, grad_qkv, w_first)
    if place.groups > 1:
        first_sums[0].step()
    h = place.groups - 1
    first_sums[h] = Scatter(
        *first_grads(
            place, h, rows, one, cot, grad_qkv[h], attended[h], sums_qkv + sums_back + sums_middle
        )
    )

    reps = []
    for h in range(place.groups - 1):
        mine = first_sums[h].end()
        line.hold(mine)
        reps.append(Reps(mine))
    if pair == 2:
        more_reps = []
        for o in lows:
            (more_reps or [second_reps])[-1].step()
            more_reps.append(Pairs(after(second_mine[o], *line.ahead)))
    last = first_sums[-1]
    last.step()
    for r in reps:
        r.step()
    out_sum = low_sum(keep, coming)
    if pair == 2:
        out_sum = out_sum + jnp.concatenate(out_found).reshape(out_sum.shape).astype(F32)
    out_sum = out_sum.astype(BF16).reshape(2, seqs, span, width)
    line.hold(out_sum)
    blocks = [out_sum[:, s] for s in range(seqs)]

    def pass_on(phase):
        chosen = [s for s in range(seqs) if s >> phase & 1]
        got = place.swap_phase(jnp.stack([blocks[s] for s in chosen]), phase)
        return chosen, got

    chosen, got = pass_on(0)
    last.step()
    mine = last.end()
    line.hold(mine)
    reps.append(Reps(mine))
    for phase in range(1, place.phases + 1):
        got = line.take(got)[0]
        for k, s in enumerate(chosen):
            blocks[s] = got[k]
        if phase < place.phases:
            chosen, got = pass_on(phase)
    if pair == 2:
        more_reps[-1].step()
    else:
        while second_reps.masks:
            second_reps.step()
        second_reps.step()
    for r in reps:
        while r.masks:
            r.step()
    for r in reps:
        r.step()
    output, grad_input = finish_tokens(place, layer_input, cotangent, vec, blocks)
    if pair == 2:
        ends = [second_reps.end()] + [r.end() for r in more_reps]
        pieces = [e[0] for e in ends] + [e[1] for e in ends]
    else:
        pieces = second_reps.end()
        pieces = jnp.where(even, pieces[0], pieces[1]), jnp.where(even, pieces[1], pieces[0])
        pieces = list(jnp.concatenate(pieces, axis=2))
    grad_w_up, grad_w_down = second_end(place, pieces)
    pieces = [p for r in reps for p in r.end()]
    grad_w_qkv, grad_w_out, lines = first_end(place, rows, width, pieces)
    ln1_gain_g, ln1_bias_g, ln2_gain_g, ln2_bias_g = [lines[r, :rows] for r in range(4)]
    qkv_g = lines[4, : 3 * rows]
    out_g = lines[5, :rows]
    up_g = lines[6, : 4 * rows]
    return (
        output,
        grad_input,
        grad_w_qkv,
        grad_w_out,
        grad_w_up,
        grad_w_down,
        ln1_gain_g,
        ln1_bias_g,
        ln2_gain_g,
        ln2_bias_g,
        qkv_g,
        out_g,
        up_g,
        out_g,
    )


def solution(mesh):
    tokens = P("rep", "fsdp", None)
    matrix = P("fsdp", None)
    vector = P("fsdp")
    return jax.shard_map(
        on_device,
        mesh=mesh,
        in_specs=(tokens, P("rep", "fsdp"), tokens) + (matrix,) * 4 + (vector,) * 8,
        out_specs=(tokens, tokens) + (matrix,) * 4 + (vector,) * 8,
        check_vma=False,
    )
```

time: 787 us -> 241 us (0.31)
  waiting for transfers between devices: 383 us -> 73.9 us
  matrix products: 176 us -> 0 us
  Pallas kernels: 0 us -> 84.6 us
  blocking collectives: 80.3 us -> 0 us
  other arithmetic: 72.3 us -> 6.86 us
  starting transfers between devices: 0.82 us -> 52.1 us
  local copies, waits for them, and re-layouts: 51.7 us -> 18.4 us
  between operations: 16.3 us -> 1.8 us
    reduce_scatter x2 -> x0, waiting for transfers between devices: 255 us -> none  [the longest x1 173 us: on_device(): lax.psum_scatter(jnp.concatenate([jnp.einsum('rc,rk->ck', input_one, grad...]
    dot_general x19 -> x0, matrix products: 176 us -> none  [the longest x1 20.5 us: on_device(): jnp.einsum('sqhd,skhd->shqk', grad_heads, values, preferred_element_type=...]
    pallas_call x0 -> x18, Pallas kernels: none -> 84.6 us  [call(): pl.pallas_call(kernel, grid=grid, in_specs=in_specs, out_specs=out_specs,...]
    ppermute x0 -> x47, waiting for transfers between devices: none -> 73.9 us  [the longest x14 41.3 us: swap_phase(): return lax.ppermute(v, 'fsdp', [(i, to(i)) for i in range(self.shards)])]
    psum x1 -> x0, waiting for transfers between devices: 64.2 us -> none  [on_device(): owned = lax.psum(owned, 'rep')]
    all_gather x6 -> x0, waiting for transfers between devices: 61.3 us -> none  [the longest x1 37.4 us: on_device(): lax.all_gather(key_flat, 'fsdp', axis=1, tiled=True)]
    ppermute x0 -> x47, starting transfers between devices: none -> 52.1 us  [the longest x16 26.9 us: swap_rep(): return lax.ppermute(v, 'rep', [(i, i ^ mask) for i in range(self.reps)])]
    psum x1 -> x0, blocking collectives: 44.4 us -> none  [on_device(): lax.psum((local_vectors[0], local_vectors[1], local_vectors[2], local_vec...]
  transfers between devices with their start and end apart: 9 -> 47, of which waited for: 5 -> 20; matrix products, arithmetic and copies ran while one was open for 33% -> 4% of each run, Pallas kernels for 0% -> 34%
where the time goes in v2:
time: 241 us; the launch traced here: 238 us
  Pallas kernels  84.6 us (35%)
  waiting for transfers between devices  73.9 us (31%)
  starting transfers between devices  52.1 us (22%)
  local copies, waits for them, and re-layouts  18.4 us (8%)
  other arithmetic  6.86 us (3%)
    pallas_call x18, Pallas kernels, call(): pl.pallas_call(kernel, grid=grid, in_specs=in_specs, out_specs=out_specs,...  84.6 us
    ppermute x14, waiting for transfers between devices, swap_phase(): return lax.ppermute(v, 'fsdp', [(i, to(i)) for i in range(self.shards)])  41.3 us
    ppermute x16, starting transfers between devices, swap_rep(): return lax.ppermute(v, 'rep', [(i, i ^ mask) for i in range(self.reps)])  26.9 us
    ppermute x14, starting transfers between devices, swap_phase(): return lax.ppermute(v, 'fsdp', [(i, to(i)) for i in range(self.shards)])  16.6 us
    ppermute x16, waiting for transfers between devices, swap_rep(): return lax.ppermute(v, 'rep', [(i, i ^ mask) for i in range(self.reps)])  16.4 us
    unnamed x98, local copies, waits for them, and re-layouts  13.2 us
    ppermute x6, waiting for transfers between devices, swap_slot(): return lax.ppermute(v, 'fsdp', [(i, to(i)) for i in range(self.shards)])  11 us
    ppermute x6, starting transfers between devices, swap_slot(): return lax.ppermute(v, 'fsdp', [(i, to(i)) for i in range(self.shards)])  7.04 us
  transfers between devices with their start and end apart: 47, of which 20 were waited for; matrix products, arithmetic and copies ran while one was open for 4% of the time, Pallas kernels for 34%

profile of v2, /device:TPU:0, one launch (start us, length us, event | category | flops | bytes accessed | tf_op | source)
XLA Modules:
  0.0 237.6 jit_solution(11878878411484002455)
XLA Ops:
  0.6 2.1 split_input.1
  2.7 3.0 %collective-permute-start.3 = (bf16[128,768]{1,0:T(8,128)(2,1)}, bf16[128,768]{1,0:T(8,128)(2,1)S(1)}, u32[]{:S(2)}, u32[]{:S(2)}) collective-permute-start(bf16[128,768]{1,0:T(8,128)(2,1)} %get-tuple-element.151), channel_id=1, source_target_pairs={{0,8},{8,0},{16,24},{24,16},{1,9},{9,1},{17,25},{25,17},{2,10},{10... | collective-permute-start | bytes 589832 | tf_op jit(solution)/shard_map/ppermute | solution.py:113
  9.2 2.1 split_cotangent.1
  12.5 2.7 %split_weights.1 = (bf16[96,1536]{1,0:T(8,128)(2,1)}, bf16[96,1536]{1,0:T(8,128)(2,1)}, bf16[112,1536]{1,0:T(8,128)(2,1)}, bf16[112,1536]{1,0:T(8,128)(2,1)}) custom-call(bf16[96,2304]{1,0:T(8,128)(2,1)} %w_qkv, bf16[96,768]{1,0:T(8,128)(2,1)} %w_out.1, bf16[96,3072]{1,0:T(8,128)(2,1)} %w_up.1, bf16[96,3072]{1,0:T(8,128)(2,1)} %w_down.1, ...), custom_call_target="tpu_custom_call" | custom-call | flops 1150000000 | bytes 3600000 | tf_op jit(solution)/shard_map/split_weights/pallas_call | solution.py:140
  15.3 2.5 %collective-permute-done.2 = bf16[128,768]{1,0:T(8,128)(2,1)S(1)} collective-permute-done((bf16[128,768]{1,0:T(8,128)(2,1)}, bf16[128,768]{1,0:T(8,128)(2,1)S(1)}, u32[]{:S(2)}, u32[]{:S(2)}) %collective-permute-start.2) | collective-permute-done | bytes 196640 | tf_op jit(solution)/shard_map/ppermute | solution.py:103
  18.4 2.2 collective-permute-done.5
  20.7 1.6 collective-permute-start.6
  22.3 1.5 collective-permute-start.7
  24.6 3.6 %collective-permute-done.6 = bf16[128,768]{1,0:T(8,128)(2,1)S(1)} collective-permute-done((bf16[128,768]{1,0:T(8,128)(2,1)S(1)}, bf16[128,768]{1,0:T(8,128)(2,1)S(1)}, u32[]{:S(2)}, u32[]{:S(2)}) %collective-permute-start.6) | collective-permute-done | bytes 196640 | tf_op jit(solution)/shard_map/ppermute | solution.py:103
  28.3 4.9 %collective-permute-done.8 = bf16[128,768]{1,0:T(8,128)(2,1)S(1)} collective-permute-done((bf16[128,768]{1,0:T(8,128)(2,1)S(1)}, bf16[128,768]{1,0:T(8,128)(2,1)S(1)}, u32[]{:S(2)}, u32[]{:S(2)}) %collective-permute-start.8) | collective-permute-done | bytes 196640 | tf_op jit(solution)/shard_map/ppermute | solution.py:103
  33.3 1.6 collective-permute-start.11
  34.9 4.0 %collective-permute-done.4 = bf16[384,768]{1,0:T(8,128)(2,1)S(1)} collective-permute-done((bf16[384,768]{1,0:T(8,128)(2,1)S(1)}, bf16[384,768]{1,0:T(8,128)(2,1)S(1)}, u32[]{:S(2)}, u32[]{:S(2)}) %collective-permute-start.4) | collective-permute-done | bytes 589856 | tf_op jit(solution)/shard_map/ppermute | solution.py:113
  40.8 5.7 %collective-permute-done.11.rest_1_ = bf16[224,1536]{1,0:T(8,128)(2,1)S(1)} collective-permute-done((bf16[224,1536]{1,0:T(8,128)(2,1)S(1)}, bf16[224,1536]{1,0:T(8,128)(2,1)S(1)}, u32[]{:S(2)}, u32[]{:S(2)}) %collective-permute-start.11) | collective-permute-done | bytes 688160 | tf_op jit(solution)/shard_map/ppermute | solution.py:110
  46.9 1.5 collective-permute-done.13
  48.4 2.8 %collective-permute-done.14.rest_2_ = bf16[224,1536]{1,0:T(8,128)(2,1)S(1)} collective-permute-done((bf16[224,1536]{1,0:T(8,128)(2,1)S(1)}, bf16[224,1536]{1,0:T(8,128)(2,1)S(1)}, u32[]{:S(2)}, u32[]{:S(2)}) %collective-permute-start.14) | collective-permute-done | bytes 688160 | tf_op jit(solution)/shard_map/ppermute | solution.py:110
  51.2 7.4 %collective-permute-done.15.rest_3_ = bf16[224,1536]{1,0:T(8,128)(2,1)S(1)} collective-permute-done((bf16[224,1536]{1,0:T(8,128)(2,1)S(1)}, bf16[224,1536]{1,0:T(8,128)(2,1)S(1)}, u32[]{:S(2)}, u32[]{:S(2)}) %collective-permute-start.15) | collective-permute-done | bytes 688160 | tf_op jit(solution)/shard_map/ppermute | solution.py:110
  62.6 6.4 %middle_1.1 = (bf16[2,512,768]{2,1,0:T(8,128)(2,1)S(1)}, bf16[2,512,768]{2,1,0:T(8,128)(2,1)S(1)}, bf16[2,512,768]{2,1,0:T(8,128)(2,1)S(1)}, bf16[2,512,768]{2,1,0:T(8,128)(2,1)S(1)}, f32[8,768]{1,0:T(8,128)S(1)}) custom-call(bf16[512,768]{1,0:T(8,128)(2,1)S(1)} %constant_dynamic-update-slice_fusion.13.refs_0_, ...), custom_call_target="tpu_custom_call" | custom-call | flops 115000000 | bytes 360000 | tf_op jit(solution)/shard_map/middle_1/pallas_call | solution.py:140
  69.0 4.0 %back_1.1 = (bf16[2,512,768]{2,1,0:T(8,128)(2,1)S(1)}, bf16[1,2,512,768]{3,2,1,0:T(8,128)(2,1)S(1)}, f32[8,768]{1,0:T(8,128)S(1)}) custom-call(bf16[2,512,768]{2,1,0:T(8,128)(2,1)S(1)} %get-tuple-element.197.refs_0_, bf16[2,512,768]{2,1,0:T(8,128)(2,1)S(1)} %get-tuple-element.198.refs_1_, bf16[2,512,768]{2,1,0:T(8,128)(2,1)S(1)} %get-tuple-element.199.refs_2_, ...), custom_call_target="tpu_custom_call" | custom-call | flops 115000000 | bytes 360000 | tf_op jit(solution)/shard_map/back_1/pallas_call | solution.py:140
  74.7 1.8 collective-permute-start.20
  76.4 6.4 %middle_0.1 = (bf16[2,512,768]{2,1,0:T(8,128)(2,1)S(1)}, bf16[2,512,768]{2,1,0:T(8,128)(2,1)S(1)}, bf16[2,512,768]{2,1,0:T(8,128)(2,1)S(1)}, bf16[2,512,768]{2,1,0:T(8,128)(2,1)S(1)}, f32[8,768]{1,0:T(8,128)S(1)}) custom-call(bf16[512,768]{1,0:T(8,128)(2,1)S(1)} %get-tuple-element.219.refs_0_, bf16[512,768]{1,0:T(8,128)(2,1)S(1)} %collective-permute-done.9.refs_1_, ...), custom_call_target="tpu_custom_call" | custom-call | flops 11500000256 | bytes 36000000 | tf_op jit(solution)/shard_map/middle_0/pallas_call | solution.py:140
  85.4 7.1 %second_grads.1 = (bf16[2,192,1536]{2,1,0:T(8,128)(2,1)S(1)}, bf16[2,192,1536]{2,1,0:T(8,128)(2,1)S(1)}) custom-call(bf16[1024,768]{1,0:T(8,128)(2,1)S(1)} %bitcast.85, bf16[1024,768]{1,0:T(8,128)(2,1)S(1)} %bitcast.84, bf16[1024,768]{1,0:T(8,128)(2,1)S(1)} %bitcast.83, bf16[1024,768]{1,0:T(8,128)(2,1)S(1)} %bitcast.81, bf16[1024,768]{1,0:T(8,128)(2,1)S(1)} %bitcast.82, ...), custom_call_target="tpu_custom_call" | custom-call | flops 115000000 | bytes 360000 | tf_op jit(solution)/shard_map/second_grads/pallas_call | solution.py:140
  93.4 5.4 %front.1 = (bf16[2,512,768]{2,1,0:T(8,128)(2,1)S(1)}, bf16[2,512,192]{2,1,0:T(8,128)(2,1)S(1)}, bf16[2,512,192]{2,1,0:T(8,128)(2,1)S(1)}, bf16[2,512,192]{2,1,0:...) custom-call(bf16[512,768]{1,0:T(8,128)(2,1)S(1)} %get-tuple-element., ...), custom_call_target="tpu_custom_call" | custom-call | flops 115000000 | bytes 360000 | tf_op jit(solution)/shard_map/front/pallas_call | solution.py:140
  100.4 14.5 %attention_0.1 = (bf16[2,512,192]{2,1,0:T(8,128)(2,1)S(1)}, bf16[2,512,576]{2,1,0:T(8,128)(2,1)S(1)}, f32[8,576]{1,0:T(8,128)S(1)}) custom-call(bf16[2,512,192]{2,1,0:T(8,128)(2,1)S(1)} %get-tuple-element.227.q_in, bf16[2,512,192]{2,1,0:T(8,128)(2,1)S(1)} %get-tuple-element.228.k_in, bf16[2,512,192]{2,1,0:T(8,128)(2,1)S(1)} %get-tuple-element.229.v_in, ...), custom_call_target="tpu_custom_call" | custom-call | flops 11500000256 | bytes 36000000 | tf_op jit(solution)/shard_map/attention_0/pallas_call | solution.py:140
  115.2 1.6 collective-permute-start.25
  116.7 2.8 %first_grads_0.1 = (bf16[2,192,768]{2,1,0:T(8,128)(2,1)S(1)}, bf16[2,192,768]{2,1,0:T(8,128)(2,1)}) custom-call(bf16[1024,768]{1,0:T(8,128)(2,1)S(1)} %bitcast.78, bf16[1024,576]{1,0:T(8,128)(2,1)S(1)} %bitcast.87, bf16[1024,192]{1,0:T(8,128)(2,1)S(1)} %bitcast.88, bf16[512,768]{1,0:T(8,128)(2,1)S(1)} %constant_dynamic-update-slice_fusion.9.refs_2_.refs_6_.refs_0_.refs_3_, ...), custom_call_target="tpu_custom_call" | custom-call | flops 115000000 | bytes 360000 | tf_op jit(solution)/shard_map/first_grads_0/pallas_call | solution.py:140
  120.4 1.7 collective-permute-start.24
  122.6 14.6 %attention_1.1 = (bf16[2,512,192]{2,1,0:T(8,128)(2,1)S(1)}, bf16[2,512,576]{2,1,0:T(8,128)(2,1)S(1)}, f32[8,576]{1,0:T(8,128)S(1)}) custom-call(bf16[2,512,192]{2,1,0:T(8,128)(2,1)S(1)} %get-tuple-element.240.q_in, bf16[2,512,192]{2,1,0:T(8,128)(2,1)S(1)} %get-tuple-element.241.k_in, bf16[2,512,192]{2,1,0:T(8,128)(2,1)S(1)} %get-tuple-element.242.v_in, ...), custom_call_target="tpu_custom_call" | custom-call | flops 11500000256 | bytes 36000000 | tf_op jit(solution)/shard_map/attention_1/pallas_call | solution.py:140
  140.6 2.6 %collective-permute-start.31 = (bf16[96,1536]{1,0:T(8,128)(2,1)}, bf16[96,1536]{1,0:T(8,128)(2,1)S(1)}, u32[]{:S(2)}, u32[]{:S(2)}) collective-permute-start(bf16[96,1536]{1,0:T(8,128)(2,1)} %get-tuple-element.298), channel_id=1, source_target_pairs={{0,16},{8,24},{16,0},{24,8},{1,17},{9,25},{17,1},{25,9},{2,18},{10... | collective-permute-start | bytes 884744 | tf_op jit(solution)/shard_map/ppermute | solution.py:113
  143.2 1.7 copy-done.6
  153.8 7.4 %back_0.1 = (bf16[2,512,768]{2,1,0:T(8,128)(2,1)S(1)}, bf16[1,2,512,768]{3,2,1,0:T(8,128)(2,1)S(1)}, f32[8,768]{1,0:T(8,128)S(1)}) custom-call(bf16[2,512,768]{2,1,0:T(8,128)(2,1)S(1)} %copy-done.25, bf16[2,512,768]{2,1,0:T(8,128)(2,1)S(1)} %copy-done.8, bf16[2,512,768]{2,1,0:T(8,128)(2,1)S(1)} %copy-done.10, bf16[2,512,192]{2,1,0:T(8,128)(2,1)S(1)} %copy-done.19, ...), custom_call_target="tpu_custom_call" | custom-call | flops 11500000256 | bytes 36000000 | tf_op jit(solution)/shard_map/back_0/pallas_call | solution.py:140
  163.0 2.6 %first_grads_1.1 = (bf16[2,224,768]{2,1,0:T(8,128)(2,1)S(1)}, bf16[2,224,768]{2,1,0:T(8,128)(2,1)S(1)}) custom-call(bf16[1024,768]{1,0:T(8,128)(2,1)S(1)} %bitcast.79, bf16[1024,576]{1,0:T(8,128)(2,1)S(1)} %bitcast.86, bf16[1024,192]{1,0:T(8,128)(2,1)S(1)} %bitcast.89, ...), custom_call_target="tpu_custom_call" | custom-call | flops 115000000 | bytes 360000 | tf_op jit(solution)/shard_map/first_grads_1/pallas_call | solution.py:140
  168.0 1.6 collective-permute-start.35
  169.7 7.0 %collective-permute-done.30 = bf16[2,224,768]{2,1,0:T(8,128)(2,1)S(1)} collective-permute-done((bf16[2,224,768]{2,1,0:T(8,128)(2,1)S(1)}, bf16[2,224,768]{2,1,0:T(8,128)(2,1)S(1)}, u32[]{:S(2)}, u32[]{:S(2)}) %collective-permute-start.30) | collective-permute-done | bytes 688160 | tf_op jit(solution)/shard_map/ppermute | solution.py:110
  176.8 1.5 collective-permute-start.33
  179.9 4.2 %collective-permute-done.33 = bf16[224,768]{1,0:T(8,128)(2,1)S(1)} collective-permute-done((bf16[224,768]{1,0:T(8,128)(2,1)S(1)}, bf16[224,768]{1,0:T(8,128)(2,1)S(1)}, u32[]{:S(2)}, u32[]{:S(2)}) %collective-permute-start.33) | collective-permute-done | bytes 344096 | tf_op jit(solution)/shard_map/ppermute | solution.py:110
  185.8 6.7 %collective-permute-done.39 = bf16[2,2,128,768]{3,2,1,0:T(8,128)(2,1)S(1)} collective-permute-done((bf16[2,2,128,768]{3,2,1,0:T(8,128)(2,1)S(1)}, bf16[2,2,128,768]{3,2,1,0:T(8,128)(2,1)S(1)}, u32[]{:S(2)}, u32[]{:S(2)}) %collective-permute-start.39) | collective-permute-done | bytes 786464 | tf_op jit(solution)/shard_map/ppermute | solution.py:110
  194.1 1.6 collective-permute-start.46
  195.7 2.6 %collective-permute-start.42 = (bf16[2,96,384]{2,1,0:T(8,128)(2,1)S(1)}, bf16[2,96,384]{2,1,0:T(8,128)(2,1)S(1)}, u32[]{:S(2)}, u32[]{:S(2)}) collective-permute-start(bf16[2,96,384]{2,1,0:T(8,128)(2,1)S(1)} %add_convert_fusion.15), channel_id=1, source_target_pairs={{0,16},{8,24},{16,0},{24,8},{1,17},{9,25},{17,1},{25,9},{2,18},{10... | collective-permute-start | bytes 442376 | tf_op jit(solution)/shard_map/ppermute | solution.py:113
  198.7 6.0 %collective-permute-done.40 = bf16[2,2,128,768]{3,2,1,0:T(8,128)(2,1)S(1)} collective-permute-done((bf16[2,2,128,768]{3,2,1,0:T(8,128)(2,1)S(1)}, bf16[2,2,128,768]{3,2,1,0:T(8,128)(2,1)S(1)}, u32[]{:S(2)}, u32[]{:S(2)}) %collective-permute-start.40) | collective-permute-done | bytes 786464 | tf_op jit(solution)/shard_map/ppermute | solution.py:110
  204.7 6.8 %collective-permute-done.38 = bf16[96,1536]{1,0:T(8,128)(2,1)S(1)} collective-permute-done((bf16[96,1536]{1,0:T(8,128)(2,1)}, bf16[96,1536]{1,0:T(8,128)(2,1)S(1)}, u32[]{:S(2)}, u32[]{:S(2)}) %collective-permute-start.38) | collective-permute-done | bytes 294944 | tf_op jit(solution)/shard_map/ppermute | solution.py:113
  212.6 2.7 %collective-permute-done.37 = bf16[2,112,384]{2,1,0:T(8,128)(2,1)S(1)} collective-permute-done((bf16[2,112,384]{2,1,0:T(8,128)(2,1)S(1)}, bf16[2,112,384]{2,1,0:T(8,128)(2,1)S(1)}, u32[]{:S(2)}, u32[]{:S(2)}) %collective-permute-start.37) | collective-permute-done | bytes 172064 | tf_op jit(solution)/shard_map/ppermute | solution.py:113
  215.4 4.4 %collective-permute-start.41 = (bf16[2,112,384]{2,1,0:T(8,128)(2,1)S(1)}, bf16[2,112,384]{2,1,0:T(8,128)(2,1)S(1)}, u32[]{:S(2)}, u32[]{:S(2)}) collective-permute-start(bf16[2,112,384]{2,1,0:T(8,128)(2,1)S(1)} %add_convert_fusion.13), channel_id=1, source_target_pairs={{0,16},{8,24},{16,0},{24,8},{1,17},{9,25},{17,1},{25,9},{2,18},{10... | collective-permute-start | bytes 516104 | tf_op jit(solution)/shard_map/ppermute | solution.py:113
  219.9 2.5 %collective-permute-start.44 = (bf16[2,96,384]{2,1,0:T(8,128)(2,1)S(1)}, bf16[2,96,384]{2,1,0:T(8,128)(2,1)S(1)}, u32[]{:S(2)}, u32[]{:S(2)}) collective-permute-start(bf16[2,96,384]{2,1,0:T(8,128)(2,1)S(1)} %add_convert_fusion.14.refs_0_), channel_id=1, source_target_pairs={{0,8},{8,0},{16,24},{24,16},{1,9},{9,1},{17,25},{25,17},{2,10},{10... | collective-permute-start | bytes 442376 | tf_op jit(solution)/shard_map/ppermute | solution.py:113
  222.5 2.2 collective-permute-done.41
  224.8 4.9 %collective-permute-start.43 = (bf16[2,112,384]{2,1,0:T(8,128)(2,1)S(1)}, bf16[2,112,384]{2,1,0:T(8,128)(2,1)S(1)}, u32[]{:S(2)}, u32[]{:S(2)}) collective-permute-start(bf16[2,112,384]{2,1,0:T(8,128)(2,1)S(1)} %add_convert_fusion.12.refs_2_), channel_id=1, source_target_pairs={{0,8},{8,0},{16,24},{24,16},{1,9},{9,1},{17,25},{25,17},{2,10},{10... | collective-permute-start | bytes 516104 | tf_op jit(solution)/shard_map/ppermute | solution.py:113
  229.7 2.1 finish_tokens.1
  231.8 1.6 second_end.1
  233.4 1.5 first_end.1
  (200 shorter events, 46.0 us)
Async XLA Ops:
  2.7 12.5 %collective-permute-start.3 = (bf16[128,768]{1,0:T(8,128)(2,1)}, bf16[128,768]{1,0:T(8,128)(2,1)S(1)}, u32[]{:S(2)}, u32[]{:S(2)}) collective-permute-start(bf16[128,768]{1,0:T(8,128)(2,1)} %get-tuple-element.151), channel_id=1, source_target_pairs={{0,8},{8,0},{16,24},{24,16},{1,9},{9,1},{17,25},{25,17},{2,10},{10... | collective-permute-start | bytes 589832 | tf_op jit(solution)/shard_map/ppermute | solution.py:113
  5.8 9.5 %collective-permute-start = (bf16[128,768]{1,0:T(8,128)(2,1)}, bf16[128,768]{1,0:T(8,128)(2,1)S(1)}, u32[]{:S(2)}, u32[]{:S(2)}) collective-permute-start(bf16[128,768]{1,0:T(8,128)(2,1)} %get-tuple-element.152), channel_id=1, source_target_pairs={{0,2},{1,5},{2,0},{3,7},{4,6},{5,1},{6,4},{7,3},{8,10},{9,13},{10,... | collective-permute-start | bytes 589832 | tf_op jit(solution)/shard_map/ppermute | solution.py:103
  7.2 8.0 %collective-permute-start.1 = (bf16[128,768]{1,0:T(8,128)(2,1)}, bf16[128,768]{1,0:T(8,128)(2,1)S(1)}, u32[]{:S(2)}, u32[]{:S(2)}) collective-permute-start(bf16[128,768]{1,0:T(8,128)(2,1)} %get-tuple-element.153), channel_id=1, source_target_pairs={{0,4},{1,3},{2,6},{3,1},{4,0},{5,7},{6,2},{7,5},{8,12},{9,11},{10,... | collective-permute-start | bytes 589832 | tf_op jit(solution)/shard_map/ppermute | solution.py:103
  8.8 9.0 %collective-permute-start.2 = (bf16[128,768]{1,0:T(8,128)(2,1)}, bf16[128,768]{1,0:T(8,128)(2,1)S(1)}, u32[]{:S(2)}, u32[]{:S(2)}) collective-permute-start(bf16[128,768]{1,0:T(8,128)(2,1)} %get-tuple-element.154), channel_id=1, source_target_pairs={{0,6},{1,7},{2,4},{3,5},{4,2},{5,3},{6,0},{7,1},{8,14},{9,15},{10,... | collective-permute-start | bytes 589832 | tf_op jit(solution)/shard_map/ppermute | solution.py:103
  17.8 6.8 %collective-permute-start.9 = (bf16[512,768]{1,0:T(8,128)(2,1)S(1)}, bf16[512,768]{1,0:T(8,128)(2,1)S(1)}, u32[]{:S(2)}, u32[]{:S(2)}) collective-permute-start(bf16[512,768]{1,0:T(8,128)(2,1)S(1)} %get-tuple-element.219.refs_0_), channel_id=1, source_target_pairs={{0,1},{1,0},{2,3},{3,2},{4,5},{5,4},{6,7},{7,6},{8,9},{9,8},{10,11... | collective-permute-start | bytes 2359304 | tf_op jit(solution)/shard_map/ppermute | solution.py:96
  17.9 2.8 %collective-permute-start.5 = (bf16[112,1536]{1,0:T(8,128)(2,1)S(1)}, bf16[112,1536]{1,0:T(8,128)(2,1)S(1)}, u32[]{:S(2)}, u32[]{:S(2)}) collective-permute-start(bf16[112,1536]{1,0:T(8,128)(2,1)S(1)} %copy-done.39), channel_id=1, source_target_pairs={{0,1},{1,0},{2,3},{3,2},{4,5},{5,4},{6,7},{7,6},{8,9},{9,8},{10,11... | collective-permute-start | bytes 1032200 | tf_op jit(solution)/shard_map/ppermute | solution.py:96
  20.7 7.5 %collective-permute-start.6 = (bf16[128,768]{1,0:T(8,128)(2,1)S(1)}, bf16[128,768]{1,0:T(8,128)(2,1)S(1)}, u32[]{:S(2)}, u32[]{:S(2)}) collective-permute-start(bf16[128,768]{1,0:T(8,128)(2,1)S(1)} %copy-done.43), channel_id=1, source_target_pairs={{0,2},{1,5},{2,0},{3,7},{4,6},{5,1},{6,4},{7,3},{8,10},{9,13},{10,... | collective-permute-start | bytes 589832 | tf_op jit(solution)/shard_map/ppermute | solution.py:103
  22.3 6.0 %collective-permute-start.7 = (bf16[128,768]{1,0:T(8,128)(2,1)S(1)}, bf16[128,768]{1,0:T(8,128)(2,1)S(1)}, u32[]{:S(2)}, u32[]{:S(2)}) collective-permute-start(bf16[128,768]{1,0:T(8,128)(2,1)S(1)} %copy-done.42), channel_id=1, source_target_pairs={{0,4},{1,3},{2,6},{3,1},{4,0},{5,7},{6,2},{7,5},{8,12},{9,11},{10,... | collective-permute-start | bytes 589832 | tf_op jit(solution)/shard_map/ppermute | solution.py:103
  23.8 9.3 %collective-permute-start.8 = (bf16[128,768]{1,0:T(8,128)(2,1)S(1)}, bf16[128,768]{1,0:T(8,128)(2,1)S(1)}, u32[]{:S(2)}, u32[]{:S(2)}) collective-permute-start(bf16[128,768]{1,0:T(8,128)(2,1)S(1)} %copy-done.41), channel_id=1, source_target_pairs={{0,6},{1,7},{2,4},{3,5},{4,2},{5,3},{6,0},{7,1},{8,14},{9,15},{10,... | collective-permute-start | bytes 589832 | tf_op jit(solution)/shard_map/ppermute | solution.py:103
  24.3 14.5 %collective-permute-start.4 = (bf16[384,768]{1,0:T(8,128)(2,1)S(1)}, bf16[384,768]{1,0:T(8,128)(2,1)S(1)}, u32[]{:S(2)}, u32[]{:S(2)}) collective-permute-start(bf16[384,768]{1,0:T(8,128)(2,1)S(1)} %get-tuple-element.304), channel_id=1, source_target_pairs={{0,8},{8,0},{16,24},{24,16},{1,9},{9,1},{17,25},{25,17},{2,10},{10... | collective-permute-start | bytes 1769480 | tf_op jit(solution)/shard_map/ppermute | solution.py:113
  33.2 7.6 %collective-permute-start.12 = (bf16[512,768]{1,0:T(8,128)(2,1)S(1)}, bf16[512,768]{1,0:T(8,128)(2,1)S(1)}, u32[]{:S(2)}, u32[]{:S(2)}) collective-permute-start(bf16[512,768]{1,0:T(8,128)(2,1)S(1)} %constant_dynamic-update-slice_fusion.9.refs_2_.refs_6_.refs_0_.refs_3_), channel_id=1, source_target_pairs={{0,1},{1,0},{2,3},{3,2},{4,5},{5,4},{6,7},{7,6},{8,9},{9,8},{10,11... | collective-permute-start | bytes 2359304 | tf_op jit(solution)/shard_map/ppermute | solution.py:96
  33.3 13.2 %collective-permute-start.11 = (bf16[224,1536]{1,0:T(8,128)(2,1)S(1)}, bf16[224,1536]{1,0:T(8,128)(2,1)S(1)}, u32[]{:S(2)}, u32[]{:S(2)}) collective-permute-start(bf16[224,1536]{1,0:T(8,128)(2,1)S(1)} %constant_dynamic-update-slice_fusion.7.rest_0_), channel_id=1, source_target_pairs={{0,2},{1,5},{2,0},{3,7},{4,6},{5,1},{6,4},{7,3},{8,10},{9,13},{10,... | collective-permute-start | bytes 2064392 | tf_op jit(solution)/shard_map/ppermute | solution.py:110
  38.9 7.9 %collective-permute-start.10 = (bf16[512,768]{1,0:T(8,128)(2,1)S(1)}, bf16[512,768]{1,0:T(8,128)(2,1)S(1)}, u32[]{:S(2)}, u32[]{:S(2)}) collective-permute-start(bf16[512,768]{1,0:T(8,128)(2,1)S(1)} %constant_dynamic-update-slice_fusion.13.refs_0_), channel_id=1, source_target_pairs={{0,1},{1,0},{2,3},{3,2},{4,5},{5,4},{6,7},{7,6},{8,9},{9,8},{10,11... | collective-permute-start | bytes 2359304 | tf_op jit(solution)/shard_map/ppermute | solution.py:96
  39.0 20.0 %collective-permute-start.18 = (bf16[512,768]{1,0:T(8,128)(2,1)S(1)}, bf16[512,768]{1,0:T(8,128)(2,1)S(1)}, u32[]{:S(2)}, u32[]{:S(2)}) collective-permute-start(bf16[512,768]{1,0:T(8,128)(2,1)S(1)} %constant_dynamic-update-slice_fusion.9.refs_2_.refs_6_.refs_0_.refs_3_), channel_id=1, source_target_pairs={{0,8},{8,0},{16,24},{24,16},{1,9},{9,1},{17,25},{25,17},{2,10},{10... | collective-permute-start | bytes 2359304 | tf_op jit(solution)/shard_map/ppermute | solution.py:113
  39.3 11.9 %collective-permute-start.14 = (bf16[224,1536]{1,0:T(8,128)(2,1)S(1)}, bf16[224,1536]{1,0:T(8,128)(2,1)S(1)}, u32[]{:S(2)}, u32[]{:S(2)}) collective-permute-start(bf16[224,1536]{1,0:T(8,128)(2,1)S(1)} %constant_dynamic-update-slice_fusion.7.rest_0_), channel_id=1, source_target_pairs={{0,4},{1,3},{2,6},{3,1},{4,0},{5,7},{6,2},{7,5},{8,12},{9,11},{10,... | collective-permute-start | bytes 2064392 | tf_op jit(solution)/shard_map/ppermute | solution.py:110
  40.8 81.8 %copy-start = (bf16[512,768]{1,0:T(8,128)(2,1)}, bf16[512,768]{1,0:T(8,128)(2,1)S(1)}, u32[]{:S(2)}) copy-start(bf16[512,768]{1,0:T(8,128)(2,1)S(1)} %collective-permute-done.12.refs_3_.refs_7_.refs_1_.refs_4_) | copy-start | bytes 2359300
  46.5 12.1 %collective-permute-start.15 = (bf16[224,1536]{1,0:T(8,128)(2,1)S(1)}, bf16[224,1536]{1,0:T(8,128)(2,1)S(1)}, u32[]{:S(2)}, u32[]{:S(2)}) collective-permute-start(bf16[224,1536]{1,0:T(8,128)(2,1)S(1)} %collective-permute-done.11.rest_1_), channel_id=1, source_target_pairs={{0,4},{1,3},{2,6},{3,1},{4,0},{5,7},{6,2},{7,5},{8,12},{9,11},{10,... | collective-permute-start | bytes 2064392 | tf_op jit(solution)/shard_map/ppermute | solution.py:110
  46.8 1.6 collective-permute-start.13
  58.9 3.7 %collective-permute-start.19 = (bf16[512,768]{1,0:T(8,128)(2,1)S(1)}, bf16[512,768]{1,0:T(8,128)(2,1)S(1)}, u32[]{:S(2)}, u32[]{:S(2)}) collective-permute-start(bf16[512,768]{1,0:T(8,128)(2,1)S(1)} %collective-permute-done.18.refs_2_.refs_8_), channel_id=1, source_target_pairs={{0,1},{1,0},{2,3},{3,2},{4,5},{5,4},{6,7},{7,6},{8,9},{9,8},{10,11... | collective-permute-start | bytes 2359304 | tf_op jit(solution)/shard_map/ppermute | solution.py:96
  59.0 15.6 %collective-permute-start.16 = (bf16[192,1536]{1,0:T(8,128)(2,1)S(1)}, bf16[192,1536]{1,0:T(8,128)(2,1)S(1)}, u32[]{:S(2)}, u32[]{:S(2)}) collective-permute-start(bf16[192,1536]{1,0:T(8,128)(2,1)S(1)} %constant_dynamic-update-slice_fusion.15.rest_0_), channel_id=1, source_target_pairs={{0,2},{1,5},{2,0},{3,7},{4,6},{5,1},{6,4},{7,3},{8,10},{9,13},{10,... | collective-permute-start | bytes 1769480 | tf_op jit(solution)/shard_map/ppermute | solution.py:110
  60.5 14.1 %collective-permute-start.17 = (bf16[192,1536]{1,0:T(8,128)(2,1)S(1)}, bf16[192,1536]{1,0:T(8,128)(2,1)S(1)}, u32[]{:S(2)}, u32[]{:S(2)}) collective-permute-start(bf16[192,1536]{1,0:T(8,128)(2,1)S(1)} %constant_dynamic-update-slice_fusion.15.rest_0_), channel_id=1, source_target_pairs={{0,4},{1,3},{2,6},{3,1},{4,0},{5,7},{6,2},{7,5},{8,12},{9,11},{10,... | collective-permute-start | bytes 1769480 | tf_op jit(solution)/shard_map/ppermute | solution.py:110
  73.1 9.7 %collective-permute-start.21 = (bf16[2,512,768]{2,1,0:T(8,128)(2,1)S(1)}, bf16[2,512,768]{2,1,0:T(8,128)(2,1)S(1)}, u32[]{:S(2)}, u32[]{:S(2)}) collective-permute-start(bf16[2,512,768]{2,1,0:T(8,128)(2,1)S(1)} %bitcast.91), channel_id=1, source_target_pairs={{0,1},{1,0},{2,3},{3,2},{4,5},{5,4},{6,7},{7,6},{8,9},{9,8},{10,11... | collective-permute-start | bytes 4718600 | tf_op jit(solution)/shard_map/ppermute | solution.py:96
  74.7 18.2 %collective-permute-start.20 = (bf16[192,1536]{1,0:T(8,128)(2,1)S(1)}, bf16[192,1536]{1,0:T(8,128)(2,1)S(1)}, u32[]{:S(2)}, u32[]{:S(2)}) collective-permute-start(bf16[192,1536]{1,0:T(8,128)(2,1)S(1)} %collective-permute-done.16.rest_1_), channel_id=1, source_target_pairs={{0,4},{1,3},{2,6},{3,1},{4,0},{5,7},{6,2},{7,5},{8,12},{9,11},{10,... | collective-permute-start | bytes 1769480 | tf_op jit(solution)/shard_map/ppermute | solution.py:110
  84.1 15.2 %collective-permute-start.23 = (bf16[3,128,768]{2,1,0:T(8,128)(2,1)S(1)}, bf16[3,128,768]{2,1,0:T(8,128)(2,1)S(1)}, u32[]{:S(2)}, u32[]{:S(2)}) collective-permute-start(bf16[3,128,768]{2,1,0:T(8,128)(2,1)S(1)} %get-tuple-element.293), channel_id=1, source_target_pairs={{0,8},{8,0},{16,24},{24,16},{1,9},{9,1},{17,25},{25,17},{2,10},{10... | collective-permute-start | bytes 1769480 | tf_op jit(solution)/shard_map/ppermute | solution.py:113
  92.5 22.5 %collective-permute-start.22 = (bf16[2,192,1536]{2,1,0:T(8,128)(2,1)S(1)}, bf16[2,192,1536]{2,1,0:T(8,128)(2,1)S(1)}, u32[]{:S(2)}, u32[]{:S(2)}) collective-permute-start(bf16[2,192,1536]{2,1,0:T(8,128)(2,1)S(1)} %get-tuple-element.224), channel_id=1, source_target_pairs={{0,4},{1,3},{2,6},{3,1},{4,0},{5,7},{6,2},{7,5},{8,12},{9,11},{10,... | collective-permute-start | bytes 3538952 | tf_op jit(solution)/shard_map/ppermute | solution.py:110
  99.2 21.2 %collective-permute-start.26 = (bf16[3,128,768]{2,1,0:T(8,128)(2,1)S(1)}, bf16[3,128,768]{2,1,0:T(8,128)(2,1)S(1)}, u32[]{:S(2)}, u32[]{:S(2)}) collective-permute-start(bf16[3,128,768]{2,1,0:T(8,128)(2,1)S(1)} %get-tuple-element.238), channel_id=1, source_target_pairs={{0,8},{8,0},{16,24},{24,16},{1,9},{9,1},{17,25},{25,17},{2,10},{10... | collective-permute-start | bytes 1769480 | tf_op jit(solution)/shard_map/ppermute | solution.py:113
  115.2 22.1 %collective-permute-start.25 = (bf16[192,1536]{1,0:T(8,128)(2,1)S(1)}, bf16[192,1536]{1,0:T(8,128)(2,1)S(1)}, u32[]{:S(2)}, u32[]{:S(2)}) collective-permute-start(bf16[192,1536]{1,0:T(8,128)(2,1)S(1)} %fusion.1), channel_id=1, source_target_pairs={{0,2},{1,5},{2,0},{3,7},{4,6},{5,1},{6,4},{7,3},{8,10},{9,13},{10,... | collective-permute-start | bytes 1769480 | tf_op jit(solution)/shard_map/ppermute | solution.py:110
  120.4 18.5 %collective-permute-start.24 = (bf16[2,192,768]{2,1,0:T(8,128)(2,1)}, bf16[2,192,768]{2,1,0:T(8,128)(2,1)}, u32[]{:S(2)}, u32[]{:S(2)}) collective-permute-start(bf16[2,192,768]{2,1,0:T(8,128)(2,1)} %get-tuple-element.236), channel_id=1, source_target_pairs={{0,4},{1,3},{2,6},{3,1},{4,0},{5,7},{6,2},{7,5},{8,12},{9,11},{10,... | collective-permute-start | bytes 1769480 | tf_op jit(solution)/shard_map/ppermute | solution.py:110
  122.1 21.1 %collective-permute-start.28 = (bf16[2,128,768]{2,1,0:T(8,128)(2,1)}, bf16[2,128,768]{2,1,0:T(8,128)(2,1)}, u32[]{:S(2)}, u32[]{:S(2)}) collective-permute-start(bf16[2,128,768]{2,1,0:T(8,128)(2,1)} %slice.180), channel_id=1, source_target_pairs={{0,8},{8,0},{16,24},{24,16},{1,9},{9,1},{17,25},{25,17},{2,10},{10... | collective-permute-start | bytes 1179656 | tf_op jit(solution)/shard_map/ppermute | solution.py:113
  138.9 4.3 %collective-permute-start.29 = (bf16[96,1536]{1,0:T(8,128)(2,1)}, bf16[96,1536]{1,0:T(8,128)(2,1)}, u32[]{:S(2)}, u32[]{:S(2)}) collective-permute-start(bf16[96,1536]{1,0:T(8,128)(2,1)} %get-tuple-element.299), channel_id=1, source_target_pairs={{0,1},{1,0},{2,3},{3,2},{4,5},{5,4},{6,7},{7,6},{8,9},{9,8},{10,11... | collective-permute-start | bytes 884744 | tf_op jit(solution)/shard_map/ppermute | solution.py:96
  140.0 21.2 %collective-permute-start.27 = (bf16[192,768]{1,0:T(8,128)(2,1)S(1)}, bf16[192,768]{1,0:T(8,128)(2,1)S(1)}, u32[]{:S(2)}, u32[]{:S(2)}) collective-permute-start(bf16[192,768]{1,0:T(8,128)(2,1)S(1)} %fusion.3), channel_id=1, source_target_pairs={{0,2},{1,5},{2,0},{3,7},{4,6},{5,1},{6,4},{7,3},{8,10},{9,13},{10,... | collective-permute-start | bytes 884744 | tf_op jit(solution)/shard_map/ppermute | solution.py:110
  140.6 29.0 %collective-permute-start.31 = (bf16[96,1536]{1,0:T(8,128)(2,1)}, bf16[96,1536]{1,0:T(8,128)(2,1)S(1)}, u32[]{:S(2)}, u32[]{:S(2)}) collective-permute-start(bf16[96,1536]{1,0:T(8,128)(2,1)} %get-tuple-element.298), channel_id=1, source_target_pairs={{0,16},{8,24},{16,0},{24,8},{1,17},{9,25},{17,1},{25,9},{2,18},{10... | collective-permute-start | bytes 884744 | tf_op jit(solution)/shard_map/ppermute | solution.py:113
  161.3 17.2 %collective-permute-start.34 = (bf16[2,512,768]{2,1,0:T(8,128)(2,1)S(1)}, bf16[2,512,768]{2,1,0:T(8,128)(2,1)S(1)}, u32[]{:S(2)}, u32[]{:S(2)}) collective-permute-start(bf16[2,512,768]{2,1,0:T(8,128)(2,1)S(1)} %bitcast.90), channel_id=1, source_target_pairs={{0,1},{1,0},{2,3},{3,2},{4,5},{5,4},{6,7},{7,6},{8,9},{9,8},{10,11... | collective-permute-start | bytes 4718600 | tf_op jit(solution)/shard_map/ppermute | solution.py:96
  162.5 5.4 %collective-permute-start.32 = (bf16[96,768]{1,0:T(8,128)(2,1)S(1)}, bf16[96,768]{1,0:T(8,128)(2,1)S(1)}, u32[]{:S(2)}, u32[]{:S(2)}) collective-permute-start(bf16[96,768]{1,0:T(8,128)(2,1)S(1)} %get-tuple-element.303), channel_id=1, source_target_pairs={{0,1},{1,0},{2,3},{3,2},{4,5},{5,4},{6,7},{7,6},{8,9},{9,8},{10,11... | collective-permute-start | bytes 442376 | tf_op jit(solution)/shard_map/ppermute | solution.py:96
  165.7 11.0 %collective-permute-start.30 = (bf16[2,224,768]{2,1,0:T(8,128)(2,1)S(1)}, bf16[2,224,768]{2,1,0:T(8,128)(2,1)S(1)}, u32[]{:S(2)}, u32[]{:S(2)}) collective-permute-start(bf16[2,224,768]{2,1,0:T(8,128)(2,1)S(1)} %get-tuple-element.257), channel_id=1, source_target_pairs={{0,4},{1,3},{2,6},{3,1},{4,0},{5,7},{6,2},{7,5},{8,12},{9,11},{10,... | collective-permute-start | bytes 2064392 | tf_op jit(solution)/shard_map/ppermute | solution.py:110
  168.0 10.3 %collective-permute-start.35 = (bf16[2,96,384]{2,1,0:T(8,128)(2,1)S(1)}, bf16[2,96,384]{2,1,0:T(8,128)(2,1)S(1)}, u32[]{:S(2)}, u32[]{:S(2)}) collective-permute-start(bf16[2,96,384]{2,1,0:T(8,128)(2,1)S(1)} %broadcast_select_fusion.1), channel_id=1, source_target_pairs={{0,8},{8,0},{16,24},{24,16},{1,9},{9,1},{17,25},{25,17},{2,10},{10... | collective-permute-start | bytes 442376 | tf_op jit(solution)/shard_map/ppermute | solution.py:113
  176.8 7.3 %collective-permute-start.33 = (bf16[224,768]{1,0:T(8,128)(2,1)S(1)}, bf16[224,768]{1,0:T(8,128)(2,1)S(1)}, u32[]{:S(2)}, u32[]{:S(2)}) collective-permute-start(bf16[224,768]{1,0:T(8,128)(2,1)S(1)} %fusion.2), channel_id=1, source_target_pairs={{0,2},{1,5},{2,0},{3,7},{4,6},{5,1},{6,4},{7,3},{8,10},{9,13},{10,... | collective-permute-start | bytes 1032200 | tf_op jit(solution)/shard_map/ppermute | solution.py:110
  179.3 13.2 %collective-permute-start.39 = (bf16[2,2,128,768]{3,2,1,0:T(8,128)(2,1)S(1)}, bf16[2,2,128,768]{3,2,1,0:T(8,128)(2,1)S(1)}, u32[]{:S(2)}, u32[]{:S(2)}) collective-permute-start(bf16[2,2,128,768]{3,2,1,0:T(8,128)(2,1)S(1)} %pad_maximum_fusion.1), channel_id=1, source_target_pairs={{0,2},{1,5},{2,0},{3,7},{4,6},{5,1},{6,4},{7,3},{8,10},{9,13},{10,... | collective-permute-start | bytes 2359304 | tf_op jit(solution)/shard_map/ppermute | solution.py:110
  184.3 1.5 collective-permute-start.36
  192.7 12.1 %collective-permute-start.40 = (bf16[2,2,128,768]{3,2,1,0:T(8,128)(2,1)S(1)}, bf16[2,2,128,768]{3,2,1,0:T(8,128)(2,1)S(1)}, u32[]{:S(2)}, u32[]{:S(2)}) collective-permute-start(bf16[2,2,128,768]{3,2,1,0:T(8,128)(2,1)S(1)} %pad_maximum_fusion.2), channel_id=1, source_target_pairs={{0,4},{1,3},{2,6},{3,1},{4,0},{5,7},{6,2},{7,5},{8,12},{9,11},{10,... | collective-permute-start | bytes 2359304 | tf_op jit(solution)/shard_map/ppermute | solution.py:110
  193.8 17.8 %collective-permute-start.38 = (bf16[96,1536]{1,0:T(8,128)(2,1)}, bf16[96,1536]{1,0:T(8,128)(2,1)S(1)}, u32[]{:S(2)}, u32[]{:S(2)}) collective-permute-start(bf16[96,1536]{1,0:T(8,128)(2,1)} %collective-permute-done.29), channel_id=1, source_target_pairs={{0,16},{8,24},{16,0},{24,8},{1,17},{9,25},{17,1},{25,9},{2,18},{10... | collective-permute-start | bytes 884744 | tf_op jit(solution)/shard_map/ppermute | solution.py:113
  194.1 37.7 %collective-permute-start.46 = (bf16[96,1536]{1,0:T(8,128)(2,1)S(1)}, bf16[96,1536]{1,0:T(8,128)(2,1)S(1)}, u32[]{:S(2)}, u32[]{:S(2)}) collective-permute-start(bf16[96,1536]{1,0:T(8,128)(2,1)S(1)} %add_convert_fusion.9.refs_0_), channel_id=1, source_target_pairs={{0,8},{8,0},{16,24},{24,16},{1,9},{9,1},{17,25},{25,17},{2,10},{10... | collective-permute-start | bytes 884744 | tf_op jit(solution)/shard_map/ppermute | solution.py:113
  195.7 24.1 %collective-permute-start.42 = (bf16[2,96,384]{2,1,0:T(8,128)(2,1)S(1)}, bf16[2,96,384]{2,1,0:T(8,128)(2,1)S(1)}, u32[]{:S(2)}, u32[]{:S(2)}) collective-permute-start(bf16[2,96,384]{2,1,0:T(8,128)(2,1)S(1)} %add_convert_fusion.15), channel_id=1, source_target_pairs={{0,16},{8,24},{16,0},{24,8},{1,17},{9,25},{17,1},{25,9},{2,18},{10... | collective-permute-start | bytes 442376 | tf_op jit(solution)/shard_map/ppermute | solution.py:113
  198.3 17.1 %collective-permute-start.37 = (bf16[2,112,384]{2,1,0:T(8,128)(2,1)S(1)}, bf16[2,112,384]{2,1,0:T(8,128)(2,1)S(1)}, u32[]{:S(2)}, u32[]{:S(2)}) collective-permute-start(bf16[2,112,384]{2,1,0:T(8,128)(2,1)S(1)} %broadcast_select_fusion), channel_id=1, source_target_pairs={{0,8},{8,0},{16,24},{24,16},{1,9},{9,1},{17,25},{25,17},{2,10},{10... | collective-permute-start | bytes 516104 | tf_op jit(solution)/shard_map/ppermute | solution.py:113
  212.6 19.2 %collective-permute-start.45 = (bf16[96,1536]{1,0:T(8,128)(2,1)S(1)}, bf16[96,1536]{1,0:T(8,128)(2,1)S(1)}, u32[]{:S(2)}, u32[]{:S(2)}) collective-permute-start(bf16[96,1536]{1,0:T(8,128)(2,1)S(1)} %add_convert_fusion.8.refs_1_), channel_id=1, source_target_pairs={{0,8},{8,0},{16,24},{24,16},{1,9},{9,1},{17,25},{25,17},{2,10},{10... | collective-permute-start | bytes 884744 | tf_op jit(solution)/shard_map/ppermute | solution.py:113
  215.4 9.3 %collective-permute-start.41 = (bf16[2,112,384]{2,1,0:T(8,128)(2,1)S(1)}, bf16[2,112,384]{2,1,0:T(8,128)(2,1)S(1)}, u32[]{:S(2)}, u32[]{:S(2)}) collective-permute-start(bf16[2,112,384]{2,1,0:T(8,128)(2,1)S(1)} %add_convert_fusion.13), channel_id=1, source_target_pairs={{0,16},{8,24},{16,0},{24,8},{1,17},{9,25},{17,1},{25,9},{2,18},{10... | collective-permute-start | bytes 516104 | tf_op jit(solution)/shard_map/ppermute | solution.py:113
  219.9 13.5 %collective-permute-start.44 = (bf16[2,96,384]{2,1,0:T(8,128)(2,1)S(1)}, bf16[2,96,384]{2,1,0:T(8,128)(2,1)S(1)}, u32[]{:S(2)}, u32[]{:S(2)}) collective-permute-start(bf16[2,96,384]{2,1,0:T(8,128)(2,1)S(1)} %add_convert_fusion.14.refs_0_), channel_id=1, source_target_pairs={{0,8},{8,0},{16,24},{24,16},{1,9},{9,1},{17,25},{25,17},{2,10},{10... | collective-permute-start | bytes 442376 | tf_op jit(solution)/shard_map/ppermute | solution.py:113
  224.8 8.6 %collective-permute-start.43 = (bf16[2,112,384]{2,1,0:T(8,128)(2,1)S(1)}, bf16[2,112,384]{2,1,0:T(8,128)(2,1)S(1)}, u32[]{:S(2)}, u32[]{:S(2)}) collective-permute-start(bf16[2,112,384]{2,1,0:T(8,128)(2,1)S(1)} %add_convert_fusion.12.refs_2_), channel_id=1, source_target_pairs={{0,8},{8,0},{16,24},{24,16},{1,9},{9,1},{17,25},{25,17},{2,10},{10... | collective-permute-start | bytes 516104 | tf_op jit(solution)/shard_map/ppermute | solution.py:113
  (43 other events, 257.0 us)

commit v3 on v2

--- a/solution.py
+++ b/solution.py
@@ -12,30 +12,25 @@
 ROT = 16
 TILE = 256
 VEC = 16
-HEADS = 3
-
-COST = {
-    "split_input": 1.0,
-    "split_cotangent": 1.0,
-    "split_weights": 1.0,
+COSTS = {
     "tables_second": 0.1,
     "middle_1": 0.1,
     "back_1": 0.1,
-    "middle_0": 10.0,
     "second_grads": 0.1,
+    "back_0": 2,
+    "vector_grads": 10,
+    "second_end": 0.3,
+    "pause_7": 0.3,
+    "pause_8": 0.3,
+    "pause_9": 0.3,
+    "pause_10": 0.3,
+    "pause_11": 0.3,
+    "pause_12": 0.3,
+    "pause_13": 0.3,
     "tables_first": 0.1,
     "front": 0.1,
-    "attention_0": 10.0,
-    "first_grads_0": 0.1,
-    "attention_1": 10.0,
-    "back_0": 10.0,
-    "first_grads_1": 0.1,
-    "finish_tokens": 1.0,
-    "second_end": 1.0,
-    "first_end": 1.0,
 }
-FLOPS = 1.15e9
-BYTES = 3.6e6
+DEFAULT = 20
 
 EPS = 1e-05
 NEG = -1e30
@@ -64,7 +59,8 @@
         self.pair = 2 if reps % 2 == 0 and H % (2 * self.low_count) == 0 else 1
         self.parts = self.pair * self.low_count
         self.line = Line()
-        self.groups = H // self.low_count // HEADS
+        self.heads = 2 if H // self.low_count % 2 == 0 else 3
+        self.groups = H // self.low_count // self.heads
         self.masks = []
         while 2 ** len(self.masks) < seqs:
             self.masks.append(2 ** len(self.masks))
@@ -121,9 +117,15 @@
     return pl.BlockSpec(shape, lambda *_: (0,) * len(shape))
 
 
+def pause_kernel(source, out):
+    out[...] = source[...] + 1.0
+
+
 class Line:
     def __init__(self):
         self.ahead = []
+        self.count = jnp.zeros((8, 128), F32)
+        self.pauses = 0
 
     def take(self, *arrays):
         found = lax.optimization_barrier((*arrays, *self.ahead))[: len(arrays)]
@@ -132,6 +134,13 @@
 
     def hold(self, *arrays):
         self.ahead.extend(arrays)
+
+    def pause(self):
+        small = jax.ShapeDtypeStruct((8, 128), F32)
+        block = whole(small.shape)
+        self.pauses += 1
+        name = f"pause_{self.pauses}"
+        self.count = self.call(pause_kernel, name, (1,), [block], block, small, [], [self.count], 4)
 
     def call(self, kernel, name, grid, in_specs, out_specs, out_shape, scratch, args, vmem=40):
         args = list(args)
@@ -146,7 +155,8 @@
             scratch_shapes=scratch,
             compiler_params=pltpu.CompilerParams(vmem_limit_bytes=vmem * 2**20),
             cost_estimate=pl.CostEstimate(
-                flops=int(COST[name] * FLOPS), bytes_accessed=int(COST[name] * BYTES),
+                flops=(cost := int(COSTS.get(name, DEFAULT) * 1.15e9)),
+                bytes_accessed=int(cost // 320),
                 transcendentals=0,
             ),
             name=name,
@@ -180,7 +190,7 @@
     rows = w_qkv.shape[0]
     parts, low_count = place.parts, place.low_count
     width = w_out.shape[1]
-    step = HEADS * HD
+    step = place.heads * HD
     hidden = w_up.shape[1] // parts
     firsts, seconds = outs[:low_count], outs[low_count:]
     for k in range(low_count):
@@ -249,7 +259,7 @@
     seqs, low_count, parts = place.seqs, place.low_count, place.parts
     block = rows + VEC
     width = w_out.shape[0]
-    step = HEADS * HD
+    step = place.heads * HD
     low = place.low()
     for s in range(seqs):
         owner = place.owner(s)
@@ -291,7 +301,7 @@
     shapes = [
         jax.ShapeDtypeStruct((width, slots[0].shape[1]), BF16),
         jax.ShapeDtypeStruct((8, width), F32),
-        jax.ShapeDtypeStruct((8, 3 * HEADS * HD), F32),
+        jax.ShapeDtypeStruct((8, 3 * place.heads * HD), F32),
         jax.ShapeDtypeStruct((place.shards, VEC, slots[0].shape[1]), F32),
     ]
     return place.line.call(
@@ -303,7 +313,7 @@
         shapes,
         [],
         slots,
-        vmem=16,
+        vmem=40,
     )
 
 
@@ -390,7 +400,7 @@
 def front_kernel(place, steps, *refs):
     tokens, refs = refs[: place.low_count], refs[place.low_count :]
     weight, vec, bias, cosine, sine, one_out, *outs = refs
-    step = HEADS * HD
+    step = place.heads * HD
     one = (norm(piece_now(tokens, steps)) * vec[0:1, :] + vec[1:2, :]).astype(BF16)
     one_out[0] = one
     copies = 2 * step // 128
@@ -409,7 +419,7 @@
 def front(place, tokens, weight, vec, bias, cosine, sine):
     groups = len(tokens)
     count, width = tokens[0].shape
-    step = HEADS * HD
+    step = place.heads * HD
     split = 2
     lines = count // split
     by_step = lambda cols: pl.BlockSpec((1, lines, cols), lambda g: (g // split, g % split, 0))
@@ -424,7 +434,7 @@
         [shaped(width)] + [shaped(step)] * (3 * place.groups),
         [],
         [*tokens, weight, vec, bias, cosine, sine],
-        vmem=24,
+        vmem=20,
     )
     return outs[0], [outs[1 + 3 * h : 4 + 3 * h] for h in range(place.groups)]
 
@@ -479,7 +489,7 @@
         [jax.ShapeDtypeStruct((groups, count, width), BF16)] * 4 + [jax.ShapeDtypeStruct((8, width), F32)],
         [],
         [*tokens, *grads, vec, weight],
-        vmem=24,
+        vmem=20,
     )
 
 
@@ -520,31 +530,48 @@
         keys_turned = keys.astype(F32).T.astype(BF16)
         values_turned = values.astype(F32).T.astype(BF16)
         for i in range(length // TILE):
-            seen = (i + 1) * TILE
-            here = slice(i * TILE, seen)
+            here = slice(i * TILE, (i + 1) * TILE)
             query = qs[h, here, :]
             grad = gs[h, here, :]
             first = first_in[:, here]
-            raw = dot(keys[:seen], query, NT) * 0.125
-            key_index = lax.broadcasted_iota(I32, (seen, TILE), 0)
-            query_index = i * TILE + lax.broadcasted_iota(I32, (seen, TILE), 1)
-            raw = jnp.where((key_index >= first) & (key_index <= query_index), raw, NEG)
-            weights = jnp.exp(raw - jnp.max(raw, axis=0, keepdims=True))
-            probs = weights * (1.0 / jnp.sum(weights, axis=0, keepdims=True))
-            grad_probs = dot(values[:seen], grad, NT)
-            carried = jnp.sum(probs * grad_probs, axis=0, keepdims=True)
-            grad_scores = (probs * (grad_probs - carried)).astype(BF16)
-            low = probs.astype(BF16)
-            o_turned[h, :, here] = dot(values_turned[:, :seen], low, NN)
-            gq_turned[h, :, here] = dot(keys_turned[:, :seen], grad_scores, NN)
-            gk_part = dot(grad_scores, query, NN)
-            gv_part = dot(low, grad, NN)
-            if i > 0:
-                old = slice(0, i * TILE)
-                gk_sum[h, old, :] += gk_part[: i * TILE]
-                gv_sum[h, old, :] += gv_part[: i * TILE]
-            gk_sum[h, here, :] = gk_part[i * TILE :]
-            gv_sum[h, here, :] = gv_part[i * TILE :]
+            tiles = [slice(j * TILE, (j + 1) * TILE) for j in range(i + 1)]
+            scores, grads = [], []
+            for j, tile in enumerate(tiles):
+                raw = dot(keys[tile], query, NT) * (0.125 * 1.4426950408889634)
+                key_index = j * TILE + lax.broadcasted_iota(I32, (TILE, TILE), 0)
+                seen = key_index >= first
+                if j == i:
+                    query_index = i * TILE + lax.broadcasted_iota(I32, (TILE, TILE), 1)
+                    seen = seen & (key_index <= query_index)
+                scores.append(jnp.where(seen, raw, NEG))
+            top = functools.reduce(
+                jnp.maximum, [jnp.max(raw, axis=0, keepdims=True) for raw in scores]
+            )
+            weights = [jnp.exp2(raw - top) for raw in scores]
+            share = 1.0 / sum(jnp.sum(w, axis=0, keepdims=True) for w in weights)
+            grads = [dot(values[tile], grad, NT) for tile in tiles]
+            carried = share * sum(
+                jnp.sum(w * g, axis=0, keepdims=True) for w, g in zip(weights, grads)
+            )
+            out, gq = None, None
+            for j, tile in enumerate(tiles):
+                probs = weights[j] * share
+                low = probs.astype(BF16)
+                grad_scores = (probs * (grads[j] - carried)).astype(BF16)
+                out_part = dot(values_turned[:, tile], low, NN)
+                gq_part = dot(keys_turned[:, tile], grad_scores, NN)
+                gk_part = dot(grad_scores, query, NN)
+                gv_part = dot(low, grad, NN)
+                out = out_part if j == 0 else out + out_part
+                gq = gq_part if j == 0 else gq + gq_part
+                if j < i:
+                    gk_sum[h, tile, :] += gk_part
+                    gv_sum[h, tile, :] += gv_part
+                else:
+                    gk_sum[h, tile, :] = gk_part
+                    gv_sum[h, tile, :] = gv_part
+            o_turned[h, :, here] = out
+            gq_turned[h, :, here] = gq
         return carry
 
     lax.fori_loop(0, heads, one_head, 0)
@@ -593,6 +620,7 @@
         + [pltpu.VMEM((heads, HD, length), F32)] * 2
         + [pltpu.VMEM((heads, length, HD), F32)] * 2,
         args,
+        vmem=16 * (length // 1024),
     )
 
 
@@ -616,7 +644,7 @@
     sums[3:4, :] += jnp.sum(two, axis=0, keepdims=True)
     if groups:
         first = refs[5 + 2 * groups]
-        cols = HEADS * HD
+        cols = place.heads * HD
         one = None
         for h in range(groups):
             term = dot(grad_qkv[h][0], first[:, 3 * cols * h : 3 * cols * (h + 1)], NT)
@@ -669,7 +697,7 @@
         ],
         [],
         args + fixed,
-        vmem=32,
+        vmem=24,
     )
 
 
@@ -728,81 +756,100 @@
         [jax.ShapeDtypeStruct(half, BF16)] * 2,
         [pltpu.VMEM((width, width), F32), pltpu.VMEM((2 * half[0],) + half[1:], BF16)],
         flat,
-    )
-
-
-def first_grads_kernel(place, rows, last, *refs):
-    one, grad_qkv, attended = refs[:3]
-    cot, refs = refs[3 : 3 + place.low_count], (None,) * 4 + refs[3 + place.low_count :]
-    keep, send, total, turned_rows = refs[-4:]
-    seqs, low_count, parts = place.seqs, place.low_count, place.parts
-    width = one.shape[1]
-    step = HEADS * HD
-    block = rows + (VEC if last else 0)
-    half = seqs // 2
-    total[:, : 3 * step] = dot(one[...], grad_qkv[...], TN)
-    total[:, 3 * step :] = product(cot, [attended])
-    store_rows(place, rows, block, total, turned_rows, slice(0, width))
-    if last:
-        at_qkv = 4 + place.groups
-        sums_qkv, sums_back, sums_middle = (
-            refs[4:at_qkv],
-            refs[at_qkv : at_qkv + place.pair],
-            refs[at_qkv + place.pair : -4],
-        )
-        back = sum(s[...] for s in sums_back)
-        up = sum(s[0:1, :] for s in sums_middle)
-        grad = sums_middle[0][1:2, :] * (1.0 / low_count)
-        zero = jnp.zeros((1, step), F32)
-        all_qkv = jnp.concatenate(
-            [
-                jnp.where(place.low() == k, sums_qkv[h][0:1, g * step : (g + 1) * step], zero)
-                for g in range(3)
-                for k in range(low_count)
-                for h in range(place.groups)
-            ],
-            axis=1,
-        )
-        all_up = jnp.concatenate(
-            [jnp.where(place.part() == k, up, 0.0) for k in range(parts)], axis=1
-        )
-        lines = [(back[r : r + 1], rows) for r in range(4)]
-        lines += [(all_qkv, 3 * rows), (grad, rows), (all_up, 4 * rows)]
-        for i in range(seqs):
-            for l in range(low_count):
-                n = i * low_count + l
-                made = [
-                    jnp.concatenate(
-                        [v[:, n * size : (n + 1) * size], jnp.zeros((1, width - size), F32)], axis=1
-                    )
-                    for v, size in lines
-                ]
-                made.append(jnp.zeros((VEC - len(made), width), F32))
-                made = jnp.concatenate(made, axis=0).astype(BF16)
-                for s in range(seqs):
-                    for o in range(low_count):
-
-                        @pl.when((place.owner(s) == i) & ((place.low() ^ o) == l))
-                        def _():
-                            turned_rows[s, o * block + rows : (o + 1) * block, :] = made
-
-    keep[...] = turned_rows[:half]
-    send[...] = turned_rows[half:]
-
-
-def first_grads(place, group, rows, one, cot, grad_qkv, attended, sums):
+        vmem=20,
+    )
+
+
+def first_grads_kernel(place, rows, count, one, *refs):
+    grad_qkv, attended, refs = refs[:count], refs[count : 2 * count], refs[2 * count :]
+    cot, (keep, send, total, ordered) = refs[:-4], refs[-4:]
+    half = place.seqs // 2
+    step = place.heads * HD
+    for h in range(count):
+        total[:, : 3 * step] = dot(one[...], grad_qkv[h][...], TN)
+        total[:, 3 * step :] = product(cot, [attended[h]])
+        store_rows(place, rows, rows, total, ordered, slice(4 * step * h, 4 * step * (h + 1)))
+    keep[...] = ordered[:half]
+    send[...] = ordered[half:]
+
+
+def first_grads(place, number, rows, one, cot, grad_qkv, attended):
     width = one.shape[2]
-    args = [v.reshape(-1, v.shape[2]) for v in (one, grad_qkv, attended)] + list(cot) + list(sums)
-    half = (place.seqs // 2, place.low_count * (rows + (VEC if sums else 0)), width)
+    step = place.heads * HD
+    count = len(attended)
+    args = [v.reshape(-1, v.shape[2]) for v in (one, *grad_qkv, *attended)] + list(cot)
+    half = (place.seqs // 2, place.low_count * rows, 4 * step * count)
     return place.line.call(
-        functools.partial(first_grads_kernel, place, rows, bool(sums)),
-        f"first_grads_{group}",
+        functools.partial(first_grads_kernel, place, rows, count),
+        f"first_grads_{number}",
         (1,),
         [whole(v.shape) for v in args],
         [whole(half)] * 2,
         [jax.ShapeDtypeStruct(half, BF16)] * 2,
-        [pltpu.VMEM((width, width), F32), pltpu.VMEM((2 * half[0],) + half[1:], BF16)],
+        [pltpu.VMEM((width, 4 * step), F32), pltpu.VMEM((2 * half[0],) + half[1:], BF16)],
         args,
+        vmem=16,
+    )
+
+
+def vectors_kernel(place, rows, *refs):
+    sums_qkv = refs[: place.groups]
+    sums_back = refs[place.groups : place.groups + place.pair]
+    sums_middle = refs[place.groups + place.pair : -4]
+    keep, send, lines_kept, ordered = refs[-4:]
+    seqs, low_count, parts = place.seqs, place.low_count, place.parts
+    width = keep.shape[2]
+    step = place.heads * HD
+    half = seqs // 2
+    back = sum(s[...] for s in sums_back)
+    up = sum(s[0:1, :] for s in sums_middle)
+    grad = sums_middle[0][1:2, :] * (1.0 / low_count)
+    zero = jnp.zeros((1, step), F32)
+    all_qkv = jnp.concatenate(
+        [
+            jnp.where(place.low() == k, sums_qkv[h][0:1, g * step : (g + 1) * step], zero)
+            for g in range(3)
+            for k in range(low_count)
+            for h in range(place.groups)
+        ],
+        axis=1,
+    )
+    all_up = jnp.concatenate([jnp.where(place.part() == k, up, 0.0) for k in range(parts)], axis=1)
+    lines = [(back[r : r + 1], rows) for r in range(4)]
+    lines += [(all_qkv, 3 * rows), (grad, rows), (all_up, 4 * rows)]
+    for n in range(place.shards):
+        made = [
+            jnp.concatenate(
+                [v[:, n * size : (n + 1) * size], jnp.zeros((1, width - size), F32)], axis=1
+            )
+            for v, size in lines
+        ]
+        made.append(jnp.zeros((VEC - len(made), width), F32))
+        lines_kept[n] = jnp.concatenate(made, axis=0)
+    for s in range(seqs):
+        for o in range(low_count):
+            n = place.owner(s) * low_count + (place.low() ^ o)
+            ordered[s, o * VEC : (o + 1) * VEC, :] = lines_kept[n].astype(BF16)
+    keep[...] = ordered[:half]
+    send[...] = ordered[half:]
+
+
+def vector_grads(place, rows, width, sums_qkv, sums_back, sums_middle):
+    half = (place.seqs // 2, place.low_count * VEC, width)
+    args = [*sums_qkv, *sums_back, *sums_middle]
+    return place.line.call(
+        functools.partial(vectors_kernel, place, rows),
+        "vector_grads",
+        (1,),
+        [whole(v.shape) for v in args],
+        [whole(half)] * 2,
+        [jax.ShapeDtypeStruct(half, BF16)] * 2,
+        [
+            pltpu.VMEM((place.shards, VEC, width), F32),
+            pltpu.VMEM((2 * half[0],) + half[1:], BF16),
+        ],
+        args,
+        vmem=16,
     )
 
 
@@ -838,52 +885,52 @@
     )
 
 
-def first_end_kernel(place, rows, *refs):
-    w_qkv, w_out, lines = refs[-3:]
+def first_end_kernel(place, rows, counts, *refs):
+    found, refs = refs[: 2 * len(counts)], refs[2 * len(counts) + 1 :]
+    w_qkv, w_out, vectors = refs[0], refs[1], refs[2:]
     low_count, groups = place.low_count, place.groups
     width = w_out.shape[1]
-    step = HEADS * HD
-    found = refs[:-3]
+    step = place.heads * HD
     even = (lax.axis_index("rep") % 2) == 0
-    count = len(found) // groups
     total = None
-    for h in range(groups):
-        ours = found[h * count : (h + 1) * count]
+    first = 0
+    for i, count in enumerate(counts):
         for o in range(low_count):
-            if count == 1:
-                piece = ours[0][o].astype(F32)
-            else:
-                mine, other = ours[0][o].astype(F32), ours[1][o].astype(F32)
-                piece = jnp.concatenate(
-                    [jnp.where(even, mine, other), jnp.where(even, other, mine)], axis=1
-                )
+            mine, other = found[2 * i][o].astype(F32), found[2 * i + 1][o].astype(F32)
+            piece = jnp.concatenate(
+                [jnp.where(even, mine, other), jnp.where(even, other, mine)], axis=1
+            )
             for k in range(low_count):
 
                 @pl.when(place.low() == k)
                 def _():
-                    begin = ((k ^ o) * groups + h) * step
-                    for g in range(3):
-                        to = g * width + begin
-                        w_qkv[:, to : to + step] = piece[:rows, g * step : (g + 1) * step]
-                    w_out[:, begin : begin + step] = piece[:rows, 3 * step :]
-
-            if h == groups - 1:
+                    for h in range(count):
+                        begin = ((k ^ o) * groups + first + h) * step
+                        for g in range(3):
+                            to = g * width + begin
+                            part = (4 * h + g) * step
+                            w_qkv[:, to : to + step] = piece[:rows, part : part + step]
+                        part = (4 * h + 3) * step
+                        w_out[:, begin : begin + step] = piece[:rows, part : part + step]
+
+            if i == len(counts) - 1:
                 total = piece[rows:] if total is None else total + piece[rows:]
-    lines[...] = total
-
-
-def first_end(place, rows, width, pieces):
+        first += count
+    for r, out in enumerate(vectors):
+        out[...] = total[r : r + 1, : out.shape[1]]
+
+
+def first_end(place, rows, width, counts, pieces):
+    shapes = [(rows, 3 * width), (rows, width)]
+    shapes += [(1, n * rows) for n in (1, 1, 1, 1, 3, 1, 4)]
+    pieces = pieces + [place.line.count]
     return place.line.call(
-        functools.partial(first_end_kernel, place, rows),
+        functools.partial(first_end_kernel, place, rows, counts),
         "first_end",
         (1,),
         [whole(p.shape) for p in pieces],
-        [whole((rows, 3 * width)), whole((rows, width)), whole((VEC, width))],
-        [
-            jax.ShapeDtypeStruct((rows, 3 * width), F32),
-            jax.ShapeDtypeStruct((rows, width), F32),
-            jax.ShapeDtypeStruct((VEC, width), F32),
-        ],
+        [whole(v) for v in shapes],
+        [jax.ShapeDtypeStruct(v, F32) for v in shapes],
         [],
         pieces,
     )
@@ -1039,16 +1086,17 @@
         rest = jnp.concatenate(coming[: seqs - 1], axis=0)
         line.hold(rest)
         later_x = place.swap_rep(rest, 1)
+    sent = lax.optimization_barrier((*split_c[1:], *coming))[: seqs - 1]
+    coming_c = [place.swap_slot(v, j) for v, j in zip(sent, range(1, seqs))]
+    line.hold(block_x)
     coming_second = line.take(*coming_second)
     block_second = jnp.concatenate([seconds[0], *coming_second], axis=0)
-    line.hold(block_x, block_second)
-    sent = line.take(*split_c[1:])
-    coming_c = [place.swap_slot(v, j) for v, j in zip(sent, range(1, seqs))]
+    line.hold(block_second)
     tokens[0].extend(line.take(*coming_x))
     coming_c = line.take(*coming_c)
+    second = Gather(line.take(block_second)[0])
     block_c = jnp.concatenate([split_c[0], *coming_c], axis=0)
     line.hold(block_c)
-    second = Gather(line.take(block_second)[0])
     grads.append([block_c])
     coming_c = to_low(block_c)
     if pair == 2:
@@ -1083,86 +1131,104 @@
         keep, send, sums_back[z] = back(
             place, z, normed[z], hidden[z], grad_up[z], attended, grad_qkv, vec, w_second, w_first
         )
-        return keep, [place.swap_low(send[o - 1], o) for o in lows]
+        return keep, [place.swap_low(send[o - 1][r], o) for o in lows for r in range(2)]
 
     def low_sum(keep, coming):
-        total = keep.astype(F32)
-        for v in line.take(*coming):
-            total = total + v.astype(F32)
-        return total
+        coming = line.take(*coming)
+        return jnp.stack(
+            [sum([v.astype(F32) for v in coming[r::2]], keep[r].astype(F32)) for r in range(2)]
+        )
 
     if pair == 2:
         grads.append([other_c, *line.take(*coming_c)])
         forward(1)
         keep, coming = backward(1, [], [], None)
     first.step(more=1)
+    out_pieces, out_found, out_coming = [], [], []
+
+    def next_piece():
+        if out_coming:
+            out_found.append(line.take(out_coming.pop())[0])
+        if out_pieces:
+            out_coming.append(place.swap_rep(after(out_pieces.pop(0), *line.ahead), 1))
+
+    if pair == 2:
+        line.pause()
+        coming = line.take(*coming)
+        sums = [
+            sum(v.astype(F32) for v in [keep[r]] + list(coming[r::2])).astype(BF16) for r in range(2)
+        ]
+        cut = 3 * sums[0].shape[0] // 4
+        out_pieces += [sums[0][:cut], jnp.concatenate([sums[0][cut:], sums[1]])]
+        line.hold(*out_pieces)
+        next_piece()
     forward(0)
-    out_pieces, out_found = [], []
-
-    def next_piece():
-        if out_pieces:
-            out_found.append(line.take(out_coming.pop())[0])
-            out_pieces.pop(0)
-        if out_pieces:
-            out_coming.append(place.swap_rep(after(out_pieces[0], out_found[-1]), 1))
-
-    out_coming = []
-    if pair == 2:
-        out_other = low_sum(keep, coming).astype(BF16).reshape(2 * seqs, span, width)
-        cuts = [2 * seqs * k // 8 for k in (0, 3, 6, 8)]
-        out_pieces = [out_other[a:b] for a, b in zip(cuts, cuts[1:])]
-        line.hold(*out_pieces)
-        out_coming.append(place.swap_rep(out_pieces[0], 1))
     second_sums = Scatter(*second_grads(place, rows, two, grad_up, grads, hidden))
 
+    next_piece()
     first.step()
     w_first, seen, cosine, sine = first_tables(place, first.slots, lines_kept, rows, width, span)
     one, heads = front(place, tokens[0], w_first, vec, bias, cosine, sine)
-    attended, grad_qkv, sums_qkv, first_sums = [[None] * place.groups for _ in range(4)]
+    attended, grad_qkv, sums_qkv = [[None] * place.groups for _ in range(3)]
     cot = grads[0]
-    for h in range(place.groups):
-        next_piece()
+
+    def attend(h):
         attended[h], grad_qkv[h], sums_qkv[h] = attention(
             place, h, span, *heads[h], cot, w_first, seen, cosine, sine
         )
-        second_sums.step()
-        if h > 0:
-            first_sums[h - 1].step()
-        if h < place.groups - 1:
-            first_sums[h] = Scatter(
-                *first_grads(place, h, rows, one, cot, grad_qkv[h], attended[h], [])
+
+    first_sums, counts = [], []
+
+    def close(number, chosen):
+        counts.append(len(chosen))
+        first_sums.append(
+            Scatter(
+                *first_grads(
+                    place, number, rows, one, cot,
+                    [grad_qkv[h] for h in chosen], [attended[h] for h in chosen],
+                )
             )
+        )
+
+    last_group = place.groups - 1
+    for h in range(last_group):
+        attend(h)
+        if second_sums.phase >= 0:
+            second_sums.step()
+        if h == 1:
+            next_piece()
+    if last_group:
+        close(0, list(range(last_group)))
     while second_sums.phase >= 0:
         second_sums.step()
     second_mine = second_sums.end()
     line.hold(second_mine)
-    while out_pieces:
+    while out_coming:
         next_piece()
-    second_reps = Pairs(second_mine[0]) if pair == 2 else Reps(second_mine)
+    second_reps = Pairs(second_mine) if pair == 2 else Reps(second_mine)
+    attend(last_group)
+    for v in first_sums:
+        v.step()
+    close(1, [last_group])
     keep, coming = backward(0, attended, grad_qkv, w_first)
-    if place.groups > 1:
-        first_sums[0].step()
-    h = place.groups - 1
-    first_sums[h] = Scatter(
-        *first_grads(
-            place, h, rows, one, cot, grad_qkv[h], attended[h], sums_qkv + sums_back + sums_middle
-        )
-    )
-
+
+    earlier, last = first_sums[:-1], first_sums[-1]
+    for v in earlier:
+        v.step()
+    last.step()
+    if pair == 2:
+        second_reps.step()
+    vector_sums = Scatter(
+        *vector_grads(place, rows, 4 * place.heads * HD, sums_qkv, sums_back, sums_middle)
+    )
+    line.pause()
     reps = []
-    for h in range(place.groups - 1):
-        mine = first_sums[h].end()
+    for v in earlier:
+        mine = v.end()
         line.hold(mine)
         reps.append(Reps(mine))
-    if pair == 2:
-        more_reps = []
-        for o in lows:
-            (more_reps or [second_reps])[-1].step()
-            more_reps.append(Pairs(after(second_mine[o], *line.ahead)))
-    last = first_sums[-1]
-    last.step()
-    for r in reps:
-        r.step()
+    while out_coming:
+        next_piece()
     out_sum = low_sum(keep, coming)
     if pair == 2:
         out_sum = out_sum + jnp.concatenate(out_found).reshape(out_sum.shape).astype(F32)
@@ -1175,43 +1241,54 @@
         got = place.swap_phase(jnp.stack([blocks[s] for s in chosen]), phase)
         return chosen, got
 
-    chosen, got = pass_on(0)
-    last.step()
-    mine = last.end()
-    line.hold(mine)
-    reps.append(Reps(mine))
-    for phase in range(1, place.phases + 1):
+    def passed(chosen, got):
         got = line.take(got)[0]
         for k, s in enumerate(chosen):
             blocks[s] = got[k]
-        if phase < place.phases:
-            chosen, got = pass_on(phase)
-    if pair == 2:
-        more_reps[-1].step()
-    else:
-        while second_reps.masks:
-            second_reps.step()
-        second_reps.step()
+
+    going = pass_on(0)
+    line.pause()
+    vector_sums.step()
+    last.step()
+    line.pause()
+    vector_sums.step()
+    line.pause()
+    mine = jnp.concatenate([last.end(), vector_sums.end()], axis=1)
+    line.hold(mine)
+    reps.append(Reps(mine))
+    line.pause()
+    for r in reps[:-1]:
+        r.step()
+        line.pause()
+    reps[-1].step()
+    for phase in range(1, place.phases):
+        passed(*going)
+        going = pass_on(phase)
+    line.pause()
     for r in reps:
         while r.masks:
             r.step()
+            line.pause()
     for r in reps:
         r.step()
-    output, grad_input = finish_tokens(place, layer_input, cotangent, vec, blocks)
+    if pair == 1:
+        while second_reps.masks:
+            second_reps.step()
+            line.pause()
+        second_reps.step()
+        line.pause()
     if pair == 2:
-        ends = [second_reps.end()] + [r.end() for r in more_reps]
-        pieces = [e[0] for e in ends] + [e[1] for e in ends]
+        pieces = [v[o] for v in second_reps.end() for o in range(low_count)]
     else:
         pieces = second_reps.end()
         pieces = jnp.where(even, pieces[0], pieces[1]), jnp.where(even, pieces[1], pieces[0])
         pieces = list(jnp.concatenate(pieces, axis=2))
     grad_w_up, grad_w_down = second_end(place, pieces)
+    passed(*going)
+    output, grad_input = finish_tokens(place, layer_input, cotangent, vec, blocks)
     pieces = [p for r in reps for p in r.end()]
-    grad_w_qkv, grad_w_out, lines = first_end(place, rows, width, pieces)
-    ln1_gain_g, ln1_bias_g, ln2_gain_g, ln2_bias_g = [lines[r, :rows] for r in range(4)]
-    qkv_g = lines[4, : 3 * rows]
-    out_g = lines[5, :rows]
-    up_g = lines[6, : 4 * rows]
+    grad_w_qkv, grad_w_out, *vector_outs = first_end(place, rows, width, counts, pieces)
+    vector_outs = [v.reshape(-1) for v in vector_outs]
     return (
         output,
         grad_input,
@@ -1219,14 +1296,8 @@
         grad_w_out,
         grad_w_up,
         grad_w_down,
-        ln1_gain_g,
-        ln1_bias_g,
-        ln2_gain_g,
-        ln2_bias_g,
-        qkv_g,
-        out_g,
-        up_g,
-        out_g,
+        *vector_outs,
+        vector_outs[5],
     )
 
 

time: 241 us -> 204 us (0.85)
  waiting for transfers between devices: 73.9 us -> 58.8 us
  local copies, waits for them, and re-layouts: 18.4 us -> 10.7 us
  starting transfers between devices: 52.1 us -> 45.1 us
  Pallas kernels: 84.6 us -> 80.5 us
  other arithmetic: 6.86 us -> 4.18 us
    ppermute x14 -> x16, waiting for transfers between devices: 41.3 us -> 19.9 us  [swap_phase(): return lax.ppermute(v, 'fsdp', [(i, to(i)) for i in range(self.shards)])]
    ppermute x16 -> x13, starting transfers between devices: 26.9 us -> 18 us  [swap_rep(): return lax.ppermute(v, 'rep', [(i, i ^ mask) for i in range(self.reps)])]
    ppermute x16 -> x13, waiting for transfers between devices: 16.4 us -> 23.2 us  [swap_rep(): return lax.ppermute(v, 'rep', [(i, i ^ mask) for i in range(self.reps)])]
    unnamed x98 -> x68, local copies, waits for them, and re-layouts: 13.2 us -> 8.79 us
    pallas_call x18 -> x28, Pallas kernels: 84.6 us -> 80.5 us  [call(): pl.pallas_call(kernel, grid=grid, in_specs=in_specs, out_specs=out_specs,...]
    convert_element_type x12 -> x13, other arithmetic: 4.28 us -> 1.26 us  [add(): return (a.astype(F32) + b.astype(F32)).astype(BF16)]
    ppermute x11 -> x14, waiting for transfers between devices: 5.19 us -> 6.17 us  [swap_low(): return lax.ppermute(v, 'fsdp', [(i, i ^ mask) for i in range(self.shards)])]
    ppermute x14 -> x16, starting transfers between devices: 16.6 us -> 16.9 us  [swap_phase(): return lax.ppermute(v, 'fsdp', [(i, to(i)) for i in range(self.shards)])]
  transfers between devices with their start and end apart: 47 -> 49, of which waited for: 20 -> 20; matrix products, arithmetic and copies ran while one was open for 4% -> 2% of each run, Pallas kernels for 34% -> 38%
where the time goes in v3:
time: 204 us; the launch traced here: 201 us
  Pallas kernels  80.5 us (39%)
  waiting for transfers between devices  58.8 us (29%)
  starting transfers between devices  45.1 us (22%)
  local copies, waits for them, and re-layouts  10.7 us (5%)
  other arithmetic  4.18 us (2%)
    pallas_call x28, Pallas kernels, call(): pl.pallas_call(kernel, grid=grid, in_specs=in_specs, out_specs=out_specs,...  80.5 us
    ppermute x13, waiting for transfers between devices, swap_rep(): return lax.ppermute(v, 'rep', [(i, i ^ mask) for i in range(self.reps)])  23.2 us
    ppermute x16, waiting for transfers between devices, swap_phase(): return lax.ppermute(v, 'fsdp', [(i, to(i)) for i in range(self.shards)])  19.9 us
    ppermute x13, starting transfers between devices, swap_rep(): return lax.ppermute(v, 'rep', [(i, i ^ mask) for i in range(self.reps)])  18 us
    ppermute x16, starting transfers between devices, swap_phase(): return lax.ppermute(v, 'fsdp', [(i, to(i)) for i in range(self.shards)])  16.9 us
    ppermute x6, waiting for transfers between devices, swap_slot(): return lax.ppermute(v, 'fsdp', [(i, to(i)) for i in range(self.shards)])  9.42 us
    unnamed x68, local copies, waits for them, and re-layouts  8.79 us
    ppermute x6, starting transfers between devices, swap_slot(): return lax.ppermute(v, 'fsdp', [(i, to(i)) for i in range(self.shards)])  7.95 us
  transfers between devices with their start and end apart: 49, of which 20 were waited for; matrix products, arithmetic and copies ran while one was open for 2% of the time, Pallas kernels for 38%

profile of v3, /device:TPU:0, one launch (start us, length us, event | category | flops | bytes accessed | tf_op | source)
XLA Modules:
  0.0 201.0 jit_solution(5241544388853820954)
XLA Ops:
  0.6 2.1 %split_input.1 = (bf16[128,768]{1,0:T(8,128)(2,1)}, bf16[128,768]{1,0:T(8,128)(2,1)}, bf16[128,768]{1,0:T(8,128)(2,1)}, bf16[128,768]{1,0:T(8,128)(2,1)}) custom-call(bf16[4,128,768]{2,1,0:T(8,128)(2,1)} %source.3), custom_call_target="tpu_custom_call" | custom-call | flops 23000000512 | bytes 71875000 | tf_op jit(solution)/shard_map/split_input/pallas_call | solution.py:149
  2.7 2.9 %collective-permute-start = (bf16[128,768]{1,0:T(8,128)(2,1)}, bf16[128,768]{1,0:T(8,128)(2,1)S(1)}, u32[]{:S(2)}, u32[]{:S(2)}) collective-permute-start(bf16[128,768]{1,0:T(8,128)(2,1)} %get-tuple-element.176), channel_id=1, source_target_pairs={{0,2},{1,5},{2,0},{3,7},{4,6},{5,1},{6,4},{7,3},{8,10},{9,13},{10,... | collective-permute-start | bytes 589832 | tf_op jit(solution)/shard_map/ppermute | solution.py:99
  5.6 1.5 collective-permute-start.1
  7.2 2.1 %collective-permute-start.3 = (bf16[128,768]{1,0:T(8,128)(2,1)}, bf16[128,768]{1,0:T(8,128)(2,1)S(1)}, u32[]{:S(2)}, u32[]{:S(2)}) collective-permute-start(bf16[128,768]{1,0:T(8,128)(2,1)} %get-tuple-element.175), channel_id=1, source_target_pairs={{0,8},{8,0},{16,24},{24,16},{1,9},{9,1},{17,25},{25,17},{2,10},{10... | collective-permute-start | bytes 589832 | tf_op jit(solution)/shard_map/ppermute | solution.py:109
  9.2 2.1 %split_cotangent.1 = (bf16[128,768]{1,0:T(8,128)(2,1)}, bf16[128,768]{1,0:T(8,128)(2,1)}, bf16[128,768]{1,0:T(8,128)(2,1)}, bf16[128,768]{1,0:T(8,128)(2,1)}) custom-call(bf16[4,128,768]{2,1,0:T(8,128)(2,1)} %cot.1), custom_call_target="tpu_custom_call" | custom-call | flops 23000000512 | bytes 71875000 | tf_op jit(solution)/shard_map/split_cotangent/pallas_call | solution.py:149
  12.4 2.7 %split_weights.1 = (bf16[96,1536]{1,0:T(8,128)(2,1)}, bf16[96,1536]{1,0:T(8,128)(2,1)}, bf16[112,1536]{1,0:T(8,128)(2,1)}, bf16[112,1536]{1,0:T(8,128)(2,1)}) custom-call(bf16[96,2304]{1,0:T(8,128)(2,1)} %w_qkv, bf16[96,768]{1,0:T(8,128)(2,1)} %w_out.1, bf16[96,3072]{1,0:T(8,128)(2,1)} %w_up.1, bf16[96,3072]{1,0:T(8,128)(2,1)} %w_down.1, ...), custom_call_target="tpu_custom_call" | custom-call | flops 23000000512 | bytes 71875000 | tf_op jit(solution)/shard_map/split_weights/pallas_call | solution.py:149
  16.9 1.9 collective-permute-start.4
  18.8 1.5 collective-permute-start.6
  20.3 1.3 collective-permute-start.7
  22.4 4.2 %collective-permute-done.6 = bf16[128,768]{1,0:T(8,128)(2,1)S(1)} collective-permute-done((bf16[128,768]{1,0:T(8,128)(2,1)S(1)}, bf16[128,768]{1,0:T(8,128)(2,1)S(1)}, u32[]{:S(2)}, u32[]{:S(2)}) %collective-permute-start.6) | collective-permute-done | bytes 196640 | tf_op jit(solution)/shard_map/ppermute | solution.py:99
  26.6 4.2 %collective-permute-done.8 = bf16[128,768]{1,0:T(8,128)(2,1)S(1)} collective-permute-done((bf16[128,768]{1,0:T(8,128)(2,1)S(1)}, bf16[128,768]{1,0:T(8,128)(2,1)S(1)}, u32[]{:S(2)}, u32[]{:S(2)}) %collective-permute-start.8) | collective-permute-done | bytes 196640 | tf_op jit(solution)/shard_map/ppermute | solution.py:99
  31.0 1.6 collective-permute-start.12
  32.7 1.6 collective-permute-start.10
  34.3 1.3 collective-permute-start.11
  36.5 10.3 %collective-permute-done.12.rest_1_ = bf16[224,1536]{1,0:T(8,128)(2,1)S(1)} collective-permute-done((bf16[224,1536]{1,0:T(8,128)(2,1)S(1)}, bf16[224,1536]{1,0:T(8,128)(2,1)S(1)}, u32[]{:S(2)}, u32[]{:S(2)}) %collective-permute-start.12) | collective-permute-done | bytes 688160 | tf_op jit(solution)/shard_map/ppermute | solution.py:106
  46.9 1.3 collective-permute-start.14
  49.1 1.5 collective-permute-done.16
  51.6 6.2 %collective-permute-done.14.rest_3_ = bf16[224,1536]{1,0:T(8,128)(2,1)S(1)} collective-permute-done((bf16[224,1536]{1,0:T(8,128)(2,1)S(1)}, bf16[224,1536]{1,0:T(8,128)(2,1)S(1)}, u32[]{:S(2)}, u32[]{:S(2)}) %collective-permute-start.14) | collective-permute-done | bytes 688160 | tf_op jit(solution)/shard_map/ppermute | solution.py:106
  58.7 1.6 collective-permute-start.20
  60.2 1.3 collective-permute-start.21
  61.6 1.2 copy-done.13
  64.4 6.9 %middle_1.1 = (bf16[2,512,768]{2,1,0:T(8,128)(2,1)S(1)}, bf16[2,512,768]{2,1,0:T(8,128)(2,1)S(1)}, bf16[2,512,768]{2,1,0:T(8,128)(2,1)S(1)}, bf16[2,512,768]{2,1,0:T(8,128)(2,1)S(1)}, f32[8,768]{1,0:T(8,128)S(1)}) custom-call(bf16[512,768]{1,0:T(8,128)(2,1)S(1)} %copy-done.5, bf16[512,768]{1,0:T(8,128)(2,1)S(1)} %copy-done.11, ...), custom_call_target="tpu_custom_call" | custom-call | flops 115000000 | bytes 359375 | tf_op jit(solution)/shard_map/middle_1/pallas_call | solution.py:149
  71.3 4.0 %back_1.1 = (bf16[2,512,768]{2,1,0:T(8,128)(2,1)S(1)}, bf16[1,2,512,768]{3,2,1,0:T(8,128)(2,1)S(1)}, f32[8,768]{1,0:T(8,128)S(1)}) custom-call(bf16[2,512,768]{2,1,0:T(8,128)(2,1)S(1)} %get-tuple-element.220.refs_0_, bf16[2,512,768]{2,1,0:T(8,128)(2,1)S(1)} %get-tuple-element.221.refs_1_, bf16[2,512,768]{2,1,0:T(8,128)(2,1)S(1)} %get-tuple-element.222.refs_2_, ...), custom_call_target="tpu_custom_call" | custom-call | flops 115000000 | bytes 359375 | tf_op jit(solution)/shard_map/back_1/pallas_call | solution.py:149
  81.1 6.3 %middle_0.1 = (bf16[2,512,768]{2,1,0:T(8,128)(2,1)S(1)}, bf16[2,512,768]{2,1,0:T(8,128)(2,1)S(1)}, bf16[2,512,768]{2,1,0:T(8,128)(2,1)S(1)}, bf16[2,512,768]{2,1,0:T(8,128)(2,1)S(1)}, f32[8,768]{1,0:T(8,128)S(1)}) custom-call(bf16[512,768]{1,0:T(8,128)(2,1)S(1)} %copy-done.3, bf16[512,768]{1,0:T(8,128)(2,1)S(1)} %copy-done.9, ...), custom_call_target="tpu_custom_call" | custom-call | flops 23000000512 | bytes 71875000 | tf_op jit(solution)/shard_map/middle_0/pallas_call | solution.py:149
  87.4 5.7 %second_grads.1 = (bf16[2,192,1536]{2,1,0:T(8,128)(2,1)S(1)}, bf16[2,192,1536]{2,1,0:T(8,128)(2,1)S(1)}) custom-call(bf16[1024,768]{1,0:T(8,128)(2,1)S(1)} %bitcast.99, bf16[1024,768]{1,0:T(8,128)(2,1)S(1)} %bitcast.98, bf16[1024,768]{1,0:T(8,128)(2,1)S(1)} %bitcast.97, bf16[1024,768]{1,0:T(8,128)(2,1)S(1)} %bitcast.95, bf16[1024,768]{1,0:T(8,128)(2,1)S(1)} %bitcast.96, ...), custom_call_target="tpu_custom_call" | custom-call | flops 115000000 | bytes 359375 | tf_op jit(solution)/shard_map/second_grads/pallas_call | solution.py:149
  94.9 1.9 tables_first.1
  97.3 4.8 %front.1 = (bf16[2,512,768]{2,1,0:T(8,128)(2,1)S(1)}, bf16[2,512,128]{2,1,0:T(8,128)(2,1)S(1)}, bf16[2,512,128]{2,1,0:T(8,128)(2,1)S(1)}, bf16[2,512,128]{2,1,0:...) custom-call(bf16[512,768]{1,0:T(8,128)(2,1)S(1)} %copy-done.3, ...), custom_call_target="tpu_custom_call" | custom-call | flops 115000000 | bytes 359375 | tf_op jit(solution)/shard_map/front/pallas_call | solution.py:149
  102.1 8.7 %attention_0.1 = (bf16[2,512,128]{2,1,0:T(8,128)(2,1)S(1)}, bf16[2,512,384]{2,1,0:T(8,128)(2,1)S(1)}, f32[8,384]{1,0:T(8,128)S(1)}) custom-call(bf16[2,512,128]{2,1,0:T(8,128)(2,1)S(1)} %get-tuple-element.255.q_in, bf16[2,512,128]{2,1,0:T(8,128)(2,1)S(1)} %get-tuple-element.256.k_in, bf16[2,512,128]{2,1,0:T(8,128)(2,1)S(1)} %get-tuple-element.257.v_in, ...), custom_call_target="tpu_custom_call" | custom-call | flops 23000000512 | bytes 71875000 | tf_op jit(solution)/shard_map/attention_0/pallas_call | solution.py:149
  111.5 8.8 %attention_1.1 = (bf16[2,512,128]{2,1,0:T(8,128)(2,1)S(1)}, bf16[2,512,384]{2,1,0:T(8,128)(2,1)S(1)}, f32[8,384]{1,0:T(8,128)S(1)}) custom-call(bf16[2,512,128]{2,1,0:T(8,128)(2,1)S(1)} %get-tuple-element.261.q_in, bf16[2,512,128]{2,1,0:T(8,128)(2,1)S(1)} %get-tuple-element.262.k_in, bf16[2,512,128]{2,1,0:T(8,128)(2,1)S(1)} %get-tuple-element.263.v_in, ...), custom_call_target="tpu_custom_call" | custom-call | flops 23000000512 | bytes 71875000 | tf_op jit(solution)/shard_map/attention_1/pallas_call | solution.py:149
  121.3 2.9 %first_grads_0.1 = (bf16[2,192,1024]{2,1,0:T(8,128)(2,1)S(1)}, bf16[2,192,1024]{2,1,0:T(8,128)(2,1)S(1)}) custom-call(bf16[1024,768]{1,0:T(8,128)(2,1)S(1)} %bitcast.106, bf16[1024,384]{1,0:T(8,128)(2,1)S(1)} %bitcast.100, bf16[1024,384]{1,0:T(8,128)(2,1)S(1)} %bitcast.101, bf16[1024,128]{1,0:T(8,128)(2,1)S(1)} %bitcast.103, ...), custom_call_target="tpu_custom_call" | custom-call | flops 23000000512 | bytes 71875000 | tf_op jit(solution)/shard_map/first_grads_0/pallas_call | solution.py:149
  125.1 2.7 %collective-permute-start.33 = (bf16[2,96,1536]{2,1,0:T(8,128)(2,1)S(1)}, bf16[2,96,1536]{2,1,0:T(8,128)(2,1)S(1)}, u32[]{:S(2)}, u32[]{:S(2)}) collective-permute-start(bf16[2,96,1536]{2,1,0:T(8,128)(2,1)S(1)} %pad_maximum_fusion.4), channel_id=1, source_target_pairs={{0,16},{8,24},{16,0},{24,8},{1,17},{9,25},{17,1},{25,9},{2,18},{10... | collective-permute-start | bytes 1769480 | tf_op jit(solution)/shard_map/ppermute | solution.py:109
  127.8 8.6 %attention_2.1 = (bf16[2,512,128]{2,1,0:T(8,128)(2,1)S(1)}, bf16[2,512,384]{2,1,0:T(8,128)(2,1)S(1)}, f32[8,384]{1,0:T(8,128)S(1)}) custom-call(bf16[2,512,128]{2,1,0:T(8,128)(2,1)S(1)} %get-tuple-element.276.q_in, bf16[2,512,128]{2,1,0:T(8,128)(2,1)S(1)} %get-tuple-element.277.k_in, bf16[2,512,128]{2,1,0:T(8,128)(2,1)S(1)} %get-tuple-element.278.v_in, ...), custom_call_target="tpu_custom_call" | custom-call | flops 23000000512 | bytes 71875000 | tf_op jit(solution)/shard_map/attention_2/pallas_call | solution.py:149
  137.6 1.5 first_grads_1.1
  139.1 1.4 collective-permute-start.34
  140.5 8.0 %back_0.1 = (bf16[2,512,768]{2,1,0:T(8,128)(2,1)S(1)}, bf16[1,2,512,768]{3,2,1,0:T(8,128)(2,1)S(1)}, f32[8,768]{1,0:T(8,128)S(1)}) custom-call(bf16[2,512,768]{2,1,0:T(8,128)(2,1)S(1)} %get-tuple-element.285.refs_0_, bf16[2,512,768]{2,1,0:T(8,128)(2,1)S(1)} %get-tuple-element.240.refs_1_, bf16[2,512,768]{2,1,0:T(8,128)(2,1)S(1)} %get-tuple-element.239.refs_2_, ...), custom_call_target="tpu_custom_call" | custom-call | flops 2300000000 | bytes 7187500 | tf_op jit(solution)/shard_map/back_0/pallas_call | solution.py:149
  150.6 3.8 %collective-permute-done.33 = bf16[2,96,1536]{2,1,0:T(8,128)(2,1)S(1)} collective-permute-done((bf16[2,96,1536]{2,1,0:T(8,128)(2,1)S(1)}, bf16[2,96,1536]{2,1,0:T(8,128)(2,1)S(1)}, u32[]{:S(2)}, u32[]{:S(2)}) %collective-permute-start.33) | collective-permute-done | bytes 589856 | tf_op jit(solution)/shard_map/ppermute | solution.py:109
  155.7 1.3 collective-permute-done.32
  157.7 1.4 collective-permute-start.42
  160.0 1.2 collective-permute-done.37
  163.8 1.4 collective-permute-done.39
  166.5 1.4 collective-permute-start.41
  167.9 7.2 %collective-permute-done.42 = bf16[2,96,512]{2,1,0:T(8,128)(2,1)S(1)} collective-permute-done((bf16[2,96,512]{2,1,0:T(8,128)(2,1)S(1)}, bf16[2,96,512]{2,1,0:T(8,128)(2,1)S(1)}, u32[]{:S(2)}, u32[]{:S(2)}) %collective-permute-start.42) | collective-permute-done | bytes 196640 | tf_op jit(solution)/shard_map/ppermute | solution.py:109
  175.2 2.1 %collective-permute-start.46 = (bf16[2,96,512]{2,1,0:T(8,128)(2,1)S(1)}, bf16[2,96,512]{2,1,0:T(8,128)(2,1)S(1)}, u32[]{:S(2)}, u32[]{:S(2)}) collective-permute-start(bf16[2,96,512]{2,1,0:T(8,128)(2,1)S(1)} %add_convert_fusion.9), channel_id=1, source_target_pairs={{0,16},{8,24},{16,0},{24,8},{1,17},{9,25},{17,1},{25,9},{2,18},{10... | collective-permute-start | bytes 589832 | tf_op jit(solution)/shard_map/ppermute | solution.py:109
  177.3 2.2 %collective-permute-start.45 = (bf16[2,112,256]{2,1,0:T(8,128)(2,1)S(1)}, bf16[2,112,256]{2,1,0:T(8,128)(2,1)S(1)}, u32[]{:S(2)}, u32[]{:S(2)}) collective-permute-start(bf16[2,112,256]{2,1,0:T(8,128)(2,1)S(1)} %add_convert_fusion.13), channel_id=1, source_target_pairs={{0,16},{8,24},{16,0},{24,8},{1,17},{9,25},{17,1},{25,9},{2,18},{10... | collective-permute-start | bytes 344072 | tf_op jit(solution)/shard_map/ppermute | solution.py:109
  180.4 8.8 %collective-permute-done.46 = bf16[2,96,512]{2,1,0:T(8,128)(2,1)S(1)} collective-permute-done((bf16[2,96,512]{2,1,0:T(8,128)(2,1)S(1)}, bf16[2,96,512]{2,1,0:T(8,128)(2,1)S(1)}, u32[]{:S(2)}, u32[]{:S(2)}) %collective-permute-start.46) | collective-permute-done | bytes 196640 | tf_op jit(solution)/shard_map/ppermute | solution.py:109
  191.6 1.6 second_end.1
  193.7 2.1 %finish_tokens.1 = (bf16[4,128,768]{2,1,0:T(8,128)(2,1)}, bf16[4,128,768]{2,1,0:T(8,128)(2,1)}) custom-call(bf16[4,128,768]{2,1,0:T(8,128)(2,1)S(1)} %copy-done.16, bf16[4,128,768]{2,1,0:T(8,128)(2,1)S(1)} %copy-done.17, f32[8,768]{1,0:T(8,128)S(1)} %get-tuple-element.216.refs_4_.refs_3_.refs_9_.vec, bf16[2,128,768]{2,1,0:T(8,128)(2,1)S(1)} %get-tuple-element.336.rest_0_, ...), custom_call_target="tpu_custom_call" | custom-call | flops 23000000512 | bytes 71875000 | tf_op jit(solution)/shard_map/finish_tokens/pallas_call | solution.py:149
  195.9 1.2 collective-permute-done.47.refs_3_
  (194 shorter events, 36.8 us)
Async XLA Ops:
  2.7 12.5 %collective-permute-start = (bf16[128,768]{1,0:T(8,128)(2,1)}, bf16[128,768]{1,0:T(8,128)(2,1)S(1)}, u32[]{:S(2)}, u32[]{:S(2)}) collective-permute-start(bf16[128,768]{1,0:T(8,128)(2,1)} %get-tuple-element.176), channel_id=1, source_target_pairs={{0,2},{1,5},{2,0},{3,7},{4,6},{5,1},{6,4},{7,3},{8,10},{9,13},{10,... | collective-permute-start | bytes 589832 | tf_op jit(solution)/shard_map/ppermute | solution.py:99
  5.6 9.6 %collective-permute-start.1 = (bf16[128,768]{1,0:T(8,128)(2,1)}, bf16[128,768]{1,0:T(8,128)(2,1)S(1)}, u32[]{:S(2)}, u32[]{:S(2)}) collective-permute-start(bf16[128,768]{1,0:T(8,128)(2,1)} %get-tuple-element.177), channel_id=1, source_target_pairs={{0,4},{1,3},{2,6},{3,1},{4,0},{5,7},{6,2},{7,5},{8,12},{9,11},{10,... | collective-permute-start | bytes 589832 | tf_op jit(solution)/shard_map/ppermute | solution.py:99
  7.2 9.0 %collective-permute-start.2 = (bf16[128,768]{1,0:T(8,128)(2,1)}, bf16[128,768]{1,0:T(8,128)(2,1)S(1)}, u32[]{:S(2)}, u32[]{:S(2)}) collective-permute-start(bf16[128,768]{1,0:T(8,128)(2,1)} %get-tuple-element.178), channel_id=1, source_target_pairs={{0,6},{1,7},{2,4},{3,5},{4,2},{5,3},{6,0},{7,1},{8,14},{9,15},{10,... | collective-permute-start | bytes 589832 | tf_op jit(solution)/shard_map/ppermute | solution.py:99
  7.2 9.0 %collective-permute-start.3 = (bf16[128,768]{1,0:T(8,128)(2,1)}, bf16[128,768]{1,0:T(8,128)(2,1)S(1)}, u32[]{:S(2)}, u32[]{:S(2)}) collective-permute-start(bf16[128,768]{1,0:T(8,128)(2,1)} %get-tuple-element.175), channel_id=1, source_target_pairs={{0,8},{8,0},{16,24},{24,16},{1,9},{9,1},{17,25},{25,17},{2,10},{10... | collective-permute-start | bytes 589832 | tf_op jit(solution)/shard_map/ppermute | solution.py:109
  16.3 6.0 %collective-permute-start.9 = (bf16[512,768]{1,0:T(8,128)(2,1)S(1)}, bf16[512,768]{1,0:T(8,128)(2,1)S(1)}, u32[]{:S(2)}, u32[]{:S(2)}) collective-permute-start(bf16[512,768]{1,0:T(8,128)(2,1)S(1)} %get-tuple-element.248.refs_0_), channel_id=1, source_target_pairs={{0,1},{1,0},{2,3},{3,2},{4,5},{5,4},{6,7},{7,6},{8,9},{9,8},{10,11... | collective-permute-start | bytes 2359304 | tf_op jit(solution)/shard_map/ppermute | solution.py:92
  16.4 5.2 %collective-permute-start.5 = (bf16[112,1536]{1,0:T(8,128)(2,1)S(1)}, bf16[112,1536]{1,0:T(8,128)(2,1)S(1)}, u32[]{:S(2)}, u32[]{:S(2)}) collective-permute-start(bf16[112,1536]{1,0:T(8,128)(2,1)S(1)} %copy-done.24), channel_id=1, source_target_pairs={{0,1},{1,0},{2,3},{3,2},{4,5},{5,4},{6,7},{7,6},{8,9},{9,8},{10,11... | collective-permute-start | bytes 1032200 | tf_op jit(solution)/shard_map/ppermute | solution.py:92
  16.9 15.6 %collective-permute-start.4 = (bf16[384,768]{1,0:T(8,128)(2,1)S(1)}, bf16[384,768]{1,0:T(8,128)(2,1)S(1)}, u32[]{:S(2)}, u32[]{:S(2)}) collective-permute-start(bf16[384,768]{1,0:T(8,128)(2,1)S(1)} %get-tuple-element.362), channel_id=1, source_target_pairs={{0,8},{8,0},{16,24},{24,16},{1,9},{9,1},{17,25},{25,17},{2,10},{10... | collective-permute-start | bytes 1769480 | tf_op jit(solution)/shard_map/ppermute | solution.py:109
  18.8 7.8 %collective-permute-start.6 = (bf16[128,768]{1,0:T(8,128)(2,1)S(1)}, bf16[128,768]{1,0:T(8,128)(2,1)S(1)}, u32[]{:S(2)}, u32[]{:S(2)}) collective-permute-start(bf16[128,768]{1,0:T(8,128)(2,1)S(1)} %copy-done.28), channel_id=1, source_target_pairs={{0,2},{1,5},{2,0},{3,7},{4,6},{5,1},{6,4},{7,3},{8,10},{9,13},{10,... | collective-permute-start | bytes 589832 | tf_op jit(solution)/shard_map/ppermute | solution.py:99
  20.3 6.3 %collective-permute-start.7 = (bf16[128,768]{1,0:T(8,128)(2,1)S(1)}, bf16[128,768]{1,0:T(8,128)(2,1)S(1)}, u32[]{:S(2)}, u32[]{:S(2)}) collective-permute-start(bf16[128,768]{1,0:T(8,128)(2,1)S(1)} %copy-done.27), channel_id=1, source_target_pairs={{0,4},{1,3},{2,6},{3,1},{4,0},{5,7},{6,2},{7,5},{8,12},{9,11},{10,... | collective-permute-start | bytes 589832 | tf_op jit(solution)/shard_map/ppermute | solution.py:99
  21.6 9.2 %collective-permute-start.8 = (bf16[128,768]{1,0:T(8,128)(2,1)S(1)}, bf16[128,768]{1,0:T(8,128)(2,1)S(1)}, u32[]{:S(2)}, u32[]{:S(2)}) collective-permute-start(bf16[128,768]{1,0:T(8,128)(2,1)S(1)} %copy-done.26), channel_id=1, source_target_pairs={{0,6},{1,7},{2,4},{3,5},{4,2},{5,3},{6,0},{7,1},{8,14},{9,15},{10,... | collective-permute-start | bytes 589832 | tf_op jit(solution)/shard_map/ppermute | solution.py:99
  30.9 4.8 %collective-permute-start.13 = (bf16[512,768]{1,0:T(8,128)(2,1)S(1)}, bf16[512,768]{1,0:T(8,128)(2,1)S(1)}, u32[]{:S(2)}, u32[]{:S(2)}) collective-permute-start(bf16[512,768]{1,0:T(8,128)(2,1)S(1)} %constant_dynamic-update-slice_fusion.9.refs_2_.refs_6_.refs_0_.refs_4_), channel_id=1, source_target_pairs={{0,1},{1,0},{2,3},{3,2},{4,5},{5,4},{6,7},{7,6},{8,9},{9,8},{10,11... | collective-permute-start | bytes 2359304 | tf_op jit(solution)/shard_map/ppermute | solution.py:92
  31.0 15.9 %collective-permute-start.12 = (bf16[224,1536]{1,0:T(8,128)(2,1)S(1)}, bf16[224,1536]{1,0:T(8,128)(2,1)S(1)}, u32[]{:S(2)}, u32[]{:S(2)}) collective-permute-start(bf16[224,1536]{1,0:T(8,128)(2,1)S(1)} %constant_dynamic-update-slice_fusion.7.rest_0_), channel_id=1, source_target_pairs={{0,2},{1,5},{2,0},{3,7},{4,6},{5,1},{6,4},{7,3},{8,10},{9,13},{10,... | collective-permute-start | bytes 2064392 | tf_op jit(solution)/shard_map/ppermute | solution.py:106
  32.6 15.6 %collective-permute-start.15 = (bf16[512,768]{1,0:T(8,128)(2,1)S(1)}, bf16[512,768]{1,0:T(8,128)(2,1)S(1)}, u32[]{:S(2)}, u32[]{:S(2)}) collective-permute-start(bf16[512,768]{1,0:T(8,128)(2,1)S(1)} %constant_dynamic-update-slice_fusion.13.refs_0_), channel_id=1, source_target_pairs={{0,1},{1,0},{2,3},{3,2},{4,5},{5,4},{6,7},{7,6},{8,9},{9,8},{10,11... | collective-permute-start | bytes 2359304 | tf_op jit(solution)/shard_map/ppermute | solution.py:92
  32.7 25.9 %collective-permute-start.10 = (bf16[512,768]{1,0:T(8,128)(2,1)S(1)}, bf16[512,768]{1,0:T(8,128)(2,1)S(1)}, u32[]{:S(2)}, u32[]{:S(2)}) collective-permute-start(bf16[512,768]{1,0:T(8,128)(2,1)S(1)} %constant_dynamic-update-slice_fusion.9.refs_2_.refs_6_.refs_0_.refs_4_), channel_id=1, source_target_pairs={{0,8},{8,0},{16,24},{24,16},{1,9},{9,1},{17,25},{25,17},{2,10},{10... | collective-permute-start | bytes 2359304 | tf_op jit(solution)/shard_map/ppermute | solution.py:109
  34.3 16.4 %collective-permute-start.11 = (bf16[224,1536]{1,0:T(8,128)(2,1)S(1)}, bf16[224,1536]{1,0:T(8,128)(2,1)S(1)}, u32[]{:S(2)}, u32[]{:S(2)}) collective-permute-start(bf16[224,1536]{1,0:T(8,128)(2,1)S(1)} %constant_dynamic-update-slice_fusion.7.rest_0_), channel_id=1, source_target_pairs={{0,4},{1,3},{2,6},{3,1},{4,0},{5,7},{6,2},{7,5},{8,12},{9,11},{10,... | collective-permute-start | bytes 2064392 | tf_op jit(solution)/shard_map/ppermute | solution.py:106
  46.9 10.9 %collective-permute-start.14 = (bf16[224,1536]{1,0:T(8,128)(2,1)S(1)}, bf16[224,1536]{1,0:T(8,128)(2,1)S(1)}, u32[]{:S(2)}, u32[]{:S(2)}) collective-permute-start(bf16[224,1536]{1,0:T(8,128)(2,1)S(1)} %collective-permute-done.12.rest_1_), channel_id=1, source_target_pairs={{0,4},{1,3},{2,6},{3,1},{4,0},{5,7},{6,2},{7,5},{8,12},{9,11},{10,... | collective-permute-start | bytes 2064392 | tf_op jit(solution)/shard_map/ppermute | solution.py:106
  49.1 1.6 collective-permute-start.16
  58.7 5.7 %collective-permute-start.17 = (bf16[512,768]{1,0:T(8,128)(2,1)S(1)}, bf16[512,768]{1,0:T(8,128)(2,1)S(1)}, u32[]{:S(2)}, u32[]{:S(2)}) collective-permute-start(bf16[512,768]{1,0:T(8,128)(2,1)S(1)} %collective-permute-done.10.refs_2_.refs_8_), channel_id=1, source_target_pairs={{0,1},{1,0},{2,3},{3,2},{4,5},{5,4},{6,7},{7,6},{8,9},{9,8},{10,11... | collective-permute-start | bytes 2359304 | tf_op jit(solution)/shard_map/ppermute | solution.py:92
  58.7 17.3 %collective-permute-start.20 = (bf16[192,1536]{1,0:T(8,128)(2,1)S(1)}, bf16[192,1536]{1,0:T(8,128)(2,1)}, u32[]{:S(2)}, u32[]{:S(2)}) collective-permute-start(bf16[192,1536]{1,0:T(8,128)(2,1)S(1)} %constant_dynamic-update-slice_fusion.15.rest_0_), channel_id=1, source_target_pairs={{0,2},{1,5},{2,0},{3,7},{4,6},{5,1},{6,4},{7,3},{8,10},{9,13},{10,... | collective-permute-start | bytes 1769480 | tf_op jit(solution)/shard_map/ppermute | solution.py:106
  60.2 15.8 %collective-permute-start.21 = (bf16[192,1536]{1,0:T(8,128)(2,1)S(1)}, bf16[192,1536]{1,0:T(8,128)(2,1)}, u32[]{:S(2)}, u32[]{:S(2)}) collective-permute-start(bf16[192,1536]{1,0:T(8,128)(2,1)S(1)} %constant_dynamic-update-slice_fusion.15.rest_0_), channel_id=1, source_target_pairs={{0,4},{1,3},{2,6},{3,1},{4,0},{5,7},{6,2},{7,5},{8,12},{9,11},{10,... | collective-permute-start | bytes 1769480 | tf_op jit(solution)/shard_map/ppermute | solution.py:106
  75.4 2.4 %collective-permute-start.18 = (bf16[512,768]{1,0:T(8,128)(2,1)S(1)}, bf16[512,768]{1,0:T(8,128)(2,1)S(1)}, u32[]{:S(2)}, u32[]{:S(2)}) collective-permute-start(bf16[512,768]{1,0:T(8,128)(2,1)S(1)} %get-tuple-element.347), channel_id=1, source_target_pairs={{0,1},{1,0},{2,3},{3,2},{4,5},{5,4},{6,7},{7,6},{8,9},{9,8},{10,11... | collective-permute-start | bytes 2359304 | tf_op jit(solution)/shard_map/ppermute | solution.py:92
  75.5 3.4 %collective-permute-start.19 = (bf16[512,768]{1,0:T(8,128)(2,1)S(1)}, bf16[512,768]{1,0:T(8,128)(2,1)S(1)}, u32[]{:S(2)}, u32[]{:S(2)}) collective-permute-start(bf16[512,768]{1,0:T(8,128)(2,1)S(1)} %get-tuple-element.346), channel_id=1, source_target_pairs={{0,1},{1,0},{2,3},{3,2},{4,5},{5,4},{6,7},{7,6},{8,9},{9,8},{10,11... | collective-permute-start | bytes 2359304 | tf_op jit(solution)/shard_map/ppermute | solution.py:92
  76.0 18.9 %collective-permute-start.22 = (bf16[192,1536]{1,0:T(8,128)(2,1)}, bf16[192,1536]{1,0:T(8,128)(2,1)S(1)}, u32[]{:S(2)}, u32[]{:S(2)}) collective-permute-start(bf16[192,1536]{1,0:T(8,128)(2,1)} %collective-permute-done.20.rest_1_), channel_id=1, source_target_pairs={{0,4},{1,3},{2,6},{3,1},{4,0},{5,7},{6,2},{7,5},{8,12},{9,11},{10,... | collective-permute-start | bytes 1769480 | tf_op jit(solution)/shard_map/ppermute | solution.py:106
  79.4 15.4 %collective-permute-start.23 = (bf16[384,768]{1,0:T(8,128)(2,1)S(1)}, bf16[384,768]{1,0:T(8,128)(2,1)S(1)}, u32[]{:S(2)}, u32[]{:S(2)}) collective-permute-start(bf16[384,768]{1,0:T(8,128)(2,1)S(1)} %slice.232), channel_id=1, source_target_pairs={{0,8},{8,0},{16,24},{24,16},{1,9},{9,1},{17,25},{25,17},{2,10},{10... | collective-permute-start | bytes 1769480 | tf_op jit(solution)/shard_map/ppermute | solution.py:109
  93.2 17.7 %collective-permute-start.25 = (bf16[2,192,1536]{2,1,0:T(8,128)(2,1)S(1)}, bf16[2,192,1536]{2,1,0:T(8,128)(2,1)S(1)}, u32[]{:S(2)}, u32[]{:S(2)}) collective-permute-start(bf16[2,192,1536]{2,1,0:T(8,128)(2,1)S(1)} %get-tuple-element.254), channel_id=1, source_target_pairs={{0,4},{1,3},{2,6},{3,1},{4,0},{5,7},{6,2},{7,5},{8,12},{9,11},{10,... | collective-permute-start | bytes 3538952 | tf_op jit(solution)/shard_map/ppermute | solution.py:106
  96.8 24.4 %collective-permute-start.24 = (bf16[640,768]{1,0:T(8,128)(2,1)S(1)}, bf16[640,768]{1,0:T(8,128)(2,1)S(1)}, u32[]{:S(2)}, u32[]{:S(2)}) collective-permute-start(bf16[640,768]{1,0:T(8,128)(2,1)S(1)} %pad_maximum_fusion.1), channel_id=1, source_target_pairs={{0,8},{8,0},{16,24},{24,16},{1,9},{9,1},{17,25},{25,17},{2,10},{10... | collective-permute-start | bytes 2949128 | tf_op jit(solution)/shard_map/ppermute | solution.py:109
  111.0 9.9 %collective-permute-start.26 = (bf16[192,1536]{1,0:T(8,128)(2,1)S(1)}, bf16[192,1536]{1,0:T(8,128)(2,1)S(1)}, u32[]{:S(2)}, u32[]{:S(2)}) collective-permute-start(bf16[192,1536]{1,0:T(8,128)(2,1)S(1)} %fusion.3), channel_id=1, source_target_pairs={{0,2},{1,5},{2,0},{3,7},{4,6},{5,1},{6,4},{7,3},{8,10},{9,13},{10,... | collective-permute-start | bytes 1769480 | tf_op jit(solution)/shard_map/ppermute | solution.py:106
  121.2 3.8 %collective-permute-start.28 = (bf16[96,1536]{1,0:T(8,128)(2,1)S(1)}, bf16[96,1536]{1,0:T(8,128)(2,1)S(1)}, u32[]{:S(2)}, u32[]{:S(2)}) collective-permute-start(bf16[96,1536]{1,0:T(8,128)(2,1)S(1)} %get-tuple-element.357), channel_id=1, source_target_pairs={{0,1},{1,0},{2,3},{3,2},{4,5},{5,4},{6,7},{7,6},{8,9},{9,8},{10,11... | collective-permute-start | bytes 884744 | tf_op jit(solution)/shard_map/ppermute | solution.py:92
  124.2 12.2 %collective-permute-start.27 = (bf16[2,192,1024]{2,1,0:T(8,128)(2,1)S(1)}, bf16[2,192,1024]{2,1,0:T(8,128)(2,1)S(1)}, u32[]{:S(2)}, u32[]{:S(2)}) collective-permute-start(bf16[2,192,1024]{2,1,0:T(8,128)(2,1)S(1)} %get-tuple-element.272), channel_id=1, source_target_pairs={{0,4},{1,3},{2,6},{3,1},{4,0},{5,7},{6,2},{7,5},{8,12},{9,11},{10,... | collective-permute-start | bytes 2359304 | tf_op jit(solution)/shard_map/ppermute | solution.py:106
  125.1 29.3 %collective-permute-start.33 = (bf16[2,96,1536]{2,1,0:T(8,128)(2,1)S(1)}, bf16[2,96,1536]{2,1,0:T(8,128)(2,1)S(1)}, u32[]{:S(2)}, u32[]{:S(2)}) collective-permute-start(bf16[2,96,1536]{2,1,0:T(8,128)(2,1)S(1)} %pad_maximum_fusion.4), channel_id=1, source_target_pairs={{0,16},{8,24},{16,0},{24,8},{1,17},{9,25},{17,1},{25,9},{2,18},{10... | collective-permute-start | bytes 1769480 | tf_op jit(solution)/shard_map/ppermute | solution.py:109
  136.5 12.7 %collective-permute-start.31 = (bf16[192,1024]{1,0:T(8,128)(2,1)S(1)}, bf16[192,1024]{1,0:T(8,128)(2,1)S(1)}, u32[]{:S(2)}, u32[]{:S(2)}) collective-permute-start(bf16[192,1024]{1,0:T(8,128)(2,1)S(1)} %fusion.4), channel_id=1, source_target_pairs={{0,2},{1,5},{2,0},{3,7},{4,6},{5,1},{6,4},{7,3},{8,10},{9,13},{10,... | collective-permute-start | bytes 1179656 | tf_op jit(solution)/shard_map/ppermute | solution.py:106
  139.1 10.1 %collective-permute-start.34 = (bf16[2,192,512]{2,1,0:T(8,128)(2,1)S(1)}, bf16[2,192,512]{2,1,0:T(8,128)(2,1)S(1)}, u32[]{:S(2)}, u32[]{:S(2)}) collective-permute-start(bf16[2,192,512]{2,1,0:T(8,128)(2,1)S(1)} %get-tuple-element.290), channel_id=1, source_target_pairs={{0,4},{1,3},{2,6},{3,1},{4,0},{5,7},{6,2},{7,5},{8,12},{9,11},{10,... | collective-permute-start | bytes 1179656 | tf_op jit(solution)/shard_map/ppermute | solution.py:106
  148.7 9.0 %collective-permute-start.29 = (bf16[512,768]{1,0:T(8,128)(2,1)S(1)}, bf16[512,768]{1,0:T(8,128)(2,1)S(1)}, u32[]{:S(2)}, u32[]{:S(2)}) collective-permute-start(bf16[512,768]{1,0:T(8,128)(2,1)S(1)} %get-tuple-element.343), channel_id=1, source_target_pairs={{0,1},{1,0},{2,3},{3,2},{4,5},{5,4},{6,7},{7,6},{8,9},{9,8},{10,11... | collective-permute-start | bytes 2359304 | tf_op jit(solution)/shard_map/ppermute | solution.py:92
  148.8 10.3 %collective-permute-start.30 = (bf16[512,768]{1,0:T(8,128)(2,1)S(1)}, bf16[512,768]{1,0:T(8,128)(2,1)S(1)}, u32[]{:S(2)}, u32[]{:S(2)}) collective-permute-start(bf16[512,768]{1,0:T(8,128)(2,1)S(1)} %get-tuple-element.342), channel_id=1, source_target_pairs={{0,1},{1,0},{2,3},{3,2},{4,5},{5,4},{6,7},{7,6},{8,9},{9,8},{10,11... | collective-permute-start | bytes 2359304 | tf_op jit(solution)/shard_map/ppermute | solution.py:92
  149.3 13.2 %collective-permute-start.36 = (bf16[192,512]{1,0:T(8,128)(2,1)S(1)}, bf16[192,512]{1,0:T(8,128)(2,1)S(1)}, u32[]{:S(2)}, u32[]{:S(2)}) collective-permute-start(bf16[192,512]{1,0:T(8,128)(2,1)S(1)} %fusion.5), channel_id=1, source_target_pairs={{0,2},{1,5},{2,0},{3,7},{4,6},{5,1},{6,4},{7,3},{8,10},{9,13},{10,... | collective-permute-start | bytes 589832 | tf_op jit(solution)/shard_map/ppermute | solution.py:106
  154.7 36.9 %collective-permute-start.44 = (bf16[2,96,1536]{2,1,0:T(8,128)(2,1)S(1)}, bf16[2,96,1536]{2,1,0:T(8,128)(2,1)S(1)}, u32[]{:S(2)}, u32[]{:S(2)}) collective-permute-start(bf16[2,96,1536]{2,1,0:T(8,128)(2,1)S(1)} %add_convert_fusion.1), channel_id=1, source_target_pairs={{0,8},{8,0},{16,24},{24,16},{1,9},{9,1},{17,25},{25,17},{2,10},{10... | collective-permute-start | bytes 1769480 | tf_op jit(solution)/shard_map/ppermute | solution.py:109
  155.4 1.5 collective-permute-start.32
  157.0 4.3 %collective-permute-start.37 = (bf16[2,32,512]{2,1,0:T(8,128)(2,1)S(1)}, bf16[2,32,512]{2,1,0:T(8,128)(2,1)S(1)}, u32[]{:S(2)}, u32[]{:S(2)}) collective-permute-start(bf16[2,32,512]{2,1,0:T(8,128)(2,1)S(1)} %get-tuple-element.299), channel_id=1, source_target_pairs={{0,4},{1,3},{2,6},{3,1},{4,0},{5,7},{6,2},{7,5},{8,12},{9,11},{10,... | collective-permute-start | bytes 196616 | tf_op jit(solution)/shard_map/ppermute | solution.py:106
  157.7 17.4 %collective-permute-start.42 = (bf16[2,96,512]{2,1,0:T(8,128)(2,1)S(1)}, bf16[2,96,512]{2,1,0:T(8,128)(2,1)S(1)}, u32[]{:S(2)}, u32[]{:S(2)}) collective-permute-start(bf16[2,96,512]{2,1,0:T(8,128)(2,1)S(1)} %broadcast_select_fusion), channel_id=1, source_target_pairs={{0,8},{8,0},{16,24},{24,16},{1,9},{9,1},{17,25},{25,17},{2,10},{10... | collective-permute-start | bytes 589832 | tf_op jit(solution)/shard_map/ppermute | solution.py:109
  161.2 4.0 %collective-permute-start.39 = (bf16[32,512]{1,0:T(8,128)(2,1)S(1)}, bf16[32,512]{1,0:T(8,128)(2,1)S(1)}, u32[]{:S(2)}, u32[]{:S(2)}) collective-permute-start(bf16[32,512]{1,0:T(8,128)(2,1)S(1)} %fusion.8), channel_id=1, source_target_pairs={{0,2},{1,5},{2,0},{3,7},{4,6},{5,1},{6,4},{7,3},{8,10},{9,13},{10,... | collective-permute-start | bytes 98312 | tf_op jit(solution)/shard_map/ppermute | solution.py:106
  162.6 16.9 %collective-permute-start.35 = (bf16[2,2,128,768]{3,2,1,0:T(8,128)(2,1)S(1)}, bf16[2,2,128,768]{3,2,1,0:T(8,128)(2,1)S(1)}, u32[]{:S(2)}, u32[]{:S(2)}) collective-permute-start(bf16[2,2,128,768]{3,2,1,0:T(8,128)(2,1)S(1)} %pad_maximum_fusion.2), channel_id=1, source_target_pairs={{0,2},{1,5},{2,0},{3,7},{4,6},{5,1},{6,4},{7,3},{8,10},{9,13},{10,... | collective-permute-start | bytes 2359304 | tf_op jit(solution)/shard_map/ppermute | solution.py:106
  163.7 1.6 collective-permute-start.38
  166.5 10.7 %collective-permute-start.41 = (bf16[2,112,256]{2,1,0:T(8,128)(2,1)S(1)}, bf16[2,112,256]{2,1,0:T(8,128)(2,1)S(1)}, u32[]{:S(2)}, u32[]{:S(2)}) collective-permute-start(bf16[2,112,256]{2,1,0:T(8,128)(2,1)S(1)} %broadcast_select_fusion.1), channel_id=1, source_target_pairs={{0,8},{8,0},{16,24},{24,16},{1,9},{9,1},{17,25},{25,17},{2,10},{10... | collective-permute-start | bytes 344072 | tf_op jit(solution)/shard_map/ppermute | solution.py:109
  175.2 14.0 %collective-permute-start.46 = (bf16[2,96,512]{2,1,0:T(8,128)(2,1)S(1)}, bf16[2,96,512]{2,1,0:T(8,128)(2,1)S(1)}, u32[]{:S(2)}, u32[]{:S(2)}) collective-permute-start(bf16[2,96,512]{2,1,0:T(8,128)(2,1)S(1)} %add_convert_fusion.9), channel_id=1, source_target_pairs={{0,16},{8,24},{16,0},{24,8},{1,17},{9,25},{17,1},{25,9},{2,18},{10... | collective-permute-start | bytes 589832 | tf_op jit(solution)/shard_map/ppermute | solution.py:109
  177.3 13.2 %collective-permute-start.45 = (bf16[2,112,256]{2,1,0:T(8,128)(2,1)S(1)}, bf16[2,112,256]{2,1,0:T(8,128)(2,1)S(1)}, u32[]{:S(2)}, u32[]{:S(2)}) collective-permute-start(bf16[2,112,256]{2,1,0:T(8,128)(2,1)S(1)} %add_convert_fusion.13), channel_id=1, source_target_pairs={{0,16},{8,24},{16,0},{24,8},{1,17},{9,25},{17,1},{25,9},{2,18},{10... | collective-permute-start | bytes 344072 | tf_op jit(solution)/shard_map/ppermute | solution.py:109
  179.7 13.5 %collective-permute-start.43 = (bf16[2,2,128,768]{3,2,1,0:T(8,128)(2,1)S(1)}, bf16[2,2,128,768]{3,2,1,0:T(8,128)(2,1)S(1)}, u32[]{:S(2)}, u32[]{:S(2)}) collective-permute-start(bf16[2,2,128,768]{3,2,1,0:T(8,128)(2,1)S(1)} %pad_maximum_fusion.3), channel_id=1, source_target_pairs={{0,4},{1,3},{2,6},{3,1},{4,0},{5,7},{6,2},{7,5},{8,12},{9,11},{10,... | collective-permute-start | bytes 2359304 | tf_op jit(solution)/shard_map/ppermute | solution.py:106
  189.3 6.6 %collective-permute-start.48 = (bf16[2,96,512]{2,1,0:T(8,128)(2,1)S(1)}, bf16[2,96,512]{2,1,0:T(8,128)(2,1)S(1)}, u32[]{:S(2)}, u32[]{:S(2)}) collective-permute-start(bf16[2,96,512]{2,1,0:T(8,128)(2,1)S(1)} %add_convert_fusion.8.refs_0_), channel_id=1, source_target_pairs={{0,8},{8,0},{16,24},{24,16},{1,9},{9,1},{17,25},{25,17},{2,10},{10... | collective-permute-start | bytes 589832 | tf_op jit(solution)/shard_map/ppermute | solution.py:109
  190.6 6.6 %collective-permute-start.47 = (bf16[2,112,256]{2,1,0:T(8,128)(2,1)S(1)}, bf16[2,112,256]{2,1,0:T(8,128)(2,1)S(1)}, u32[]{:S(2)}, u32[]{:S(2)}) collective-permute-start(bf16[2,112,256]{2,1,0:T(8,128)(2,1)S(1)} %add_convert_fusion.12.refs_2_), channel_id=1, source_target_pairs={{0,8},{8,0},{16,24},{24,16},{1,9},{9,1},{17,25},{25,17},{2,10},{10... | collective-permute-start | bytes 344072 | tf_op jit(solution)/shard_map/ppermute | solution.py:109
  (30 other events, 192.3 us)

commit v4 on v3

--- a/solution.py
+++ b/solution.py
@@ -917,12 +917,12 @@
                 total = piece[rows:] if total is None else total + piece[rows:]
         first += count
     for r, out in enumerate(vectors):
-        out[...] = total[r : r + 1, : out.shape[1]]
+        out[...] = total[5 if r == 7 else r, : out.shape[0]]
 
 
 def first_end(place, rows, width, counts, pieces):
     shapes = [(rows, 3 * width), (rows, width)]
-    shapes += [(1, n * rows) for n in (1, 1, 1, 1, 3, 1, 4)]
+    shapes += [(n * rows,) for n in (1, 1, 1, 1, 3, 1, 4, 1)]
     pieces = pieces + [place.line.count]
     return place.line.call(
         functools.partial(first_end_kernel, place, rows, counts),
@@ -1216,8 +1216,6 @@
     for v in earlier:
         v.step()
     last.step()
-    if pair == 2:
-        second_reps.step()
     vector_sums = Scatter(
         *vector_grads(place, rows, 4 * place.heads * HD, sums_qkv, sums_back, sums_middle)
     )
@@ -1247,6 +1245,8 @@
             blocks[s] = got[k]
 
     going = pass_on(0)
+    if pair == 2:
+        second_reps.step()
     line.pause()
     vector_sums.step()
     last.step()
@@ -1288,7 +1288,6 @@
     output, grad_input = finish_tokens(place, layer_input, cotangent, vec, blocks)
     pieces = [p for r in reps for p in r.end()]
     grad_w_qkv, grad_w_out, *vector_outs = first_end(place, rows, width, counts, pieces)
-    vector_outs = [v.reshape(-1) for v in vector_outs]
     return (
         output,
         grad_input,
@@ -1297,7 +1296,6 @@
         grad_w_up,
         grad_w_down,
         *vector_outs,
-        vector_outs[5],
     )
 
 

time: 204 us -> 200 us (0.980)
  waiting for transfers between devices: 58.8 us -> 54.5 us
  starting transfers between devices: 45.1 us -> 47.6 us
    ppermute x13, waiting for transfers between devices: 23.2 us -> 16.9 us  [swap_rep(): return lax.ppermute(v, 'rep', [(i, i ^ mask) for i in range(self.reps)])]
    ppermute x16, waiting for transfers between devices: 19.9 us -> 22.2 us  [swap_phase(): return lax.ppermute(v, 'fsdp', [(i, to(i)) for i in range(self.shards)])]
    unnamed x68 -> x67, local copies, waits for them, and re-layouts: 8.79 us -> 7.19 us
  transfers between devices with their start and end apart: 49 -> 49, of which waited for: 20 -> 17; matrix products, arithmetic and copies ran while one was open for 2% -> 2% of each run, Pallas kernels for 38% -> 39%
where the time goes in v4:
time: 200 us; the launch traced here: 196 us
  Pallas kernels  80.6 us (40%)
  waiting for transfers between devices  54.5 us (27%)
  starting transfers between devices  47.6 us (24%)
  local copies, waits for them, and re-layouts  9.08 us (5%)
  other arithmetic  2.89 us (1%)
    pallas_call x28, Pallas kernels, call(): pl.pallas_call(kernel, grid=grid, in_specs=in_specs, out_specs=out_specs,...  80.6 us
    ppermute x16, waiting for transfers between devices, swap_phase(): return lax.ppermute(v, 'fsdp', [(i, to(i)) for i in range(self.shards)])  22.2 us
    ppermute x13, starting transfers between devices, swap_rep(): return lax.ppermute(v, 'rep', [(i, i ^ mask) for i in range(self.reps)])  19.4 us
    ppermute x16, starting transfers between devices, swap_phase(): return lax.ppermute(v, 'fsdp', [(i, to(i)) for i in range(self.shards)])  17.6 us
    ppermute x13, waiting for transfers between devices, swap_rep(): return lax.ppermute(v, 'rep', [(i, i ^ mask) for i in range(self.reps)])  16.9 us
    ppermute x6, waiting for transfers between devices, swap_slot(): return lax.ppermute(v, 'fsdp', [(i, to(i)) for i in range(self.shards)])  9.39 us
    ppermute x6, starting transfers between devices, swap_slot(): return lax.ppermute(v, 'fsdp', [(i, to(i)) for i in range(self.shards)])  7.95 us
    unnamed x67, local copies, waits for them, and re-layouts  7.19 us
  transfers between devices with their start and end apart: 49, of which 17 were waited for; matrix products, arithmetic and copies ran while one was open for 2% of the time, Pallas kernels for 39%

profile of v4, /device:TPU:0, one launch (start us, length us, event | category | flops | bytes accessed | tf_op | source)
XLA Modules:
  0.0 196.4 jit_solution(4185578771166098503)
XLA Ops:
  0.6 2.1 %split_input.1 = (bf16[128,768]{1,0:T(8,128)(2,1)}, bf16[128,768]{1,0:T(8,128)(2,1)}, bf16[128,768]{1,0:T(8,128)(2,1)}, bf16[128,768]{1,0:T(8,128)(2,1)}) custom-call(bf16[4,128,768]{2,1,0:T(8,128)(2,1)} %source.3), custom_call_target="tpu_custom_call" | custom-call | flops 23000000512 | bytes 71875000 | tf_op jit(solution)/shard_map/split_input/pallas_call | solution.py:149
  2.7 2.9 %collective-permute-start = (bf16[128,768]{1,0:T(8,128)(2,1)}, bf16[128,768]{1,0:T(8,128)(2,1)S(1)}, u32[]{:S(2)}, u32[]{:S(2)}) collective-permute-start(bf16[128,768]{1,0:T(8,128)(2,1)} %get-tuple-element.177), channel_id=1, source_target_pairs={{0,2},{1,5},{2,0},{3,7},{4,6},{5,1},{6,4},{7,3},{8,10},{9,13},{10,... | collective-permute-start | bytes 589832 | tf_op jit(solution)/shard_map/ppermute | solution.py:99
  5.6 1.5 collective-permute-start.1
  7.2 2.1 %collective-permute-start.3 = (bf16[128,768]{1,0:T(8,128)(2,1)}, bf16[128,768]{1,0:T(8,128)(2,1)S(1)}, u32[]{:S(2)}, u32[]{:S(2)}) collective-permute-start(bf16[128,768]{1,0:T(8,128)(2,1)} %get-tuple-element.176), channel_id=1, source_target_pairs={{0,8},{8,0},{16,24},{24,16},{1,9},{9,1},{17,25},{25,17},{2,10},{10... | collective-permute-start | bytes 589832 | tf_op jit(solution)/shard_map/ppermute | solution.py:109
  9.2 2.1 %split_cotangent.1 = (bf16[128,768]{1,0:T(8,128)(2,1)}, bf16[128,768]{1,0:T(8,128)(2,1)}, bf16[128,768]{1,0:T(8,128)(2,1)}, bf16[128,768]{1,0:T(8,128)(2,1)}) custom-call(bf16[4,128,768]{2,1,0:T(8,128)(2,1)} %cot.1), custom_call_target="tpu_custom_call" | custom-call | flops 23000000512 | bytes 71875000 | tf_op jit(solution)/shard_map/split_cotangent/pallas_call | solution.py:149
  12.4 2.7 %split_weights.1 = (bf16[96,1536]{1,0:T(8,128)(2,1)}, bf16[96,1536]{1,0:T(8,128)(2,1)}, bf16[112,1536]{1,0:T(8,128)(2,1)}, bf16[112,1536]{1,0:T(8,128)(2,1)}) custom-call(bf16[96,2304]{1,0:T(8,128)(2,1)} %w_qkv, bf16[96,768]{1,0:T(8,128)(2,1)} %w_out.1, bf16[96,3072]{1,0:T(8,128)(2,1)} %w_up.1, bf16[96,3072]{1,0:T(8,128)(2,1)} %w_down.1, ...), custom_call_target="tpu_custom_call" | custom-call | flops 23000000512 | bytes 71875000 | tf_op jit(solution)/shard_map/split_weights/pallas_call | solution.py:149
  16.9 1.9 collective-permute-start.4
  18.8 1.5 collective-permute-start.6
  20.3 1.3 collective-permute-start.7
  22.4 4.2 %collective-permute-done.6 = bf16[128,768]{1,0:T(8,128)(2,1)S(1)} collective-permute-done((bf16[128,768]{1,0:T(8,128)(2,1)S(1)}, bf16[128,768]{1,0:T(8,128)(2,1)S(1)}, u32[]{:S(2)}, u32[]{:S(2)}) %collective-permute-start.6) | collective-permute-done | bytes 196640 | tf_op jit(solution)/shard_map/ppermute | solution.py:99
  26.6 4.2 %collective-permute-done.8 = bf16[128,768]{1,0:T(8,128)(2,1)S(1)} collective-permute-done((bf16[128,768]{1,0:T(8,128)(2,1)S(1)}, bf16[128,768]{1,0:T(8,128)(2,1)S(1)}, u32[]{:S(2)}, u32[]{:S(2)}) %collective-permute-start.8) | collective-permute-done | bytes 196640 | tf_op jit(solution)/shard_map/ppermute | solution.py:99
  31.0 1.6 collective-permute-start.12
  32.7 1.6 collective-permute-start.10
  34.3 1.3 collective-permute-start.11
  36.5 10.3 %collective-permute-done.12.rest_1_ = bf16[224,1536]{1,0:T(8,128)(2,1)S(1)} collective-permute-done((bf16[224,1536]{1,0:T(8,128)(2,1)S(1)}, bf16[224,1536]{1,0:T(8,128)(2,1)S(1)}, u32[]{:S(2)}, u32[]{:S(2)}) %collective-permute-start.12) | collective-permute-done | bytes 688160 | tf_op jit(solution)/shard_map/ppermute | solution.py:106
  46.9 1.3 collective-permute-start.14
  49.1 1.5 collective-permute-done.16
  51.6 6.2 %collective-permute-done.14.rest_3_ = bf16[224,1536]{1,0:T(8,128)(2,1)S(1)} collective-permute-done((bf16[224,1536]{1,0:T(8,128)(2,1)S(1)}, bf16[224,1536]{1,0:T(8,128)(2,1)S(1)}, u32[]{:S(2)}, u32[]{:S(2)}) %collective-permute-start.14) | collective-permute-done | bytes 688160 | tf_op jit(solution)/shard_map/ppermute | solution.py:106
  58.7 1.6 collective-permute-start.20
  60.2 1.3 collective-permute-start.21
  61.6 1.2 copy-done.13
  64.4 6.9 %middle_1.1 = (bf16[2,512,768]{2,1,0:T(8,128)(2,1)S(1)}, bf16[2,512,768]{2,1,0:T(8,128)(2,1)S(1)}, bf16[2,512,768]{2,1,0:T(8,128)(2,1)S(1)}, bf16[2,512,768]{2,1,0:T(8,128)(2,1)S(1)}, f32[8,768]{1,0:T(8,128)S(1)}) custom-call(bf16[512,768]{1,0:T(8,128)(2,1)S(1)} %copy-done.5, bf16[512,768]{1,0:T(8,128)(2,1)S(1)} %copy-done.11, ...), custom_call_target="tpu_custom_call" | custom-call | flops 115000000 | bytes 359375 | tf_op jit(solution)/shard_map/middle_1/pallas_call | solution.py:149
  71.3 4.0 %back_1.1 = (bf16[2,512,768]{2,1,0:T(8,128)(2,1)S(1)}, bf16[1,2,512,768]{3,2,1,0:T(8,128)(2,1)S(1)}, f32[8,768]{1,0:T(8,128)S(1)}) custom-call(bf16[2,512,768]{2,1,0:T(8,128)(2,1)S(1)} %get-tuple-element.221.refs_0_, bf16[2,512,768]{2,1,0:T(8,128)(2,1)S(1)} %get-tuple-element.222.refs_1_, bf16[2,512,768]{2,1,0:T(8,128)(2,1)S(1)} %get-tuple-element.223.refs_2_, ...), custom_call_target="tpu_custom_call" | custom-call | flops 115000000 | bytes 359375 | tf_op jit(solution)/shard_map/back_1/pallas_call | solution.py:149
  81.1 6.3 %middle_0.1 = (bf16[2,512,768]{2,1,0:T(8,128)(2,1)S(1)}, bf16[2,512,768]{2,1,0:T(8,128)(2,1)S(1)}, bf16[2,512,768]{2,1,0:T(8,128)(2,1)S(1)}, bf16[2,512,768]{2,1,0:T(8,128)(2,1)S(1)}, f32[8,768]{1,0:T(8,128)S(1)}) custom-call(bf16[512,768]{1,0:T(8,128)(2,1)S(1)} %copy-done.3, bf16[512,768]{1,0:T(8,128)(2,1)S(1)} %copy-done.9, ...), custom_call_target="tpu_custom_call" | custom-call | flops 23000000512 | bytes 71875000 | tf_op jit(solution)/shard_map/middle_0/pallas_call | solution.py:149
  87.4 5.7 %second_grads.1 = (bf16[2,192,1536]{2,1,0:T(8,128)(2,1)S(1)}, bf16[2,192,1536]{2,1,0:T(8,128)(2,1)S(1)}) custom-call(bf16[1024,768]{1,0:T(8,128)(2,1)S(1)} %bitcast.94, bf16[1024,768]{1,0:T(8,128)(2,1)S(1)} %bitcast.93, bf16[1024,768]{1,0:T(8,128)(2,1)S(1)} %bitcast.92, bf16[1024,768]{1,0:T(8,128)(2,1)S(1)} %bitcast.90, bf16[1024,768]{1,0:T(8,128)(2,1)S(1)} %bitcast.91, ...), custom_call_target="tpu_custom_call" | custom-call | flops 115000000 | bytes 359375 | tf_op jit(solution)/shard_map/second_grads/pallas_call | solution.py:149
  94.9 1.9 tables_first.1
  97.3 4.8 %front.1 = (bf16[2,512,768]{2,1,0:T(8,128)(2,1)S(1)}, bf16[2,512,128]{2,1,0:T(8,128)(2,1)S(1)}, bf16[2,512,128]{2,1,0:T(8,128)(2,1)S(1)}, bf16[2,512,128]{2,1,0:...) custom-call(bf16[512,768]{1,0:T(8,128)(2,1)S(1)} %copy-done.3, ...), custom_call_target="tpu_custom_call" | custom-call | flops 115000000 | bytes 359375 | tf_op jit(solution)/shard_map/front/pallas_call | solution.py:149
  102.1 8.7 %attention_0.1 = (bf16[2,512,128]{2,1,0:T(8,128)(2,1)S(1)}, bf16[2,512,384]{2,1,0:T(8,128)(2,1)S(1)}, f32[8,384]{1,0:T(8,128)S(1)}) custom-call(bf16[2,512,128]{2,1,0:T(8,128)(2,1)S(1)} %get-tuple-element.256.q_in, bf16[2,512,128]{2,1,0:T(8,128)(2,1)S(1)} %get-tuple-element.257.k_in, bf16[2,512,128]{2,1,0:T(8,128)(2,1)S(1)} %get-tuple-element.258.v_in, ...), custom_call_target="tpu_custom_call" | custom-call | flops 23000000512 | bytes 71875000 | tf_op jit(solution)/shard_map/attention_0/pallas_call | solution.py:149
  111.5 8.8 %attention_1.1 = (bf16[2,512,128]{2,1,0:T(8,128)(2,1)S(1)}, bf16[2,512,384]{2,1,0:T(8,128)(2,1)S(1)}, f32[8,384]{1,0:T(8,128)S(1)}) custom-call(bf16[2,512,128]{2,1,0:T(8,128)(2,1)S(1)} %get-tuple-element.262.q_in, bf16[2,512,128]{2,1,0:T(8,128)(2,1)S(1)} %get-tuple-element.263.k_in, bf16[2,512,128]{2,1,0:T(8,128)(2,1)S(1)} %get-tuple-element.264.v_in, ...), custom_call_target="tpu_custom_call" | custom-call | flops 23000000512 | bytes 71875000 | tf_op jit(solution)/shard_map/attention_1/pallas_call | solution.py:149
  121.3 2.9 %first_grads_0.1 = (bf16[2,192,1024]{2,1,0:T(8,128)(2,1)S(1)}, bf16[2,192,1024]{2,1,0:T(8,128)(2,1)S(1)}) custom-call(bf16[1024,768]{1,0:T(8,128)(2,1)S(1)} %bitcast.101, bf16[1024,384]{1,0:T(8,128)(2,1)S(1)} %bitcast.95, bf16[1024,384]{1,0:T(8,128)(2,1)S(1)} %bitcast.96, bf16[1024,128]{1,0:T(8,128)(2,1)S(1)} %bitcast.98, bf16[1024,128]{1,0:T(8,128)(2,1)S(1)} %bitcast.99, ...), custom_call_target="tpu_custom_call" | custom-call | flops 23000000512 | bytes 71875000 | tf_op jit(solution)/shard_map/first_grads_0/pallas_call | solution.py:149
  125.1 2.6 %collective-permute-start.37 = (bf16[2,96,1536]{2,1,0:T(8,128)(2,1)S(1)}, bf16[2,96,1536]{2,1,0:T(8,128)(2,1)S(1)}, u32[]{:S(2)}, u32[]{:S(2)}) collective-permute-start(bf16[2,96,1536]{2,1,0:T(8,128)(2,1)S(1)} %pad_maximum_fusion.4), channel_id=1, source_target_pairs={{0,16},{8,24},{16,0},{24,8},{1,17},{9,25},{17,1},{25,9},{2,18},{10... | collective-permute-start | bytes 1769480 | tf_op jit(solution)/shard_map/ppermute | solution.py:109
  127.8 8.6 %attention_2.1 = (bf16[2,512,128]{2,1,0:T(8,128)(2,1)S(1)}, bf16[2,512,384]{2,1,0:T(8,128)(2,1)S(1)}, f32[8,384]{1,0:T(8,128)S(1)}) custom-call(bf16[2,512,128]{2,1,0:T(8,128)(2,1)S(1)} %get-tuple-element.277.q_in, bf16[2,512,128]{2,1,0:T(8,128)(2,1)S(1)} %get-tuple-element.278.k_in, bf16[2,512,128]{2,1,0:T(8,128)(2,1)S(1)} %get-tuple-element.279.v_in, ...), custom_call_target="tpu_custom_call" | custom-call | flops 23000000512 | bytes 71875000 | tf_op jit(solution)/shard_map/attention_2/pallas_call | solution.py:149
  137.6 1.5 first_grads_1.1
  139.1 1.4 collective-permute-start.33
  140.5 8.0 %back_0.1 = (bf16[2,512,768]{2,1,0:T(8,128)(2,1)S(1)}, bf16[1,2,512,768]{3,2,1,0:T(8,128)(2,1)S(1)}, f32[8,768]{1,0:T(8,128)S(1)}) custom-call(bf16[2,512,768]{2,1,0:T(8,128)(2,1)S(1)} %get-tuple-element.286.refs_0_, bf16[2,512,768]{2,1,0:T(8,128)(2,1)S(1)} %get-tuple-element.241.refs_1_, bf16[2,512,768]{2,1,0:T(8,128)(2,1)S(1)} %get-tuple-element.240.refs_2_, ...), custom_call_target="tpu_custom_call" | custom-call | flops 2300000000 | bytes 7187500 | tf_op jit(solution)/shard_map/back_0/pallas_call | solution.py:149
  150.9 1.5 collective-permute-done.32
  153.2 1.6 collective-permute-start.42
  158.1 1.6 collective-permute-start.44
  162.4 1.2 collective-permute-start.41
  163.7 1.9 collective-permute-start.46
  165.6 14.0 %collective-permute-done.41 = bf16[2,112,256]{2,1,0:T(8,128)(2,1)S(1)} collective-permute-done((bf16[2,112,256]{2,1,0:T(8,128)(2,1)S(1)}, bf16[2,112,256]{2,1,0:T(8,128)(2,1)S(1)}, u32[]{:S(2)}, u32[]{:S(2)}) %collective-permute-start.41) | collective-permute-done | bytes 114720 | tf_op jit(solution)/shard_map/ppermute | solution.py:109
  180.7 1.4 collective-permute-start.43
  182.2 2.5 %collective-permute-start.48 = (bf16[2,96,512]{2,1,0:T(8,128)(2,1)S(1)}, bf16[2,96,512]{2,1,0:T(8,128)(2,1)S(1)}, u32[]{:S(2)}, u32[]{:S(2)}) collective-permute-start(bf16[2,96,512]{2,1,0:T(8,128)(2,1)S(1)} %add_convert_fusion.8.refs_0_), channel_id=1, source_target_pairs={{0,8},{8,0},{16,24},{24,16},{1,9},{9,1},{17,25},{25,17},{2,10},{10... | collective-permute-start | bytes 589832 | tf_op jit(solution)/shard_map/ppermute | solution.py:109
  184.8 1.9 collective-permute-done.45
  187.2 1.6 second_end.1
  188.8 4.0 %collective-permute-done.43 = bf16[2,2,128,768]{3,2,1,0:T(8,128)(2,1)S(1)} collective-permute-done((bf16[2,2,128,768]{3,2,1,0:T(8,128)(2,1)S(1)}, bf16[2,2,128,768]{3,2,1,0:T(8,128)(2,1)S(1)}, u32[]{:S(2)}, u32[]{:S(2)}) %collective-permute-start.43) | collective-permute-done | bytes 786464 | tf_op jit(solution)/shard_map/ppermute | solution.py:106
  192.9 2.1 %finish_tokens.1 = (bf16[4,128,768]{2,1,0:T(8,128)(2,1)}, bf16[4,128,768]{2,1,0:T(8,128)(2,1)}) custom-call(bf16[4,128,768]{2,1,0:T(8,128)(2,1)S(1)} %copy-done.16, bf16[4,128,768]{2,1,0:T(8,128)(2,1)S(1)} %copy-done.17, f32[8,768]{1,0:T(8,128)S(1)} %get-tuple-element.217.refs_4_.refs_3_.refs_9_.vec, bf16[2,128,768]{2,1,0:T(8,128)(2,1)S(1)} %get-tuple-element.338.rest_0_, ...), custom_call_target="tpu_custom_call" | custom-call | flops 23000000512 | bytes 71875000 | tf_op jit(solution)/shard_map/finish_tokens/pallas_call | solution.py:149
  195.0 1.2 first_end.1
  (191 shorter events, 31.3 us)
Async XLA Ops:
  2.7 12.5 %collective-permute-start = (bf16[128,768]{1,0:T(8,128)(2,1)}, bf16[128,768]{1,0:T(8,128)(2,1)S(1)}, u32[]{:S(2)}, u32[]{:S(2)}) collective-permute-start(bf16[128,768]{1,0:T(8,128)(2,1)} %get-tuple-element.177), channel_id=1, source_target_pairs={{0,2},{1,5},{2,0},{3,7},{4,6},{5,1},{6,4},{7,3},{8,10},{9,13},{10,... | collective-permute-start | bytes 589832 | tf_op jit(solution)/shard_map/ppermute | solution.py:99
  5.6 9.6 %collective-permute-start.1 = (bf16[128,768]{1,0:T(8,128)(2,1)}, bf16[128,768]{1,0:T(8,128)(2,1)S(1)}, u32[]{:S(2)}, u32[]{:S(2)}) collective-permute-start(bf16[128,768]{1,0:T(8,128)(2,1)} %get-tuple-element.178), channel_id=1, source_target_pairs={{0,4},{1,3},{2,6},{3,1},{4,0},{5,7},{6,2},{7,5},{8,12},{9,11},{10,... | collective-permute-start | bytes 589832 | tf_op jit(solution)/shard_map/ppermute | solution.py:99
  7.2 9.0 %collective-permute-start.2 = (bf16[128,768]{1,0:T(8,128)(2,1)}, bf16[128,768]{1,0:T(8,128)(2,1)S(1)}, u32[]{:S(2)}, u32[]{:S(2)}) collective-permute-start(bf16[128,768]{1,0:T(8,128)(2,1)} %get-tuple-element.179), channel_id=1, source_target_pairs={{0,6},{1,7},{2,4},{3,5},{4,2},{5,3},{6,0},{7,1},{8,14},{9,15},{10,... | collective-permute-start | bytes 589832 | tf_op jit(solution)/shard_map/ppermute | solution.py:99
  7.2 9.0 %collective-permute-start.3 = (bf16[128,768]{1,0:T(8,128)(2,1)}, bf16[128,768]{1,0:T(8,128)(2,1)S(1)}, u32[]{:S(2)}, u32[]{:S(2)}) collective-permute-start(bf16[128,768]{1,0:T(8,128)(2,1)} %get-tuple-element.176), channel_id=1, source_target_pairs={{0,8},{8,0},{16,24},{24,16},{1,9},{9,1},{17,25},{25,17},{2,10},{10... | collective-permute-start | bytes 589832 | tf_op jit(solution)/shard_map/ppermute | solution.py:109
  16.3 6.0 %collective-permute-start.9 = (bf16[512,768]{1,0:T(8,128)(2,1)S(1)}, bf16[512,768]{1,0:T(8,128)(2,1)S(1)}, u32[]{:S(2)}, u32[]{:S(2)}) collective-permute-start(bf16[512,768]{1,0:T(8,128)(2,1)S(1)} %get-tuple-element.249.refs_0_), channel_id=1, source_target_pairs={{0,1},{1,0},{2,3},{3,2},{4,5},{5,4},{6,7},{7,6},{8,9},{9,8},{10,11... | collective-permute-start | bytes 2359304 | tf_op jit(solution)/shard_map/ppermute | solution.py:92
  16.4 5.2 %collective-permute-start.5 = (bf16[112,1536]{1,0:T(8,128)(2,1)S(1)}, bf16[112,1536]{1,0:T(8,128)(2,1)S(1)}, u32[]{:S(2)}, u32[]{:S(2)}) collective-permute-start(bf16[112,1536]{1,0:T(8,128)(2,1)S(1)} %copy-done.24), channel_id=1, source_target_pairs={{0,1},{1,0},{2,3},{3,2},{4,5},{5,4},{6,7},{7,6},{8,9},{9,8},{10,11... | collective-permute-start | bytes 1032200 | tf_op jit(solution)/shard_map/ppermute | solution.py:92
  16.9 15.6 %collective-permute-start.4 = (bf16[384,768]{1,0:T(8,128)(2,1)S(1)}, bf16[384,768]{1,0:T(8,128)(2,1)S(1)}, u32[]{:S(2)}, u32[]{:S(2)}) collective-permute-start(bf16[384,768]{1,0:T(8,128)(2,1)S(1)} %get-tuple-element.364), channel_id=1, source_target_pairs={{0,8},{8,0},{16,24},{24,16},{1,9},{9,1},{17,25},{25,17},{2,10},{10... | collective-permute-start | bytes 1769480 | tf_op jit(solution)/shard_map/ppermute | solution.py:109
  18.8 7.8 %collective-permute-start.6 = (bf16[128,768]{1,0:T(8,128)(2,1)S(1)}, bf16[128,768]{1,0:T(8,128)(2,1)S(1)}, u32[]{:S(2)}, u32[]{:S(2)}) collective-permute-start(bf16[128,768]{1,0:T(8,128)(2,1)S(1)} %copy-done.28), channel_id=1, source_target_pairs={{0,2},{1,5},{2,0},{3,7},{4,6},{5,1},{6,4},{7,3},{8,10},{9,13},{10,... | collective-permute-start | bytes 589832 | tf_op jit(solution)/shard_map/ppermute | solution.py:99
  20.3 6.3 %collective-permute-start.7 = (bf16[128,768]{1,0:T(8,128)(2,1)S(1)}, bf16[128,768]{1,0:T(8,128)(2,1)S(1)}, u32[]{:S(2)}, u32[]{:S(2)}) collective-permute-start(bf16[128,768]{1,0:T(8,128)(2,1)S(1)} %copy-done.27), channel_id=1, source_target_pairs={{0,4},{1,3},{2,6},{3,1},{4,0},{5,7},{6,2},{7,5},{8,12},{9,11},{10,... | collective-permute-start | bytes 589832 | tf_op jit(solution)/shard_map/ppermute | solution.py:99
  21.6 9.2 %collective-permute-start.8 = (bf16[128,768]{1,0:T(8,128)(2,1)S(1)}, bf16[128,768]{1,0:T(8,128)(2,1)S(1)}, u32[]{:S(2)}, u32[]{:S(2)}) collective-permute-start(bf16[128,768]{1,0:T(8,128)(2,1)S(1)} %copy-done.26), channel_id=1, source_target_pairs={{0,6},{1,7},{2,4},{3,5},{4,2},{5,3},{6,0},{7,1},{8,14},{9,15},{10,... | collective-permute-start | bytes 589832 | tf_op jit(solution)/shard_map/ppermute | solution.py:99
  30.9 4.8 %collective-permute-start.13 = (bf16[512,768]{1,0:T(8,128)(2,1)S(1)}, bf16[512,768]{1,0:T(8,128)(2,1)S(1)}, u32[]{:S(2)}, u32[]{:S(2)}) collective-permute-start(bf16[512,768]{1,0:T(8,128)(2,1)S(1)} %constant_dynamic-update-slice_fusion.9.refs_2_.refs_6_.refs_0_.refs_4_), channel_id=1, source_target_pairs={{0,1},{1,0},{2,3},{3,2},{4,5},{5,4},{6,7},{7,6},{8,9},{9,8},{10,11... | collective-permute-start | bytes 2359304 | tf_op jit(solution)/shard_map/ppermute | solution.py:92
  31.0 15.9 %collective-permute-start.12 = (bf16[224,1536]{1,0:T(8,128)(2,1)S(1)}, bf16[224,1536]{1,0:T(8,128)(2,1)S(1)}, u32[]{:S(2)}, u32[]{:S(2)}) collective-permute-start(bf16[224,1536]{1,0:T(8,128)(2,1)S(1)} %constant_dynamic-update-slice_fusion.7.rest_0_), channel_id=1, source_target_pairs={{0,2},{1,5},{2,0},{3,7},{4,6},{5,1},{6,4},{7,3},{8,10},{9,13},{10,... | collective-permute-start | bytes 2064392 | tf_op jit(solution)/shard_map/ppermute | solution.py:106
  32.6 15.6 %collective-permute-start.15 = (bf16[512,768]{1,0:T(8,128)(2,1)S(1)}, bf16[512,768]{1,0:T(8,128)(2,1)S(1)}, u32[]{:S(2)}, u32[]{:S(2)}) collective-permute-start(bf16[512,768]{1,0:T(8,128)(2,1)S(1)} %constant_dynamic-update-slice_fusion.13.refs_0_), channel_id=1, source_target_pairs={{0,1},{1,0},{2,3},{3,2},{4,5},{5,4},{6,7},{7,6},{8,9},{9,8},{10,11... | collective-permute-start | bytes 2359304 | tf_op jit(solution)/shard_map/ppermute | solution.py:92
  32.7 25.9 %collective-permute-start.10 = (bf16[512,768]{1,0:T(8,128)(2,1)S(1)}, bf16[512,768]{1,0:T(8,128)(2,1)S(1)}, u32[]{:S(2)}, u32[]{:S(2)}) collective-permute-start(bf16[512,768]{1,0:T(8,128)(2,1)S(1)} %constant_dynamic-update-slice_fusion.9.refs_2_.refs_6_.refs_0_.refs_4_), channel_id=1, source_target_pairs={{0,8},{8,0},{16,24},{24,16},{1,9},{9,1},{17,25},{25,17},{2,10},{10... | collective-permute-start | bytes 2359304 | tf_op jit(solution)/shard_map/ppermute | solution.py:109
  34.3 16.4 %collective-permute-start.11 = (bf16[224,1536]{1,0:T(8,128)(2,1)S(1)}, bf16[224,1536]{1,0:T(8,128)(2,1)S(1)}, u32[]{:S(2)}, u32[]{:S(2)}) collective-permute-start(bf16[224,1536]{1,0:T(8,128)(2,1)S(1)} %constant_dynamic-update-slice_fusion.7.rest_0_), channel_id=1, source_target_pairs={{0,4},{1,3},{2,6},{3,1},{4,0},{5,7},{6,2},{7,5},{8,12},{9,11},{10,... | collective-permute-start | bytes 2064392 | tf_op jit(solution)/shard_map/ppermute | solution.py:106
  46.9 10.9 %collective-permute-start.14 = (bf16[224,1536]{1,0:T(8,128)(2,1)S(1)}, bf16[224,1536]{1,0:T(8,128)(2,1)S(1)}, u32[]{:S(2)}, u32[]{:S(2)}) collective-permute-start(bf16[224,1536]{1,0:T(8,128)(2,1)S(1)} %collective-permute-done.12.rest_1_), channel_id=1, source_target_pairs={{0,4},{1,3},{2,6},{3,1},{4,0},{5,7},{6,2},{7,5},{8,12},{9,11},{10,... | collective-permute-start | bytes 2064392 | tf_op jit(solution)/shard_map/ppermute | solution.py:106
  49.1 1.6 collective-permute-start.16
  58.7 5.7 %collective-permute-start.17 = (bf16[512,768]{1,0:T(8,128)(2,1)S(1)}, bf16[512,768]{1,0:T(8,128)(2,1)S(1)}, u32[]{:S(2)}, u32[]{:S(2)}) collective-permute-start(bf16[512,768]{1,0:T(8,128)(2,1)S(1)} %collective-permute-done.10.refs_2_.refs_8_), channel_id=1, source_target_pairs={{0,1},{1,0},{2,3},{3,2},{4,5},{5,4},{6,7},{7,6},{8,9},{9,8},{10,11... | collective-permute-start | bytes 2359304 | tf_op jit(solution)/shard_map/ppermute | solution.py:92
  58.7 17.3 %collective-permute-start.20 = (bf16[192,1536]{1,0:T(8,128)(2,1)S(1)}, bf16[192,1536]{1,0:T(8,128)(2,1)}, u32[]{:S(2)}, u32[]{:S(2)}) collective-permute-start(bf16[192,1536]{1,0:T(8,128)(2,1)S(1)} %constant_dynamic-update-slice_fusion.15.rest_0_), channel_id=1, source_target_pairs={{0,2},{1,5},{2,0},{3,7},{4,6},{5,1},{6,4},{7,3},{8,10},{9,13},{10,... | collective-permute-start | bytes 1769480 | tf_op jit(solution)/shard_map/ppermute | solution.py:106
  60.2 15.8 %collective-permute-start.21 = (bf16[192,1536]{1,0:T(8,128)(2,1)S(1)}, bf16[192,1536]{1,0:T(8,128)(2,1)}, u32[]{:S(2)}, u32[]{:S(2)}) collective-permute-start(bf16[192,1536]{1,0:T(8,128)(2,1)S(1)} %constant_dynamic-update-slice_fusion.15.rest_0_), channel_id=1, source_target_pairs={{0,4},{1,3},{2,6},{3,1},{4,0},{5,7},{6,2},{7,5},{8,12},{9,11},{10,... | collective-permute-start | bytes 1769480 | tf_op jit(solution)/shard_map/ppermute | solution.py:106
  75.4 2.4 %collective-permute-start.18 = (bf16[512,768]{1,0:T(8,128)(2,1)S(1)}, bf16[512,768]{1,0:T(8,128)(2,1)S(1)}, u32[]{:S(2)}, u32[]{:S(2)}) collective-permute-start(bf16[512,768]{1,0:T(8,128)(2,1)S(1)} %get-tuple-element.349), channel_id=1, source_target_pairs={{0,1},{1,0},{2,3},{3,2},{4,5},{5,4},{6,7},{7,6},{8,9},{9,8},{10,11... | collective-permute-start | bytes 2359304 | tf_op jit(solution)/shard_map/ppermute | solution.py:92
  75.5 3.4 %collective-permute-start.19 = (bf16[512,768]{1,0:T(8,128)(2,1)S(1)}, bf16[512,768]{1,0:T(8,128)(2,1)S(1)}, u32[]{:S(2)}, u32[]{:S(2)}) collective-permute-start(bf16[512,768]{1,0:T(8,128)(2,1)S(1)} %get-tuple-element.348), channel_id=1, source_target_pairs={{0,1},{1,0},{2,3},{3,2},{4,5},{5,4},{6,7},{7,6},{8,9},{9,8},{10,11... | collective-permute-start | bytes 2359304 | tf_op jit(solution)/shard_map/ppermute | solution.py:92
  76.0 18.9 %collective-permute-start.22 = (bf16[192,1536]{1,0:T(8,128)(2,1)}, bf16[192,1536]{1,0:T(8,128)(2,1)S(1)}, u32[]{:S(2)}, u32[]{:S(2)}) collective-permute-start(bf16[192,1536]{1,0:T(8,128)(2,1)} %collective-permute-done.20.rest_1_), channel_id=1, source_target_pairs={{0,4},{1,3},{2,6},{3,1},{4,0},{5,7},{6,2},{7,5},{8,12},{9,11},{10,... | collective-permute-start | bytes 1769480 | tf_op jit(solution)/shard_map/ppermute | solution.py:106
  79.4 15.4 %collective-permute-start.23 = (bf16[384,768]{1,0:T(8,128)(2,1)S(1)}, bf16[384,768]{1,0:T(8,128)(2,1)S(1)}, u32[]{:S(2)}, u32[]{:S(2)}) collective-permute-start(bf16[384,768]{1,0:T(8,128)(2,1)S(1)} %slice.232), channel_id=1, source_target_pairs={{0,8},{8,0},{16,24},{24,16},{1,9},{9,1},{17,25},{25,17},{2,10},{10... | collective-permute-start | bytes 1769480 | tf_op jit(solution)/shard_map/ppermute | solution.py:109
  93.2 17.7 %collective-permute-start.25 = (bf16[2,192,1536]{2,1,0:T(8,128)(2,1)S(1)}, bf16[2,192,1536]{2,1,0:T(8,128)(2,1)S(1)}, u32[]{:S(2)}, u32[]{:S(2)}) collective-permute-start(bf16[2,192,1536]{2,1,0:T(8,128)(2,1)S(1)} %get-tuple-element.255), channel_id=1, source_target_pairs={{0,4},{1,3},{2,6},{3,1},{4,0},{5,7},{6,2},{7,5},{8,12},{9,11},{10,... | collective-permute-start | bytes 3538952 | tf_op jit(solution)/shard_map/ppermute | solution.py:106
  96.8 24.4 %collective-permute-start.24 = (bf16[640,768]{1,0:T(8,128)(2,1)S(1)}, bf16[640,768]{1,0:T(8,128)(2,1)S(1)}, u32[]{:S(2)}, u32[]{:S(2)}) collective-permute-start(bf16[640,768]{1,0:T(8,128)(2,1)S(1)} %pad_maximum_fusion.1), channel_id=1, source_target_pairs={{0,8},{8,0},{16,24},{24,16},{1,9},{9,1},{17,25},{25,17},{2,10},{10... | collective-permute-start | bytes 2949128 | tf_op jit(solution)/shard_map/ppermute | solution.py:109
  111.0 9.9 %collective-permute-start.26 = (bf16[192,1536]{1,0:T(8,128)(2,1)S(1)}, bf16[192,1536]{1,0:T(8,128)(2,1)S(1)}, u32[]{:S(2)}, u32[]{:S(2)}) collective-permute-start(bf16[192,1536]{1,0:T(8,128)(2,1)S(1)} %fusion.3), channel_id=1, source_target_pairs={{0,2},{1,5},{2,0},{3,7},{4,6},{5,1},{6,4},{7,3},{8,10},{9,13},{10,... | collective-permute-start | bytes 1769480 | tf_op jit(solution)/shard_map/ppermute | solution.py:106
  121.2 3.8 %collective-permute-start.28 = (bf16[96,1536]{1,0:T(8,128)(2,1)S(1)}, bf16[96,1536]{1,0:T(8,128)(2,1)S(1)}, u32[]{:S(2)}, u32[]{:S(2)}) collective-permute-start(bf16[96,1536]{1,0:T(8,128)(2,1)S(1)} %get-tuple-element.359), channel_id=1, source_target_pairs={{0,1},{1,0},{2,3},{3,2},{4,5},{5,4},{6,7},{7,6},{8,9},{9,8},{10,11... | collective-permute-start | bytes 884744 | tf_op jit(solution)/shard_map/ppermute | solution.py:92
  124.2 12.2 %collective-permute-start.27 = (bf16[2,192,1024]{2,1,0:T(8,128)(2,1)S(1)}, bf16[2,192,1024]{2,1,0:T(8,128)(2,1)S(1)}, u32[]{:S(2)}, u32[]{:S(2)}) collective-permute-start(bf16[2,192,1024]{2,1,0:T(8,128)(2,1)S(1)} %get-tuple-element.273), channel_id=1, source_target_pairs={{0,4},{1,3},{2,6},{3,1},{4,0},{5,7},{6,2},{7,5},{8,12},{9,11},{10,... | collective-permute-start | bytes 2359304 | tf_op jit(solution)/shard_map/ppermute | solution.py:106
  125.1 30.5 %collective-permute-start.37 = (bf16[2,96,1536]{2,1,0:T(8,128)(2,1)S(1)}, bf16[2,96,1536]{2,1,0:T(8,128)(2,1)S(1)}, u32[]{:S(2)}, u32[]{:S(2)}) collective-permute-start(bf16[2,96,1536]{2,1,0:T(8,128)(2,1)S(1)} %pad_maximum_fusion.4), channel_id=1, source_target_pairs={{0,16},{8,24},{16,0},{24,8},{1,17},{9,25},{17,1},{25,9},{2,18},{10... | collective-permute-start | bytes 1769480 | tf_op jit(solution)/shard_map/ppermute | solution.py:109
  136.5 12.7 %collective-permute-start.31 = (bf16[192,1024]{1,0:T(8,128)(2,1)S(1)}, bf16[192,1024]{1,0:T(8,128)(2,1)S(1)}, u32[]{:S(2)}, u32[]{:S(2)}) collective-permute-start(bf16[192,1024]{1,0:T(8,128)(2,1)S(1)} %fusion.4), channel_id=1, source_target_pairs={{0,2},{1,5},{2,0},{3,7},{4,6},{5,1},{6,4},{7,3},{8,10},{9,13},{10,... | collective-permute-start | bytes 1179656 | tf_op jit(solution)/shard_map/ppermute | solution.py:106
  139.1 10.3 %collective-permute-start.33 = (bf16[2,192,512]{2,1,0:T(8,128)(2,1)S(1)}, bf16[2,192,512]{2,1,0:T(8,128)(2,1)S(1)}, u32[]{:S(2)}, u32[]{:S(2)}) collective-permute-start(bf16[2,192,512]{2,1,0:T(8,128)(2,1)S(1)} %get-tuple-element.291), channel_id=1, source_target_pairs={{0,4},{1,3},{2,6},{3,1},{4,0},{5,7},{6,2},{7,5},{8,12},{9,11},{10,... | collective-permute-start | bytes 1179656 | tf_op jit(solution)/shard_map/ppermute | solution.py:106
  148.7 4.5 %collective-permute-start.29 = (bf16[512,768]{1,0:T(8,128)(2,1)S(1)}, bf16[512,768]{1,0:T(8,128)(2,1)S(1)}, u32[]{:S(2)}, u32[]{:S(2)}) collective-permute-start(bf16[512,768]{1,0:T(8,128)(2,1)S(1)} %get-tuple-element.345), channel_id=1, source_target_pairs={{0,1},{1,0},{2,3},{3,2},{4,5},{5,4},{6,7},{7,6},{8,9},{9,8},{10,11... | collective-permute-start | bytes 2359304 | tf_op jit(solution)/shard_map/ppermute | solution.py:92
  148.8 6.1 %collective-permute-start.30 = (bf16[512,768]{1,0:T(8,128)(2,1)S(1)}, bf16[512,768]{1,0:T(8,128)(2,1)S(1)}, u32[]{:S(2)}, u32[]{:S(2)}) collective-permute-start(bf16[512,768]{1,0:T(8,128)(2,1)S(1)} %get-tuple-element.344), channel_id=1, source_target_pairs={{0,1},{1,0},{2,3},{3,2},{4,5},{5,4},{6,7},{7,6},{8,9},{9,8},{10,11... | collective-permute-start | bytes 2359304 | tf_op jit(solution)/shard_map/ppermute | solution.py:92
  149.5 8.4 %collective-permute-start.35 = (bf16[192,512]{1,0:T(8,128)(2,1)S(1)}, bf16[192,512]{1,0:T(8,128)(2,1)S(1)}, u32[]{:S(2)}, u32[]{:S(2)}) collective-permute-start(bf16[192,512]{1,0:T(8,128)(2,1)S(1)} %fusion.5), channel_id=1, source_target_pairs={{0,2},{1,5},{2,0},{3,7},{4,6},{5,1},{6,4},{7,3},{8,10},{9,13},{10,... | collective-permute-start | bytes 589832 | tf_op jit(solution)/shard_map/ppermute | solution.py:106
  150.7 1.8 collective-permute-start.32
  152.4 4.3 %collective-permute-start.36 = (bf16[2,32,512]{2,1,0:T(8,128)(2,1)S(1)}, bf16[2,32,512]{2,1,0:T(8,128)(2,1)S(1)}, u32[]{:S(2)}, u32[]{:S(2)}) collective-permute-start(bf16[2,32,512]{2,1,0:T(8,128)(2,1)S(1)} %get-tuple-element.299), channel_id=1, source_target_pairs={{0,4},{1,3},{2,6},{3,1},{4,0},{5,7},{6,2},{7,5},{8,12},{9,11},{10,... | collective-permute-start | bytes 196616 | tf_op jit(solution)/shard_map/ppermute | solution.py:106
  153.2 10.5 %collective-permute-start.42 = (bf16[2,96,512]{2,1,0:T(8,128)(2,1)S(1)}, bf16[2,96,512]{2,1,0:T(8,128)(2,1)S(1)}, u32[]{:S(2)}, u32[]{:S(2)}) collective-permute-start(bf16[2,96,512]{2,1,0:T(8,128)(2,1)S(1)} %broadcast_select_fusion), channel_id=1, source_target_pairs={{0,8},{8,0},{16,24},{24,16},{1,9},{9,1},{17,25},{25,17},{2,10},{10... | collective-permute-start | bytes 589832 | tf_op jit(solution)/shard_map/ppermute | solution.py:109
  156.7 4.2 %collective-permute-start.39 = (bf16[32,512]{1,0:T(8,128)(2,1)S(1)}, bf16[32,512]{1,0:T(8,128)(2,1)S(1)}, u32[]{:S(2)}, u32[]{:S(2)}) collective-permute-start(bf16[32,512]{1,0:T(8,128)(2,1)S(1)} %fusion.8), channel_id=1, source_target_pairs={{0,2},{1,5},{2,0},{3,7},{4,6},{5,1},{6,4},{7,3},{8,10},{9,13},{10,... | collective-permute-start | bytes 98312 | tf_op jit(solution)/shard_map/ppermute | solution.py:106
  158.1 29.1 %collective-permute-start.44 = (bf16[2,96,1536]{2,1,0:T(8,128)(2,1)S(1)}, bf16[2,96,1536]{2,1,0:T(8,128)(2,1)S(1)}, u32[]{:S(2)}, u32[]{:S(2)}) collective-permute-start(bf16[2,96,1536]{2,1,0:T(8,128)(2,1)S(1)} %add_convert_fusion.1), channel_id=1, source_target_pairs={{0,8},{8,0},{16,24},{24,16},{1,9},{9,1},{17,25},{25,17},{2,10},{10... | collective-permute-start | bytes 1769480 | tf_op jit(solution)/shard_map/ppermute | solution.py:109
  159.8 20.8 %collective-permute-start.34 = (bf16[2,2,128,768]{3,2,1,0:T(8,128)(2,1)S(1)}, bf16[2,2,128,768]{3,2,1,0:T(8,128)(2,1)S(1)}, u32[]{:S(2)}, u32[]{:S(2)}) collective-permute-start(bf16[2,2,128,768]{3,2,1,0:T(8,128)(2,1)S(1)} %pad_maximum_fusion.2), channel_id=1, source_target_pairs={{0,2},{1,5},{2,0},{3,7},{4,6},{5,1},{6,4},{7,3},{8,10},{9,13},{10,... | collective-permute-start | bytes 2359304 | tf_op jit(solution)/shard_map/ppermute | solution.py:106
  161.0 1.4 collective-permute-start.40
  162.4 17.2 %collective-permute-start.41 = (bf16[2,112,256]{2,1,0:T(8,128)(2,1)S(1)}, bf16[2,112,256]{2,1,0:T(8,128)(2,1)S(1)}, u32[]{:S(2)}, u32[]{:S(2)}) collective-permute-start(bf16[2,112,256]{2,1,0:T(8,128)(2,1)S(1)} %broadcast_select_fusion.1), channel_id=1, source_target_pairs={{0,8},{8,0},{16,24},{24,16},{1,9},{9,1},{17,25},{25,17},{2,10},{10... | collective-permute-start | bytes 344072 | tf_op jit(solution)/shard_map/ppermute | solution.py:109
  163.7 18.4 %collective-permute-start.46 = (bf16[2,96,512]{2,1,0:T(8,128)(2,1)S(1)}, bf16[2,96,512]{2,1,0:T(8,128)(2,1)S(1)}, u32[]{:S(2)}, u32[]{:S(2)}) collective-permute-start(bf16[2,96,512]{2,1,0:T(8,128)(2,1)S(1)} %add_convert_fusion.9), channel_id=1, source_target_pairs={{0,16},{8,24},{16,0},{24,8},{1,17},{9,25},{17,1},{25,9},{2,18},{10... | collective-permute-start | bytes 589832 | tf_op jit(solution)/shard_map/ppermute | solution.py:109
  179.6 7.1 %collective-permute-start.45 = (bf16[2,112,256]{2,1,0:T(8,128)(2,1)S(1)}, bf16[2,112,256]{2,1,0:T(8,128)(2,1)S(1)}, u32[]{:S(2)}, u32[]{:S(2)}) collective-permute-start(bf16[2,112,256]{2,1,0:T(8,128)(2,1)S(1)} %add_convert_fusion.13), channel_id=1, source_target_pairs={{0,16},{8,24},{16,0},{24,8},{1,17},{9,25},{17,1},{25,9},{2,18},{10... | collective-permute-start | bytes 344072 | tf_op jit(solution)/shard_map/ppermute | solution.py:109
  180.7 12.1 %collective-permute-start.43 = (bf16[2,2,128,768]{3,2,1,0:T(8,128)(2,1)S(1)}, bf16[2,2,128,768]{3,2,1,0:T(8,128)(2,1)S(1)}, u32[]{:S(2)}, u32[]{:S(2)}) collective-permute-start(bf16[2,2,128,768]{3,2,1,0:T(8,128)(2,1)S(1)} %pad_maximum_fusion.3), channel_id=1, source_target_pairs={{0,4},{1,3},{2,6},{3,1},{4,0},{5,7},{6,2},{7,5},{8,12},{9,11},{10,... | collective-permute-start | bytes 2359304 | tf_op jit(solution)/shard_map/ppermute | solution.py:106
  182.2 12.7 %collective-permute-start.48 = (bf16[2,96,512]{2,1,0:T(8,128)(2,1)S(1)}, bf16[2,96,512]{2,1,0:T(8,128)(2,1)S(1)}, u32[]{:S(2)}, u32[]{:S(2)}) collective-permute-start(bf16[2,96,512]{2,1,0:T(8,128)(2,1)S(1)} %add_convert_fusion.8.refs_0_), channel_id=1, source_target_pairs={{0,8},{8,0},{16,24},{24,16},{1,9},{9,1},{17,25},{25,17},{2,10},{10... | collective-permute-start | bytes 589832 | tf_op jit(solution)/shard_map/ppermute | solution.py:109
  186.8 8.2 %collective-permute-start.47 = (bf16[2,112,256]{2,1,0:T(8,128)(2,1)S(1)}, bf16[2,112,256]{2,1,0:T(8,128)(2,1)S(1)}, u32[]{:S(2)}, u32[]{:S(2)}) collective-permute-start(bf16[2,112,256]{2,1,0:T(8,128)(2,1)S(1)} %add_convert_fusion.12.refs_2_), channel_id=1, source_target_pairs={{0,8},{8,0},{16,24},{24,16},{1,9},{9,1},{17,25},{25,17},{2,10},{10... | collective-permute-start | bytes 344072 | tf_op jit(solution)/shard_map/ppermute | solution.py:109
  (30 other events, 199.8 us)

commit v5 on v4

--- a/solution.py
+++ b/solution.py
@@ -1245,8 +1245,6 @@
             blocks[s] = got[k]
 
     going = pass_on(0)
-    if pair == 2:
-        second_reps.step()
     line.pause()
     vector_sums.step()
     last.step()
@@ -1256,11 +1254,14 @@
     mine = jnp.concatenate([last.end(), vector_sums.end()], axis=1)
     line.hold(mine)
     reps.append(Reps(mine))
+    if pair == 2:
+        second_reps.step()
     line.pause()
     for r in reps[:-1]:
         r.step()
         line.pause()
     reps[-1].step()
+    line.pause()
     for phase in range(1, place.phases):
         passed(*going)
         going = pass_on(phase)

time: 200 us -> 199 us (level)
    unnamed x67 -> x75, local copies, waits for them, and re-layouts: 7.19 us -> 7.66 us
    pallas_call x28 -> x29, Pallas kernels: 80.6 us -> 80.5 us  [call(): pl.pallas_call(kernel, grid=grid, in_specs=in_specs, out_specs=out_specs,...]
  transfers between devices with their start and end apart: 49 -> 49, of which waited for: 17 -> 19; matrix products, arithmetic and copies ran while one was open for 2% -> 3% of each run, Pallas kernels for 39% -> 39%
where the time goes in v5:
time: 199 us; the launch traced here: 196 us
  Pallas kernels  80.5 us (40%)
  waiting for transfers between devices  53 us (27%)
  starting transfers between devices  46 us (23%)
  local copies, waits for them, and re-layouts  9.55 us (5%)
  other arithmetic  4.83 us (2%)
    pallas_call x29, Pallas kernels, call(): pl.pallas_call(kernel, grid=grid, in_specs=in_specs, out_specs=out_specs,...  80.5 us
    ppermute x16, waiting for transfers between devices, swap_phase(): return lax.ppermute(v, 'fsdp', [(i, to(i)) for i in range(self.shards)])  21.3 us
    ppermute x13, starting transfers between devices, swap_rep(): return lax.ppermute(v, 'rep', [(i, i ^ mask) for i in range(self.reps)])  19 us
    ppermute x16, starting transfers between devices, swap_phase(): return lax.ppermute(v, 'fsdp', [(i, to(i)) for i in range(self.shards)])  16.9 us
    ppermute x13, waiting for transfers between devices, swap_rep(): return lax.ppermute(v, 'rep', [(i, i ^ mask) for i in range(self.reps)])  16 us
    ppermute x6, waiting for transfers between devices, swap_slot(): return lax.ppermute(v, 'fsdp', [(i, to(i)) for i in range(self.shards)])  9.39 us
    ppermute x6, starting transfers between devices, swap_slot(): return lax.ppermute(v, 'fsdp', [(i, to(i)) for i in range(self.shards)])  7.95 us
    unnamed x75, local copies, waits for them, and re-layouts  7.66 us
  transfers between devices with their start and end apart: 49, of which 19 were waited for; matrix products, arithmetic and copies ran while one was open for 3% of the time, Pallas kernels for 39%

profile of v5, /device:TPU:0, one launch (start us, length us, event | category | flops | bytes accessed | tf_op | source)
XLA Modules:
  0.0 195.7 jit_solution(9560980510604049468)
XLA Ops:
  0.6 2.1 %split_input.1 = (bf16[128,768]{1,0:T(8,128)(2,1)}, bf16[128,768]{1,0:T(8,128)(2,1)}, bf16[128,768]{1,0:T(8,128)(2,1)}, bf16[128,768]{1,0:T(8,128)(2,1)}) custom-call(bf16[4,128,768]{2,1,0:T(8,128)(2,1)} %source.3), custom_call_target="tpu_custom_call" | custom-call | flops 23000000512 | bytes 71875000 | tf_op jit(solution)/shard_map/split_input/pallas_call | solution.py:149
  2.7 2.9 %collective-permute-start = (bf16[128,768]{1,0:T(8,128)(2,1)}, bf16[128,768]{1,0:T(8,128)(2,1)S(1)}, u32[]{:S(2)}, u32[]{:S(2)}) collective-permute-start(bf16[128,768]{1,0:T(8,128)(2,1)} %get-tuple-element.178), channel_id=1, source_target_pairs={{0,2},{1,5},{2,0},{3,7},{4,6},{5,1},{6,4},{7,3},{8,10},{9,13},{10,... | collective-permute-start | bytes 589832 | tf_op jit(solution)/shard_map/ppermute | solution.py:99
  5.6 1.5 collective-permute-start.1
  7.2 2.1 %collective-permute-start.3 = (bf16[128,768]{1,0:T(8,128)(2,1)}, bf16[128,768]{1,0:T(8,128)(2,1)S(1)}, u32[]{:S(2)}, u32[]{:S(2)}) collective-permute-start(bf16[128,768]{1,0:T(8,128)(2,1)} %get-tuple-element.177), channel_id=1, source_target_pairs={{0,8},{8,0},{16,24},{24,16},{1,9},{9,1},{17,25},{25,17},{2,10},{10... | collective-permute-start | bytes 589832 | tf_op jit(solution)/shard_map/ppermute | solution.py:109
  9.2 2.1 %split_cotangent.1 = (bf16[128,768]{1,0:T(8,128)(2,1)}, bf16[128,768]{1,0:T(8,128)(2,1)}, bf16[128,768]{1,0:T(8,128)(2,1)}, bf16[128,768]{1,0:T(8,128)(2,1)}) custom-call(bf16[4,128,768]{2,1,0:T(8,128)(2,1)} %cot.1), custom_call_target="tpu_custom_call" | custom-call | flops 23000000512 | bytes 71875000 | tf_op jit(solution)/shard_map/split_cotangent/pallas_call | solution.py:149
  12.4 2.7 %split_weights.1 = (bf16[96,1536]{1,0:T(8,128)(2,1)}, bf16[96,1536]{1,0:T(8,128)(2,1)}, bf16[112,1536]{1,0:T(8,128)(2,1)}, bf16[112,1536]{1,0:T(8,128)(2,1)}) custom-call(bf16[96,2304]{1,0:T(8,128)(2,1)} %w_qkv, bf16[96,768]{1,0:T(8,128)(2,1)} %w_out.1, bf16[96,3072]{1,0:T(8,128)(2,1)} %w_up.1, bf16[96,3072]{1,0:T(8,128)(2,1)} %w_down.1, ...), custom_call_target="tpu_custom_call" | custom-call | flops 23000000512 | bytes 71875000 | tf_op jit(solution)/shard_map/split_weights/pallas_call | solution.py:149
  16.9 1.9 collective-permute-start.4
  18.8 1.5 collective-permute-start.6
  20.3 1.3 collective-permute-start.7
  22.3 4.2 %collective-permute-done.6 = bf16[128,768]{1,0:T(8,128)(2,1)S(1)} collective-permute-done((bf16[128,768]{1,0:T(8,128)(2,1)S(1)}, bf16[128,768]{1,0:T(8,128)(2,1)S(1)}, u32[]{:S(2)}, u32[]{:S(2)}) %collective-permute-start.6) | collective-permute-done | bytes 196640 | tf_op jit(solution)/shard_map/ppermute | solution.py:99
  26.6 4.2 %collective-permute-done.8 = bf16[128,768]{1,0:T(8,128)(2,1)S(1)} collective-permute-done((bf16[128,768]{1,0:T(8,128)(2,1)S(1)}, bf16[128,768]{1,0:T(8,128)(2,1)S(1)}, u32[]{:S(2)}, u32[]{:S(2)}) %collective-permute-start.8) | collective-permute-done | bytes 196640 | tf_op jit(solution)/shard_map/ppermute | solution.py:99
  31.0 1.6 collective-permute-start.12
  32.7 1.6 collective-permute-start.10
  34.3 1.3 collective-permute-start.11
  36.5 10.3 %collective-permute-done.12.rest_1_ = bf16[224,1536]{1,0:T(8,128)(2,1)S(1)} collective-permute-done((bf16[224,1536]{1,0:T(8,128)(2,1)S(1)}, bf16[224,1536]{1,0:T(8,128)(2,1)S(1)}, u32[]{:S(2)}, u32[]{:S(2)}) %collective-permute-start.12) | collective-permute-done | bytes 688160 | tf_op jit(solution)/shard_map/ppermute | solution.py:106
  46.9 1.3 collective-permute-start.14
  49.1 1.5 collective-permute-done.16
  51.6 6.2 %collective-permute-done.14.rest_3_ = bf16[224,1536]{1,0:T(8,128)(2,1)S(1)} collective-permute-done((bf16[224,1536]{1,0:T(8,128)(2,1)S(1)}, bf16[224,1536]{1,0:T(8,128)(2,1)S(1)}, u32[]{:S(2)}, u32[]{:S(2)}) %collective-permute-start.14) | collective-permute-done | bytes 688160 | tf_op jit(solution)/shard_map/ppermute | solution.py:106
  58.7 1.6 collective-permute-start.20
  60.2 1.3 collective-permute-start.21
  61.6 1.2 copy-done.13
  64.4 6.9 %middle_1.1 = (bf16[2,512,768]{2,1,0:T(8,128)(2,1)S(1)}, bf16[2,512,768]{2,1,0:T(8,128)(2,1)S(1)}, bf16[2,512,768]{2,1,0:T(8,128)(2,1)S(1)}, bf16[2,512,768]{2,1,0:T(8,128)(2,1)S(1)}, f32[8,768]{1,0:T(8,128)S(1)}) custom-call(bf16[512,768]{1,0:T(8,128)(2,1)S(1)} %copy-done.5, bf16[512,768]{1,0:T(8,128)(2,1)S(1)} %copy-done.11, ...), custom_call_target="tpu_custom_call" | custom-call | flops 115000000 | bytes 359375 | tf_op jit(solution)/shard_map/middle_1/pallas_call | solution.py:149
  71.3 4.0 %back_1.1 = (bf16[2,512,768]{2,1,0:T(8,128)(2,1)S(1)}, bf16[1,2,512,768]{3,2,1,0:T(8,128)(2,1)S(1)}, f32[8,768]{1,0:T(8,128)S(1)}) custom-call(bf16[2,512,768]{2,1,0:T(8,128)(2,1)S(1)} %get-tuple-element.222.refs_0_, bf16[2,512,768]{2,1,0:T(8,128)(2,1)S(1)} %get-tuple-element.223.refs_1_, bf16[2,512,768]{2,1,0:T(8,128)(2,1)S(1)} %get-tuple-element.224.refs_2_, ...), custom_call_target="tpu_custom_call" | custom-call | flops 115000000 | bytes 359375 | tf_op jit(solution)/shard_map/back_1/pallas_call | solution.py:149
  81.1 6.3 %middle_0.1 = (bf16[2,512,768]{2,1,0:T(8,128)(2,1)S(1)}, bf16[2,512,768]{2,1,0:T(8,128)(2,1)S(1)}, bf16[2,512,768]{2,1,0:T(8,128)(2,1)S(1)}, bf16[2,512,768]{2,1,0:T(8,128)(2,1)S(1)}, f32[8,768]{1,0:T(8,128)S(1)}) custom-call(bf16[512,768]{1,0:T(8,128)(2,1)S(1)} %copy-done.3, bf16[512,768]{1,0:T(8,128)(2,1)S(1)} %copy-done.9, ...), custom_call_target="tpu_custom_call" | custom-call | flops 23000000512 | bytes 71875000 | tf_op jit(solution)/shard_map/middle_0/pallas_call | solution.py:149
  87.5 5.7 %second_grads.1 = (bf16[2,192,1536]{2,1,0:T(8,128)(2,1)S(1)}, bf16[2,192,1536]{2,1,0:T(8,128)(2,1)S(1)}) custom-call(bf16[1024,768]{1,0:T(8,128)(2,1)S(1)} %bitcast.94, bf16[1024,768]{1,0:T(8,128)(2,1)S(1)} %bitcast.93, bf16[1024,768]{1,0:T(8,128)(2,1)S(1)} %bitcast.92, bf16[1024,768]{1,0:T(8,128)(2,1)S(1)} %bitcast.90, bf16[1024,768]{1,0:T(8,128)(2,1)S(1)} %bitcast.91, ...), custom_call_target="tpu_custom_call" | custom-call | flops 115000000 | bytes 359375 | tf_op jit(solution)/shard_map/second_grads/pallas_call | solution.py:149
  94.9 1.9 tables_first.1
  97.3 4.8 %front.1 = (bf16[2,512,768]{2,1,0:T(8,128)(2,1)S(1)}, bf16[2,512,128]{2,1,0:T(8,128)(2,1)S(1)}, bf16[2,512,128]{2,1,0:T(8,128)(2,1)S(1)}, bf16[2,512,128]{2,1,0:...) custom-call(bf16[512,768]{1,0:T(8,128)(2,1)S(1)} %copy-done.3, ...), custom_call_target="tpu_custom_call" | custom-call | flops 115000000 | bytes 359375 | tf_op jit(solution)/shard_map/front/pallas_call | solution.py:149
  102.1 8.7 %attention_0.1 = (bf16[2,512,128]{2,1,0:T(8,128)(2,1)S(1)}, bf16[2,512,384]{2,1,0:T(8,128)(2,1)S(1)}, f32[8,384]{1,0:T(8,128)S(1)}) custom-call(bf16[2,512,128]{2,1,0:T(8,128)(2,1)S(1)} %get-tuple-element.257.q_in, bf16[2,512,128]{2,1,0:T(8,128)(2,1)S(1)} %get-tuple-element.258.k_in, bf16[2,512,128]{2,1,0:T(8,128)(2,1)S(1)} %get-tuple-element.259.v_in, ...), custom_call_target="tpu_custom_call" | custom-call | flops 23000000512 | bytes 71875000 | tf_op jit(solution)/shard_map/attention_0/pallas_call | solution.py:149
  111.5 8.8 %attention_1.1 = (bf16[2,512,128]{2,1,0:T(8,128)(2,1)S(1)}, bf16[2,512,384]{2,1,0:T(8,128)(2,1)S(1)}, f32[8,384]{1,0:T(8,128)S(1)}) custom-call(bf16[2,512,128]{2,1,0:T(8,128)(2,1)S(1)} %get-tuple-element.263.q_in, bf16[2,512,128]{2,1,0:T(8,128)(2,1)S(1)} %get-tuple-element.264.k_in, bf16[2,512,128]{2,1,0:T(8,128)(2,1)S(1)} %get-tuple-element.265.v_in, ...), custom_call_target="tpu_custom_call" | custom-call | flops 23000000512 | bytes 71875000 | tf_op jit(solution)/shard_map/attention_1/pallas_call | solution.py:149
  121.3 2.9 %first_grads_0.1 = (bf16[2,192,1024]{2,1,0:T(8,128)(2,1)S(1)}, bf16[2,192,1024]{2,1,0:T(8,128)(2,1)S(1)}) custom-call(bf16[1024,768]{1,0:T(8,128)(2,1)S(1)} %bitcast.101, bf16[1024,384]{1,0:T(8,128)(2,1)S(1)} %bitcast.95, bf16[1024,384]{1,0:T(8,128)(2,1)S(1)} %bitcast.96, bf16[1024,128]{1,0:T(8,128)(2,1)S(1)} %bitcast.98, bf16[1024,128]{1,0:T(8,128)(2,1)S(1)} %bitcast.99, ...), custom_call_target="tpu_custom_call" | custom-call | flops 23000000512 | bytes 71875000 | tf_op jit(solution)/shard_map/first_grads_0/pallas_call | solution.py:149
  126.0 2.6 %collective-permute-start.38 = (bf16[2,96,1536]{2,1,0:T(8,128)(2,1)}, bf16[2,96,1536]{2,1,0:T(8,128)(2,1)}, u32[]{:S(2)}, u32[]{:S(2)}) collective-permute-start(bf16[2,96,1536]{2,1,0:T(8,128)(2,1)} %pad_maximum_fusion.4), channel_id=1, source_target_pairs={{0,16},{8,24},{16,0},{24,8},{1,17},{9,25},{17,1},{25,9},{2,18},{10... | collective-permute-start | bytes 1769480 | tf_op jit(solution)/shard_map/ppermute | solution.py:109
  128.6 8.6 %attention_2.1 = (bf16[2,512,128]{2,1,0:T(8,128)(2,1)S(1)}, bf16[2,512,384]{2,1,0:T(8,128)(2,1)S(1)}, f32[8,384]{1,0:T(8,128)S(1)}) custom-call(bf16[2,512,128]{2,1,0:T(8,128)(2,1)S(1)} %get-tuple-element.278.q_in, bf16[2,512,128]{2,1,0:T(8,128)(2,1)S(1)} %get-tuple-element.279.k_in, bf16[2,512,128]{2,1,0:T(8,128)(2,1)S(1)} %get-tuple-element.280.v_in, ...), custom_call_target="tpu_custom_call" | custom-call | flops 23000000512 | bytes 71875000 | tf_op jit(solution)/shard_map/attention_2/pallas_call | solution.py:149
  138.4 1.5 first_grads_1.1
  139.9 1.4 collective-permute-start.33
  141.3 8.0 %back_0.1 = (bf16[2,512,768]{2,1,0:T(8,128)(2,1)S(1)}, bf16[1,2,512,768]{3,2,1,0:T(8,128)(2,1)S(1)}, f32[8,768]{1,0:T(8,128)S(1)}) custom-call(bf16[2,512,768]{2,1,0:T(8,128)(2,1)S(1)} %get-tuple-element.287.refs_0_, bf16[2,512,768]{2,1,0:T(8,128)(2,1)S(1)} %get-tuple-element.242.refs_1_, bf16[2,512,768]{2,1,0:T(8,128)(2,1)S(1)} %get-tuple-element.241.refs_2_, ...), custom_call_target="tpu_custom_call" | custom-call | flops 2300000000 | bytes 7187500 | tf_op jit(solution)/shard_map/back_0/pallas_call | solution.py:149
  151.7 1.5 collective-permute-done.32
  154.0 1.6 collective-permute-start.41
  160.1 1.4 collective-permute-done.37
  162.9 1.6 collective-permute-start.42
  164.5 1.2 add_convert_fusion.1
  168.2 1.3 collective-permute-start.45
  169.5 1.5 collective-permute-done.34
  171.9 13.0 %collective-permute-done.46 = bf16[2,96,512]{2,1,0:T(8,128)(2,1)S(1)} collective-permute-done((bf16[2,96,512]{2,1,0:T(8,128)(2,1)S(1)}, bf16[2,96,512]{2,1,0:T(8,128)(2,1)S(1)}, u32[]{:S(2)}, u32[]{:S(2)}) %collective-permute-start.46) | collective-permute-done | bytes 196640 | tf_op jit(solution)/shard_map/ppermute | solution.py:109
  185.0 2.4 %collective-permute-start.48 = (bf16[2,96,512]{2,1,0:T(8,128)(2,1)S(1)}, bf16[2,96,512]{2,1,0:T(8,128)(2,1)S(1)}, u32[]{:S(2)}, u32[]{:S(2)}) collective-permute-start(bf16[2,96,512]{2,1,0:T(8,128)(2,1)S(1)} %add_convert_fusion.8.refs_0_), channel_id=1, source_target_pairs={{0,8},{8,0},{16,24},{24,16},{1,9},{9,1},{17,25},{25,17},{2,10},{10... | collective-permute-start | bytes 589832 | tf_op jit(solution)/shard_map/ppermute | solution.py:109
  187.4 1.3 collective-permute-start.47
  188.8 1.6 second_end.1
  190.8 2.1 %finish_tokens.1 = (bf16[4,128,768]{2,1,0:T(8,128)(2,1)}, bf16[4,128,768]{2,1,0:T(8,128)(2,1)}) custom-call(bf16[4,128,768]{2,1,0:T(8,128)(2,1)S(1)} %copy-done.16, bf16[4,128,768]{2,1,0:T(8,128)(2,1)S(1)} %copy-done.17, f32[8,768]{1,0:T(8,128)S(1)} %get-tuple-element.218.refs_4_.refs_3_.refs_9_.vec, bf16[2,128,768]{2,1,0:T(8,128)(2,1)S(1)} %get-tuple-element.340.rest_0_, ...), custom_call_target="tpu_custom_call" | custom-call | flops 23000000512 | bytes 71875000 | tf_op jit(solution)/shard_map/finish_tokens/pallas_call | solution.py:149
  193.0 1.2 collective-permute-done.47.refs_3_
  (200 shorter events, 35.5 us)
Async XLA Ops:
  2.7 12.5 %collective-permute-start = (bf16[128,768]{1,0:T(8,128)(2,1)}, bf16[128,768]{1,0:T(8,128)(2,1)S(1)}, u32[]{:S(2)}, u32[]{:S(2)}) collective-permute-start(bf16[128,768]{1,0:T(8,128)(2,1)} %get-tuple-element.178), channel_id=1, source_target_pairs={{0,2},{1,5},{2,0},{3,7},{4,6},{5,1},{6,4},{7,3},{8,10},{9,13},{10,... | collective-permute-start | bytes 589832 | tf_op jit(solution)/shard_map/ppermute | solution.py:99
  5.6 9.6 %collective-permute-start.1 = (bf16[128,768]{1,0:T(8,128)(2,1)}, bf16[128,768]{1,0:T(8,128)(2,1)S(1)}, u32[]{:S(2)}, u32[]{:S(2)}) collective-permute-start(bf16[128,768]{1,0:T(8,128)(2,1)} %get-tuple-element.179), channel_id=1, source_target_pairs={{0,4},{1,3},{2,6},{3,1},{4,0},{5,7},{6,2},{7,5},{8,12},{9,11},{10,... | collective-permute-start | bytes 589832 | tf_op jit(solution)/shard_map/ppermute | solution.py:99
  7.2 9.0 %collective-permute-start.2 = (bf16[128,768]{1,0:T(8,128)(2,1)}, bf16[128,768]{1,0:T(8,128)(2,1)S(1)}, u32[]{:S(2)}, u32[]{:S(2)}) collective-permute-start(bf16[128,768]{1,0:T(8,128)(2,1)} %get-tuple-element.180), channel_id=1, source_target_pairs={{0,6},{1,7},{2,4},{3,5},{4,2},{5,3},{6,0},{7,1},{8,14},{9,15},{10,... | collective-permute-start | bytes 589832 | tf_op jit(solution)/shard_map/ppermute | solution.py:99
  7.2 9.0 %collective-permute-start.3 = (bf16[128,768]{1,0:T(8,128)(2,1)}, bf16[128,768]{1,0:T(8,128)(2,1)S(1)}, u32[]{:S(2)}, u32[]{:S(2)}) collective-permute-start(bf16[128,768]{1,0:T(8,128)(2,1)} %get-tuple-element.177), channel_id=1, source_target_pairs={{0,8},{8,0},{16,24},{24,16},{1,9},{9,1},{17,25},{25,17},{2,10},{10... | collective-permute-start | bytes 589832 | tf_op jit(solution)/shard_map/ppermute | solution.py:109
  16.3 6.0 %collective-permute-start.9 = (bf16[512,768]{1,0:T(8,128)(2,1)S(1)}, bf16[512,768]{1,0:T(8,128)(2,1)S(1)}, u32[]{:S(2)}, u32[]{:S(2)}) collective-permute-start(bf16[512,768]{1,0:T(8,128)(2,1)S(1)} %get-tuple-element.250.refs_0_), channel_id=1, source_target_pairs={{0,1},{1,0},{2,3},{3,2},{4,5},{5,4},{6,7},{7,6},{8,9},{9,8},{10,11... | collective-permute-start | bytes 2359304 | tf_op jit(solution)/shard_map/ppermute | solution.py:92
  16.4 5.2 %collective-permute-start.5 = (bf16[112,1536]{1,0:T(8,128)(2,1)S(1)}, bf16[112,1536]{1,0:T(8,128)(2,1)S(1)}, u32[]{:S(2)}, u32[]{:S(2)}) collective-permute-start(bf16[112,1536]{1,0:T(8,128)(2,1)S(1)} %copy-done.28), channel_id=1, source_target_pairs={{0,1},{1,0},{2,3},{3,2},{4,5},{5,4},{6,7},{7,6},{8,9},{9,8},{10,11... | collective-permute-start | bytes 1032200 | tf_op jit(solution)/shard_map/ppermute | solution.py:92
  16.9 15.6 %collective-permute-start.4 = (bf16[384,768]{1,0:T(8,128)(2,1)S(1)}, bf16[384,768]{1,0:T(8,128)(2,1)S(1)}, u32[]{:S(2)}, u32[]{:S(2)}) collective-permute-start(bf16[384,768]{1,0:T(8,128)(2,1)S(1)} %get-tuple-element.366), channel_id=1, source_target_pairs={{0,8},{8,0},{16,24},{24,16},{1,9},{9,1},{17,25},{25,17},{2,10},{10... | collective-permute-start | bytes 1769480 | tf_op jit(solution)/shard_map/ppermute | solution.py:109
  18.8 7.8 %collective-permute-start.6 = (bf16[128,768]{1,0:T(8,128)(2,1)S(1)}, bf16[128,768]{1,0:T(8,128)(2,1)S(1)}, u32[]{:S(2)}, u32[]{:S(2)}) collective-permute-start(bf16[128,768]{1,0:T(8,128)(2,1)S(1)} %copy-done.32), channel_id=1, source_target_pairs={{0,2},{1,5},{2,0},{3,7},{4,6},{5,1},{6,4},{7,3},{8,10},{9,13},{10,... | collective-permute-start | bytes 589832 | tf_op jit(solution)/shard_map/ppermute | solution.py:99
  20.3 6.3 %collective-permute-start.7 = (bf16[128,768]{1,0:T(8,128)(2,1)S(1)}, bf16[128,768]{1,0:T(8,128)(2,1)S(1)}, u32[]{:S(2)}, u32[]{:S(2)}) collective-permute-start(bf16[128,768]{1,0:T(8,128)(2,1)S(1)} %copy-done.31), channel_id=1, source_target_pairs={{0,4},{1,3},{2,6},{3,1},{4,0},{5,7},{6,2},{7,5},{8,12},{9,11},{10,... | collective-permute-start | bytes 589832 | tf_op jit(solution)/shard_map/ppermute | solution.py:99
  21.6 9.2 %collective-permute-start.8 = (bf16[128,768]{1,0:T(8,128)(2,1)S(1)}, bf16[128,768]{1,0:T(8,128)(2,1)S(1)}, u32[]{:S(2)}, u32[]{:S(2)}) collective-permute-start(bf16[128,768]{1,0:T(8,128)(2,1)S(1)} %copy-done.30), channel_id=1, source_target_pairs={{0,6},{1,7},{2,4},{3,5},{4,2},{5,3},{6,0},{7,1},{8,14},{9,15},{10,... | collective-permute-start | bytes 589832 | tf_op jit(solution)/shard_map/ppermute | solution.py:99
  30.9 4.8 %collective-permute-start.13 = (bf16[512,768]{1,0:T(8,128)(2,1)S(1)}, bf16[512,768]{1,0:T(8,128)(2,1)S(1)}, u32[]{:S(2)}, u32[]{:S(2)}) collective-permute-start(bf16[512,768]{1,0:T(8,128)(2,1)S(1)} %constant_dynamic-update-slice_fusion.9.refs_2_.refs_6_.refs_0_.refs_4_), channel_id=1, source_target_pairs={{0,1},{1,0},{2,3},{3,2},{4,5},{5,4},{6,7},{7,6},{8,9},{9,8},{10,11... | collective-permute-start | bytes 2359304 | tf_op jit(solution)/shard_map/ppermute | solution.py:92
  31.0 15.9 %collective-permute-start.12 = (bf16[224,1536]{1,0:T(8,128)(2,1)S(1)}, bf16[224,1536]{1,0:T(8,128)(2,1)S(1)}, u32[]{:S(2)}, u32[]{:S(2)}) collective-permute-start(bf16[224,1536]{1,0:T(8,128)(2,1)S(1)} %constant_dynamic-update-slice_fusion.7.rest_0_), channel_id=1, source_target_pairs={{0,2},{1,5},{2,0},{3,7},{4,6},{5,1},{6,4},{7,3},{8,10},{9,13},{10,... | collective-permute-start | bytes 2064392 | tf_op jit(solution)/shard_map/ppermute | solution.py:106
  32.6 15.6 %collective-permute-start.15 = (bf16[512,768]{1,0:T(8,128)(2,1)S(1)}, bf16[512,768]{1,0:T(8,128)(2,1)S(1)}, u32[]{:S(2)}, u32[]{:S(2)}) collective-permute-start(bf16[512,768]{1,0:T(8,128)(2,1)S(1)} %constant_dynamic-update-slice_fusion.13.refs_0_), channel_id=1, source_target_pairs={{0,1},{1,0},{2,3},{3,2},{4,5},{5,4},{6,7},{7,6},{8,9},{9,8},{10,11... | collective-permute-start | bytes 2359304 | tf_op jit(solution)/shard_map/ppermute | solution.py:92
  32.7 25.9 %collective-permute-start.10 = (bf16[512,768]{1,0:T(8,128)(2,1)S(1)}, bf16[512,768]{1,0:T(8,128)(2,1)S(1)}, u32[]{:S(2)}, u32[]{:S(2)}) collective-permute-start(bf16[512,768]{1,0:T(8,128)(2,1)S(1)} %constant_dynamic-update-slice_fusion.9.refs_2_.refs_6_.refs_0_.refs_4_), channel_id=1, source_target_pairs={{0,8},{8,0},{16,24},{24,16},{1,9},{9,1},{17,25},{25,17},{2,10},{10... | collective-permute-start | bytes 2359304 | tf_op jit(solution)/shard_map/ppermute | solution.py:109
  34.3 16.4 %collective-permute-start.11 = (bf16[224,1536]{1,0:T(8,128)(2,1)S(1)}, bf16[224,1536]{1,0:T(8,128)(2,1)S(1)}, u32[]{:S(2)}, u32[]{:S(2)}) collective-permute-start(bf16[224,1536]{1,0:T(8,128)(2,1)S(1)} %constant_dynamic-update-slice_fusion.7.rest_0_), channel_id=1, source_target_pairs={{0,4},{1,3},{2,6},{3,1},{4,0},{5,7},{6,2},{7,5},{8,12},{9,11},{10,... | collective-permute-start | bytes 2064392 | tf_op jit(solution)/shard_map/ppermute | solution.py:106
  46.9 10.9 %collective-permute-start.14 = (bf16[224,1536]{1,0:T(8,128)(2,1)S(1)}, bf16[224,1536]{1,0:T(8,128)(2,1)S(1)}, u32[]{:S(2)}, u32[]{:S(2)}) collective-permute-start(bf16[224,1536]{1,0:T(8,128)(2,1)S(1)} %collective-permute-done.12.rest_1_), channel_id=1, source_target_pairs={{0,4},{1,3},{2,6},{3,1},{4,0},{5,7},{6,2},{7,5},{8,12},{9,11},{10,... | collective-permute-start | bytes 2064392 | tf_op jit(solution)/shard_map/ppermute | solution.py:106
  49.1 1.6 collective-permute-start.16
  58.7 5.7 %collective-permute-start.17 = (bf16[512,768]{1,0:T(8,128)(2,1)S(1)}, bf16[512,768]{1,0:T(8,128)(2,1)S(1)}, u32[]{:S(2)}, u32[]{:S(2)}) collective-permute-start(bf16[512,768]{1,0:T(8,128)(2,1)S(1)} %collective-permute-done.10.refs_2_.refs_8_), channel_id=1, source_target_pairs={{0,1},{1,0},{2,3},{3,2},{4,5},{5,4},{6,7},{7,6},{8,9},{9,8},{10,11... | collective-permute-start | bytes 2359304 | tf_op jit(solution)/shard_map/ppermute | solution.py:92
  58.7 17.3 %collective-permute-start.20 = (bf16[192,1536]{1,0:T(8,128)(2,1)S(1)}, bf16[192,1536]{1,0:T(8,128)(2,1)}, u32[]{:S(2)}, u32[]{:S(2)}) collective-permute-start(bf16[192,1536]{1,0:T(8,128)(2,1)S(1)} %constant_dynamic-update-slice_fusion.15.rest_0_), channel_id=1, source_target_pairs={{0,2},{1,5},{2,0},{3,7},{4,6},{5,1},{6,4},{7,3},{8,10},{9,13},{10,... | collective-permute-start | bytes 1769480 | tf_op jit(solution)/shard_map/ppermute | solution.py:106
  60.2 15.8 %collective-permute-start.21 = (bf16[192,1536]{1,0:T(8,128)(2,1)S(1)}, bf16[192,1536]{1,0:T(8,128)(2,1)}, u32[]{:S(2)}, u32[]{:S(2)}) collective-permute-start(bf16[192,1536]{1,0:T(8,128)(2,1)S(1)} %constant_dynamic-update-slice_fusion.15.rest_0_), channel_id=1, source_target_pairs={{0,4},{1,3},{2,6},{3,1},{4,0},{5,7},{6,2},{7,5},{8,12},{9,11},{10,... | collective-permute-start | bytes 1769480 | tf_op jit(solution)/shard_map/ppermute | solution.py:106
  75.4 2.4 %collective-permute-start.18 = (bf16[512,768]{1,0:T(8,128)(2,1)S(1)}, bf16[512,768]{1,0:T(8,128)(2,1)S(1)}, u32[]{:S(2)}, u32[]{:S(2)}) collective-permute-start(bf16[512,768]{1,0:T(8,128)(2,1)S(1)} %get-tuple-element.351), channel_id=1, source_target_pairs={{0,1},{1,0},{2,3},{3,2},{4,5},{5,4},{6,7},{7,6},{8,9},{9,8},{10,11... | collective-permute-start | bytes 2359304 | tf_op jit(solution)/shard_map/ppermute | solution.py:92
  75.5 3.4 %collective-permute-start.19 = (bf16[512,768]{1,0:T(8,128)(2,1)S(1)}, bf16[512,768]{1,0:T(8,128)(2,1)S(1)}, u32[]{:S(2)}, u32[]{:S(2)}) collective-permute-start(bf16[512,768]{1,0:T(8,128)(2,1)S(1)} %get-tuple-element.350), channel_id=1, source_target_pairs={{0,1},{1,0},{2,3},{3,2},{4,5},{5,4},{6,7},{7,6},{8,9},{9,8},{10,11... | collective-permute-start | bytes 2359304 | tf_op jit(solution)/shard_map/ppermute | solution.py:92
  76.0 18.9 %collective-permute-start.22 = (bf16[192,1536]{1,0:T(8,128)(2,1)}, bf16[192,1536]{1,0:T(8,128)(2,1)S(1)}, u32[]{:S(2)}, u32[]{:S(2)}) collective-permute-start(bf16[192,1536]{1,0:T(8,128)(2,1)} %collective-permute-done.20.rest_1_), channel_id=1, source_target_pairs={{0,4},{1,3},{2,6},{3,1},{4,0},{5,7},{6,2},{7,5},{8,12},{9,11},{10,... | collective-permute-start | bytes 1769480 | tf_op jit(solution)/shard_map/ppermute | solution.py:106
  79.5 15.4 %collective-permute-start.23 = (bf16[384,768]{1,0:T(8,128)(2,1)S(1)}, bf16[384,768]{1,0:T(8,128)(2,1)S(1)}, u32[]{:S(2)}, u32[]{:S(2)}) collective-permute-start(bf16[384,768]{1,0:T(8,128)(2,1)S(1)} %slice.232), channel_id=1, source_target_pairs={{0,8},{8,0},{16,24},{24,16},{1,9},{9,1},{17,25},{25,17},{2,10},{10... | collective-permute-start | bytes 1769480 | tf_op jit(solution)/shard_map/ppermute | solution.py:109
  93.2 17.7 %collective-permute-start.25 = (bf16[2,192,1536]{2,1,0:T(8,128)(2,1)S(1)}, bf16[2,192,1536]{2,1,0:T(8,128)(2,1)S(1)}, u32[]{:S(2)}, u32[]{:S(2)}) collective-permute-start(bf16[2,192,1536]{2,1,0:T(8,128)(2,1)S(1)} %get-tuple-element.256), channel_id=1, source_target_pairs={{0,4},{1,3},{2,6},{3,1},{4,0},{5,7},{6,2},{7,5},{8,12},{9,11},{10,... | collective-permute-start | bytes 3538952 | tf_op jit(solution)/shard_map/ppermute | solution.py:106
  96.8 24.4 %collective-permute-start.24 = (bf16[640,768]{1,0:T(8,128)(2,1)S(1)}, bf16[640,768]{1,0:T(8,128)(2,1)S(1)}, u32[]{:S(2)}, u32[]{:S(2)}) collective-permute-start(bf16[640,768]{1,0:T(8,128)(2,1)S(1)} %pad_maximum_fusion.1), channel_id=1, source_target_pairs={{0,8},{8,0},{16,24},{24,16},{1,9},{9,1},{17,25},{25,17},{2,10},{10... | collective-permute-start | bytes 2949128 | tf_op jit(solution)/shard_map/ppermute | solution.py:109
  111.0 9.9 %collective-permute-start.26 = (bf16[192,1536]{1,0:T(8,128)(2,1)S(1)}, bf16[192,1536]{1,0:T(8,128)(2,1)S(1)}, u32[]{:S(2)}, u32[]{:S(2)}) collective-permute-start(bf16[192,1536]{1,0:T(8,128)(2,1)S(1)} %fusion.3), channel_id=1, source_target_pairs={{0,2},{1,5},{2,0},{3,7},{4,6},{5,1},{6,4},{7,3},{8,10},{9,13},{10,... | collective-permute-start | bytes 1769480 | tf_op jit(solution)/shard_map/ppermute | solution.py:106
  121.3 3.8 %collective-permute-start.28 = (bf16[96,1536]{1,0:T(8,128)(2,1)S(1)}, bf16[96,1536]{1,0:T(8,128)(2,1)S(1)}, u32[]{:S(2)}, u32[]{:S(2)}) collective-permute-start(bf16[96,1536]{1,0:T(8,128)(2,1)S(1)} %get-tuple-element.361), channel_id=1, source_target_pairs={{0,1},{1,0},{2,3},{3,2},{4,5},{5,4},{6,7},{7,6},{8,9},{9,8},{10,11... | collective-permute-start | bytes 884744 | tf_op jit(solution)/shard_map/ppermute | solution.py:92
  124.2 13.0 %collective-permute-start.27 = (bf16[2,192,1024]{2,1,0:T(8,128)(2,1)S(1)}, bf16[2,192,1024]{2,1,0:T(8,128)(2,1)S(1)}, u32[]{:S(2)}, u32[]{:S(2)}) collective-permute-start(bf16[2,192,1024]{2,1,0:T(8,128)(2,1)S(1)} %get-tuple-element.274), channel_id=1, source_target_pairs={{0,4},{1,3},{2,6},{3,1},{4,0},{5,7},{6,2},{7,5},{8,12},{9,11},{10,... | collective-permute-start | bytes 2359304 | tf_op jit(solution)/shard_map/ppermute | solution.py:106
  126.0 38.5 %collective-permute-start.38 = (bf16[2,96,1536]{2,1,0:T(8,128)(2,1)}, bf16[2,96,1536]{2,1,0:T(8,128)(2,1)}, u32[]{:S(2)}, u32[]{:S(2)}) collective-permute-start(bf16[2,96,1536]{2,1,0:T(8,128)(2,1)} %pad_maximum_fusion.4), channel_id=1, source_target_pairs={{0,16},{8,24},{16,0},{24,8},{1,17},{9,25},{17,1},{25,9},{2,18},{10... | collective-permute-start | bytes 1769480 | tf_op jit(solution)/shard_map/ppermute | solution.py:109
  137.3 12.7 %collective-permute-start.31 = (bf16[192,1024]{1,0:T(8,128)(2,1)S(1)}, bf16[192,1024]{1,0:T(8,128)(2,1)S(1)}, u32[]{:S(2)}, u32[]{:S(2)}) collective-permute-start(bf16[192,1024]{1,0:T(8,128)(2,1)S(1)} %fusion.4), channel_id=1, source_target_pairs={{0,2},{1,5},{2,0},{3,7},{4,6},{5,1},{6,4},{7,3},{8,10},{9,13},{10,... | collective-permute-start | bytes 1179656 | tf_op jit(solution)/shard_map/ppermute | solution.py:106
  139.9 10.4 %collective-permute-start.33 = (bf16[2,192,512]{2,1,0:T(8,128)(2,1)S(1)}, bf16[2,192,512]{2,1,0:T(8,128)(2,1)S(1)}, u32[]{:S(2)}, u32[]{:S(2)}) collective-permute-start(bf16[2,192,512]{2,1,0:T(8,128)(2,1)S(1)} %get-tuple-element.292), channel_id=1, source_target_pairs={{0,4},{1,3},{2,6},{3,1},{4,0},{5,7},{6,2},{7,5},{8,12},{9,11},{10,... | collective-permute-start | bytes 1179656 | tf_op jit(solution)/shard_map/ppermute | solution.py:106
  149.5 4.5 %collective-permute-start.29 = (bf16[512,768]{1,0:T(8,128)(2,1)S(1)}, bf16[512,768]{1,0:T(8,128)(2,1)S(1)}, u32[]{:S(2)}, u32[]{:S(2)}) collective-permute-start(bf16[512,768]{1,0:T(8,128)(2,1)S(1)} %get-tuple-element.347), channel_id=1, source_target_pairs={{0,1},{1,0},{2,3},{3,2},{4,5},{5,4},{6,7},{7,6},{8,9},{9,8},{10,11... | collective-permute-start | bytes 2359304 | tf_op jit(solution)/shard_map/ppermute | solution.py:92
  149.6 6.1 %collective-permute-start.30 = (bf16[512,768]{1,0:T(8,128)(2,1)S(1)}, bf16[512,768]{1,0:T(8,128)(2,1)S(1)}, u32[]{:S(2)}, u32[]{:S(2)}) collective-permute-start(bf16[512,768]{1,0:T(8,128)(2,1)S(1)} %get-tuple-element.346), channel_id=1, source_target_pairs={{0,1},{1,0},{2,3},{3,2},{4,5},{5,4},{6,7},{7,6},{8,9},{9,8},{10,11... | collective-permute-start | bytes 2359304 | tf_op jit(solution)/shard_map/ppermute | solution.py:92
  150.3 8.4 %collective-permute-start.35 = (bf16[192,512]{1,0:T(8,128)(2,1)S(1)}, bf16[192,512]{1,0:T(8,128)(2,1)S(1)}, u32[]{:S(2)}, u32[]{:S(2)}) collective-permute-start(bf16[192,512]{1,0:T(8,128)(2,1)S(1)} %fusion.5), channel_id=1, source_target_pairs={{0,2},{1,5},{2,0},{3,7},{4,6},{5,1},{6,4},{7,3},{8,10},{9,13},{10,... | collective-permute-start | bytes 589832 | tf_op jit(solution)/shard_map/ppermute | solution.py:106
  151.5 1.8 collective-permute-start.32
  153.3 4.3 %collective-permute-start.36 = (bf16[2,32,512]{2,1,0:T(8,128)(2,1)S(1)}, bf16[2,32,512]{2,1,0:T(8,128)(2,1)S(1)}, u32[]{:S(2)}, u32[]{:S(2)}) collective-permute-start(bf16[2,32,512]{2,1,0:T(8,128)(2,1)S(1)} %get-tuple-element.301), channel_id=1, source_target_pairs={{0,4},{1,3},{2,6},{3,1},{4,0},{5,7},{6,2},{7,5},{8,12},{9,11},{10,... | collective-permute-start | bytes 196616 | tf_op jit(solution)/shard_map/ppermute | solution.py:106
  154.0 12.3 %collective-permute-start.41 = (bf16[2,96,512]{2,1,0:T(8,128)(2,1)S(1)}, bf16[2,96,512]{2,1,0:T(8,128)(2,1)S(1)}, u32[]{:S(2)}, u32[]{:S(2)}) collective-permute-start(bf16[2,96,512]{2,1,0:T(8,128)(2,1)S(1)} %broadcast_select_fusion), channel_id=1, source_target_pairs={{0,8},{8,0},{16,24},{24,16},{1,9},{9,1},{17,25},{25,17},{2,10},{10... | collective-permute-start | bytes 589832 | tf_op jit(solution)/shard_map/ppermute | solution.py:109
  157.5 4.0 %collective-permute-start.37 = (bf16[32,512]{1,0:T(8,128)(2,1)S(1)}, bf16[32,512]{1,0:T(8,128)(2,1)S(1)}, u32[]{:S(2)}, u32[]{:S(2)}) collective-permute-start(bf16[32,512]{1,0:T(8,128)(2,1)S(1)} %fusion.8), channel_id=1, source_target_pairs={{0,2},{1,5},{2,0},{3,7},{4,6},{5,1},{6,4},{7,3},{8,10},{9,13},{10,... | collective-permute-start | bytes 98312 | tf_op jit(solution)/shard_map/ppermute | solution.py:106
  158.9 12.1 %collective-permute-start.34 = (bf16[2,2,128,768]{3,2,1,0:T(8,128)(2,1)S(1)}, bf16[2,2,128,768]{3,2,1,0:T(8,128)(2,1)S(1)}, u32[]{:S(2)}, u32[]{:S(2)}) collective-permute-start(bf16[2,2,128,768]{3,2,1,0:T(8,128)(2,1)S(1)} %pad_maximum_fusion.2), channel_id=1, source_target_pairs={{0,2},{1,5},{2,0},{3,7},{4,6},{5,1},{6,4},{7,3},{8,10},{9,13},{10,... | collective-permute-start | bytes 2359304 | tf_op jit(solution)/shard_map/ppermute | solution.py:106
  160.0 1.7 collective-permute-start.40
  162.9 5.3 %collective-permute-start.42 = (bf16[2,112,256]{2,1,0:T(8,128)(2,1)S(1)}, bf16[2,112,256]{2,1,0:T(8,128)(2,1)S(1)}, u32[]{:S(2)}, u32[]{:S(2)}) collective-permute-start(bf16[2,112,256]{2,1,0:T(8,128)(2,1)S(1)} %broadcast_select_fusion.1), channel_id=1, source_target_pairs={{0,8},{8,0},{16,24},{24,16},{1,9},{9,1},{17,25},{25,17},{2,10},{10... | collective-permute-start | bytes 344072 | tf_op jit(solution)/shard_map/ppermute | solution.py:109
  165.7 22.9 %collective-permute-start.44 = (bf16[2,96,1536]{2,1,0:T(8,128)(2,1)S(1)}, bf16[2,96,1536]{2,1,0:T(8,128)(2,1)S(1)}, u32[]{:S(2)}, u32[]{:S(2)}) collective-permute-start(bf16[2,96,1536]{2,1,0:T(8,128)(2,1)S(1)} %add_convert_fusion.1), channel_id=1, source_target_pairs={{0,8},{8,0},{16,24},{24,16},{1,9},{9,1},{17,25},{25,17},{2,10},{10... | collective-permute-start | bytes 1769480 | tf_op jit(solution)/shard_map/ppermute | solution.py:109
  166.4 18.5 %collective-permute-start.46 = (bf16[2,96,512]{2,1,0:T(8,128)(2,1)S(1)}, bf16[2,96,512]{2,1,0:T(8,128)(2,1)S(1)}, u32[]{:S(2)}, u32[]{:S(2)}) collective-permute-start(bf16[2,96,512]{2,1,0:T(8,128)(2,1)S(1)} %add_convert_fusion.9), channel_id=1, source_target_pairs={{0,16},{8,24},{16,0},{24,8},{1,17},{9,25},{17,1},{25,9},{2,18},{10... | collective-permute-start | bytes 589832 | tf_op jit(solution)/shard_map/ppermute | solution.py:109
  168.2 19.2 %collective-permute-start.45 = (bf16[2,112,256]{2,1,0:T(8,128)(2,1)S(1)}, bf16[2,112,256]{2,1,0:T(8,128)(2,1)S(1)}, u32[]{:S(2)}, u32[]{:S(2)}) collective-permute-start(bf16[2,112,256]{2,1,0:T(8,128)(2,1)S(1)} %add_convert_fusion.13), channel_id=1, source_target_pairs={{0,16},{8,24},{16,0},{24,8},{1,17},{9,25},{17,1},{25,9},{2,18},{10... | collective-permute-start | bytes 344072 | tf_op jit(solution)/shard_map/ppermute | solution.py:109
  171.1 19.2 %collective-permute-start.43 = (bf16[2,2,128,768]{3,2,1,0:T(8,128)(2,1)S(1)}, bf16[2,2,128,768]{3,2,1,0:T(8,128)(2,1)S(1)}, u32[]{:S(2)}, u32[]{:S(2)}) collective-permute-start(bf16[2,2,128,768]{3,2,1,0:T(8,128)(2,1)S(1)} %pad_maximum_fusion.3), channel_id=1, source_target_pairs={{0,4},{1,3},{2,6},{3,1},{4,0},{5,7},{6,2},{7,5},{8,12},{9,11},{10,... | collective-permute-start | bytes 2359304 | tf_op jit(solution)/shard_map/ppermute | solution.py:106
  185.0 8.1 %collective-permute-start.48 = (bf16[2,96,512]{2,1,0:T(8,128)(2,1)S(1)}, bf16[2,96,512]{2,1,0:T(8,128)(2,1)S(1)}, u32[]{:S(2)}, u32[]{:S(2)}) collective-permute-start(bf16[2,96,512]{2,1,0:T(8,128)(2,1)S(1)} %add_convert_fusion.8.refs_0_), channel_id=1, source_target_pairs={{0,8},{8,0},{16,24},{24,16},{1,9},{9,1},{17,25},{25,17},{2,10},{10... | collective-permute-start | bytes 589832 | tf_op jit(solution)/shard_map/ppermute | solution.py:109
  187.4 6.8 %collective-permute-start.47 = (bf16[2,112,256]{2,1,0:T(8,128)(2,1)S(1)}, bf16[2,112,256]{2,1,0:T(8,128)(2,1)S(1)}, u32[]{:S(2)}, u32[]{:S(2)}) collective-permute-start(bf16[2,112,256]{2,1,0:T(8,128)(2,1)S(1)} %add_convert_fusion.12.refs_2_), channel_id=1, source_target_pairs={{0,8},{8,0},{16,24},{24,16},{1,9},{9,1},{17,25},{25,17},{2,10},{10... | collective-permute-start | bytes 344072 | tf_op jit(solution)/shard_map/ppermute | solution.py:109
  (34 other events, 214.0 us)
